TPU v7x, 128 devices: a whole 4x4x4 slice. The times are simulated.
128 devices in a mesh: dp: 16 (over x, y_hi, core), seq: 8 (over y_lo, z).
Axes of the slice: x: 4, y: 4 (y_hi: 2, y_lo: 2; y = y_hi * 2 + y_lo), z: 4, core: 2. Of those that a mesh axis runs over, the one named last changes fastest.
Arguments:
- latents: bfloat16 [16, 8, 256, 1152], P('dp', 'seq'), may hold values from -6 to 6
- cotangent: bfloat16 [16, 8, 256, 1152], P('dp', 'seq'), may hold values from -6 to 6
- modulation: float32 [16, 2, 3, 1152], P('dp'), may hold values from -3 to 3
- qk_gains: float32 [2, 2, 72], replicated, may hold values from 0.6 to 2
- spatial_qkv: bfloat16 [1152, 1728], replicated, may hold values from -0.1875 to 0.1875
- spatial_out: bfloat16 [576, 1152], replicated, may hold values from -0.25 to 0.25
- temporal_qkv: bfloat16 [1152, 1728], replicated, may hold values from -0.1875 to 0.1875
- temporal_out: bfloat16 [576, 1152], replicated, may hold values from -0.25 to 0.25
Outputs:
- block_output: bfloat16 [16, 8, 256, 1152], P('dp', 'seq')
- latents_grad: bfloat16 [16, 8, 256, 1152], P('dp', 'seq')
- spatial_qkv_grad: float32 [1152, 1728], P(('dp', 'seq'))
- spatial_out_grad: float32 [576, 1152], P(None, ('dp', 'seq'))
- temporal_qkv_grad: float32 [1152, 1728], P(('dp', 'seq'))
- temporal_out_grad: float32 [576, 1152], P(None, ('dp', 'seq'))
All inputs are finite; a program needn't handle non-finite values.
Results may differ from a plain program's by a relative error of at most 0.035.
Values may be sent and summed in bfloat16 or wider, within the bound.
No kernel may reach another device: no remote copies, remote signals or barrier semaphores. Data moves between devices by JAX's collectives and lax.ppermute only.
A program may use at most 192 MiB of HBM per device.

v0:
```python
import jax
import jax.numpy as jnp
from jax import lax
from jax.sharding import PartitionSpec as P

HEAD_DIM = 72
HEADS = 8


EPS = 1e-06


def modulate(x32, shift, scale):
    mean = jnp.mean(x32, axis=-1, keepdims=True)
    centered = x32 - mean
    variance = jnp.mean(centered * centered, axis=-1, keepdims=True)
    return (centered * lax.rsqrt(variance + EPS) * (1.0 + scale) + shift).astype(jnp.bfloat16)


def head_norm(part, gain):
    wide = part.astype(jnp.float32)
    square = jnp.mean(wide * wide, axis=-1, keepdims=True)
    return (wide * lax.rsqrt(square + EPS) * gain).astype(jnp.bfloat16)


def attend(qkv, gains, frames_first):
    leading = qkv.shape[:-1]
    parts = qkv.reshape(leading + (3, HEADS, HEAD_DIM))
    query = head_norm(parts[..., 0, :, :], gains[0])
    keys = head_norm(parts[..., 1, :, :], gains[1])
    values = parts[..., 2, :, :]
    if frames_first:
        scores = jnp.einsum("lbhd,mbhd->bhlm", query, keys, preferred_element_type=jnp.float32)
    else:
        scores = jnp.einsum("blhd,bmhd->bhlm", query, keys, preferred_element_type=jnp.float32)
    scores = scores * HEAD_DIM ** (-0.5)
    highest = jnp.max(scores, axis=-1, keepdims=True)
    expo = jnp.exp(scores - highest)
    probs = (expo / jnp.sum(expo, axis=-1, keepdims=True)).astype(jnp.bfloat16)
    if frames_first:
        result = jnp.einsum("bhlm,mbhd->lbhd", probs, values, preferred_element_type=jnp.float32)
    else:
        result = jnp.einsum("bhlm,bmhd->blhd", probs, values, preferred_element_type=jnp.float32)
    return result.astype(jnp.bfloat16).reshape(leading + (HEADS * HEAD_DIM,))


def outer_sum(left, right):
    flat_left = left.reshape(-1, left.shape[-1])
    flat_right = right.reshape(-1, right.shape[-1])
    return lax.dot_general(
        flat_left, flat_right, (((0,), (0,)), ((), ())), preferred_element_type=jnp.float32
    )


def times_t(left, weight):
    return lax.dot_general(
        left, weight, (((left.ndim - 1,), (1,)), ((), ())), preferred_element_type=jnp.float32
    )


def shards(
    latents, cotangent, modulation, qk_gains, spatial_qkv, spatial_out, temporal_qkv, temporal_out
):
    blocks = modulation[0]
    x32 = latents[0].astype(jnp.float32)
    normed_s = modulate(x32, blocks[0, 0], blocks[0, 1])
    qkv_s = jnp.dot(normed_s, spatial_qkv, preferred_element_type=jnp.float32).astype(jnp.bfloat16)
    att_s, back_s = jax.vjp(lambda t: attend(t, qk_gains[0], False), qkv_s)
    middle = (
        x32 + blocks[0, 2] * jnp.dot(att_s, spatial_out, preferred_element_type=jnp.float32)
    ).astype(jnp.bfloat16)
    mid32 = middle.astype(jnp.float32)
    normed_t = modulate(mid32, blocks[1, 0], blocks[1, 1])
    qkv_frame = jnp.dot(normed_t, temporal_qkv, preferred_element_type=jnp.float32).astype(
        jnp.bfloat16
    )
    qkv_patch = lax.all_to_all(qkv_frame, "seq", split_axis=1, concat_axis=0, tiled=True)
    att_patch, back_t = jax.vjp(lambda t: attend(t, qk_gains[1], True), qkv_patch)
    att_t = lax.all_to_all(att_patch, "seq", split_axis=0, concat_axis=1, tiled=True)
    output = (
        mid32 + blocks[1, 2] * jnp.dot(att_t, temporal_out, preferred_element_type=jnp.float32)
    ).astype(jnp.bfloat16)
    cot32 = cotangent[0].astype(jnp.float32)
    scaled_t = (blocks[1, 2] * cot32).astype(jnp.bfloat16)
    grad_t_out = outer_sum(att_t, scaled_t)
    att_grad_t = times_t(scaled_t, temporal_out).astype(jnp.bfloat16)
    att_grad_patch = lax.all_to_all(att_grad_t, "seq", split_axis=1, concat_axis=0, tiled=True)
    qkv_grad_patch = back_t(att_grad_patch)[0]
    qkv_grad_t = lax.all_to_all(qkv_grad_patch, "seq", split_axis=0, concat_axis=1, tiled=True)
    grad_t_qkv = outer_sum(normed_t, qkv_grad_t)
    normed_grad_t = times_t(qkv_grad_t, temporal_qkv).astype(jnp.bfloat16)
    temporal_qkv_grad, temporal_out_grad = (
        lax.psum_scatter(grad_t_qkv, ("dp", "seq"), scatter_dimension=0, tiled=True),
        lax.psum_scatter(grad_t_out, ("dp", "seq"), scatter_dimension=1, tiled=True),
    )
    pre_back_t = jax.vjp(lambda v: modulate(v, blocks[1, 0], blocks[1, 1]), mid32)[1]
    middle_grad = (cot32 + pre_back_t(normed_grad_t)[0]).astype(jnp.bfloat16)
    mg32 = middle_grad.astype(jnp.float32)
    scaled_s = (blocks[0, 2] * mg32).astype(jnp.bfloat16)
    grad_s_out = outer_sum(att_s, scaled_s)
    att_grad_s = times_t(scaled_s, spatial_out).astype(jnp.bfloat16)
    qkv_grad_s = back_s(att_grad_s)[0]
    grad_s_qkv = outer_sum(normed_s, qkv_grad_s)
    normed_grad_s = times_t(qkv_grad_s, spatial_qkv).astype(jnp.bfloat16)
    pre_back_s = jax.vjp(lambda v: modulate(v, blocks[0, 0], blocks[0, 1]), x32)[1]
    latents_grad = (mg32 + pre_back_s(normed_grad_s)[0]).astype(jnp.bfloat16)
    spatial_qkv_grad, spatial_out_grad = (
        lax.psum_scatter(grad_s_qkv, ("dp", "seq"), scatter_dimension=0, tiled=True),
        lax.psum_scatter(grad_s_out, ("dp", "seq"), scatter_dimension=1, tiled=True),
    )
    return (
        output[None],
        latents_grad[None],
        spatial_qkv_grad,
        spatial_out_grad,
        temporal_qkv_grad,
        temporal_out_grad,
    )


def solution(mesh):
    return jax.shard_map(
        shards,
        mesh=mesh,
        in_specs=(
            P("dp", "seq", None, None),
            P("dp", "seq", None, None),
            P("dp", None, None, None),
            P(),
            P(),
            P(),
            P(),
            P(),
        ),
        out_specs=(
            P("dp", "seq", None, None),
            P("dp", "seq", None, None),
            P(("dp", "seq"), None),
            P(None, ("dp", "seq")),
            P(("dp", "seq"), None),
            P(None, ("dp", "seq")),
        ),
        check_vma=False,
    )
```

profile of v0, /device:TPU:0, one launch (start us, length us, event | category | flops | bytes accessed | tf_op | source)
XLA Modules:
  0.0 427.5 jit_solution(7144803901779509026)
XLA Ops:
  7.2 1.0 slice_reduce_fusion.1
  8.2 2.1 fusion.58
  11.5 2.7 reduce.46
  14.2 1.1 reshape.739
  15.2 6.9 %all-to-all-start.2 = ((bf16[8,2,9216]{2,1,0:T(2,128)(2,1)}), bf16[8,2,9216]{2,1,0:T(2,128)(2,1)}, u32[]{:S(2)}, u32[]{:S(2)}) async-start(bf16[8,2,9216]{2,1,0:T(2,128)(2,1)} %reshape.739), calls=%async_computation.2 | async-start | bytes 589824 | tf_op jit(solution)/shard_map/all_to_all | solution.py:87
  23.3 3.6 convolution_convert_fusion.1
  30.4 1.1 copy-done.6
  34.1 2.4 fusion.10
  36.5 5.0 %copy.71 = bf16[1,256,1728]{2,0,1:T(2,128)(2,1)} copy(bf16[1,256,1728]{1,2,0:T(8,128)(2,1)} %fusion.10) | data formatting | bytes 1769472 | tf_op jit(solution)/shard_map/convert_element_type | solution.py:74
  41.5 8.4 %reduce.45 = bf16[256,1728]{1,0:T(8,128)(2,1)} reduce(bf16[256,1,1728]{2,1,0:T(2,128)(2,1)} %bitcast.274, bf16[]{:T(256)} %broadcast.540), dimensions={1}, to_apply=%bitcast.228.reduce_sub_computation | reduce | bytes 1769474
  49.9 3.8 reshape.737
  53.8 5.7 %all-to-all-start = ((bf16[8,2,27648]{2,1,0:T(2,128)(2,1)}), bf16[8,2,27648]{2,1,0:T(2,128)(2,1)}, u32[]{:S(2)}, u32[]{:S(2)}) async-start(bf16[8,2,27648]{2,1,0:T(2,128)(2,1)} %reshape.737), calls=%async_computation | async-start | bytes 1769472 | tf_op jit(solution)/shard_map/all_to_all | solution.py:77
  59.5 3.3 reshape.740
  62.7 3.7 bitcast_reduce_fusion.1
  66.4 2.3 reshape.713
  68.7 3.3 all-to-all-done
  72.1 6.0 %reshape.738 = bf16[256,1,1728]{2,1,0:T(2,128)(2,1)} reshape(bf16[8,2,27648]{2,1,0:T(2,128)(2,1)} %all-to-all-done) | data formatting | bytes 1769472
  78.0 7.6 %bitcast_reduce_fusion = bf16[256,1728]{1,0:T(8,128)(2,1)} fusion(bf16[256,1,1728]{2,1,0:T(2,128)(2,1)} %reshape.738), kind=kLoop, calls=%fused_computation.255 | loop fusion | bytes 1769472 | tf_op jit(solution)/shard_map/all_to_all | solution.py:77
  85.7 4.2 reshape.710
  89.9 2.5 fusion.168
  94.3 1.4 fusion.145
  95.7 0.9 copy.78
  96.6 2.2 fusion.65
  98.7 1.6 copy.74
  100.3 1.4 fusion.144
  101.7 1.5 copy.75
  103.2 2.4 fusion.170
  106.1 1.0 copy-done.33
  108.1 1.4 convert_reduce_fusion.2
  110.7 2.7 fusion.68
  113.5 2.5 fusion.72
  116.0 0.9 copy.80
  116.9 2.2 reshape.711
  119.1 4.1 all-to-all-start.1
  123.2 1.6 copy.86
  124.8 1.4 multiply_multiply_fusion
  126.2 1.5 copy.87
  127.7 1.6 copy.83
  129.3 1.4 multiply_multiply_fusion.1
  130.7 1.5 copy.84
  132.2 2.2 fusion.118
  134.5 0.9 fusion.119
  136.9 1.4 copy.88
  138.3 3.6 reshape.714
  141.9 5.8 %all-to-all-start.3 = ((bf16[8,32,1728]{2,1,0:T(8,128)(2,1)}), bf16[8,32,1728]{2,1,0:T(8,128)(2,1)}, u32[]{:S(2)}, u32[]{:S(2)}) async-start(bf16[8,32,1728]{2,1,0:T(8,128)(2,1)} %reshape.714), calls=%async_computation.3 | async-start | bytes 1835008 | tf_op jit(solution)/shard_map/all_to_all | solution.py:89
  147.9 3.4 fusion.104
  151.3 9.1 %all-to-all-done.3 = bf16[8,32,1728]{2,1,0:T(8,128)(2,1)} async-done(((bf16[8,32,1728]{2,1,0:T(8,128)(2,1)}), bf16[8,32,1728]{2,1,0:T(8,128)(2,1)}, u32[]{:S(2)}, u32[]{:S(2)}) %all-to-all-start.3) | async-done | bytes 884768 | tf_op jit(solution)/shard_map/all_to_all | solution.py:89
  160.5 4.3 %multiply_reduce_fusion.1 = (f32[256]{0:T(256)S(1)}, f32[256,1152]{1,0:T(8,128)S(1)}) fusion(f32[256,1152]{1,0:T(8,128)} %copy-done.2, f32[256]{0:T(256)S(1)} %copy-done.63, f32[1152]{0:T(1024)S(1)} %copy-done.47, bf16[256,1728]{1,0:T(8,128)(2,1)} %bitcast.34, bf16[1152,1728]{0,1:T(8,128)(2,1)} %param.14), kind=kOutput, calls=%fused_computation.97 | convolution fusion | flops 1020985088 | bytes 7232000 | tf_op jit(solution)/shard_map/dot_general | solution.py:56
  167.3 2.3 fusion.128
  169.6 5.9 %fusion.161 = f32[1152,1728]{1,0:T(8,128)} fusion(bf16[256,1728]{1,0:T(8,128)(2,1)} %bitcast.34, f32[256,1152]{1,0:T(8,128)S(1)} %copy-done.3, f32[1152]{0:T(1024)S(1)} %copy-done.45, f32[1152]{0:T(1024)S(1)} %copy-done.47, f32[256]{0:T(256)S(1)} %copy-done.65, f32[256]{0:T(256)S(1)} %copy-done.63), kind=kOutput, calls=%fused_computation.248 | convolution fusion | flops 1020690432 | bytes 10038272 | tf_op jit(solution)/shard_map/dot_general | solution.py:50
  177.4 1.1 convert_reduce_fusion
  178.5 1.1 fusion.53
  179.7 1.2 fusion.93
  181.4 0.9 copy-done.7
  182.3 4.7 %fusion.100 = f32[1152,1728]{1,0:T(8,128)} fusion(bf16[256,1728]{0,1:T(8,128)(2,1)S(1)} %bitcast.282, bf16[1,1,256,1152]{3,2,1,0:T(8,128)(2,1)S(1)} %copy-done.7, f32[1152]{0:T(1024)S(1)} %copy-done.43, f32[1152]{0:T(1024)S(1)} %copy-done.39, f32[256]{0:T(256)S(1)} %copy-done.61, f32[256]{0:T(256)S(1)} %copy-done.59), kind=kOutput, calls=%fused_computation.162 | convolution fusion | flops 1020985344 | bytes 9448448 | tf_op jit(solution)/shard_map/dot_general | solution.py:50
  187.1 1.2 copy-done.4
  188.3 2.9 fusion.9
  191.2 3.6 fusion.41
  196.1 1.3 fusion.107
  197.4 217.1 %all-reduce.13.cloned.1.call-done = (f32[1152,1728]{1,0:T(8,128)}, f32[576,1152]{0,1:T(8,128)}, f32[1152,1728]{1,0:T(8,128)}, f32[576,1152]{0,1:T(8,128)}) async-done(((f32[1152,1728]{1,0:T(8,128)}, f32[576,1152]{0,1:T(8,128)}, f32[1152,1728]{1,0:T(8,128)}, f32[576,1152]{0,1:T(8,128)}), (f32[1152,1728]{1,0:T(8,128)}, f32[576,1152]{0,1:T(8,128)}, f32[1152,1728]{1,0:T(8,128)}, ...) | async-done | bytes 21233680
  414.4 1.6 constant_dynamic-slice_fusion.3
  416.0 1.5 constant_dynamic-slice_fusion.2
  417.5 1.6 constant_dynamic-slice_fusion.1
  419.0 1.5 constant_dynamic-slice_fusion
  (200 shorter events, 20.3 us)
Async XLA Ops:
  7.2 23.2 %copy-start = (bf16[576,1152]{1,0:T(8,128)(2,1)S(1)}, bf16[576,1152]{1,0:T(8,128)(2,1)}, u32[]{:S(2)}) copy-start(bf16[576,1152]{1,0:T(8,128)(2,1)} %param.13) | copy-start | bytes 3981316
  8.2 2.8 copy-start.40
  8.2 15.1 %copy-start.38 = (f32[1152]{0:T(1024)}, f32[1152]{0:T(1024)S(1)}, u32[]{:S(2)}) copy-start(f32[1152]{0:T(1024)S(1)} %get-tuple-element.14) | copy-start | bytes 13828
  8.2 15.1 %copy-start.42 = (f32[1152]{0:T(1024)}, f32[1152]{0:T(1024)S(1)}, u32[]{:S(2)}) copy-start(f32[1152]{0:T(1024)S(1)} %get-tuple-element.13) | copy-start | bytes 13828
  8.2 22.2 %copy-start.48 = (f32[1152]{0:T(1024)}, f32[1152]{0:T(1024)S(1)}, u32[]{:S(2)}) copy-start(f32[1152]{0:T(1024)S(1)} %get-tuple-element.15) | copy-start | bytes 13828
  8.2 25.1 %copy-start.44 = (f32[1152]{0:T(1024)}, f32[1152]{0:T(1024)S(1)}, u32[]{:S(2)}) copy-start(f32[1152]{0:T(1024)S(1)} %get-tuple-element.11) | copy-start | bytes 13828
  8.2 25.1 %copy-start.46 = (f32[1152]{0:T(1024)}, f32[1152]{0:T(1024)S(1)}, u32[]{:S(2)}) copy-start(f32[1152]{0:T(1024)S(1)} %get-tuple-element.12) | copy-start | bytes 13828
  10.9 11.3 %copy-start.74 = (f32[2,2,72]{2,1,0:T(2,128)S(1)}, f32[2,2,72]{2,1,0:T(2,128)}, u32[]{:S(2)}) copy-start(f32[2,2,72]{2,1,0:T(2,128)} %param.11) | copy-start | bytes 3460
  10.9 11.8 %copy-start.5 = (bf16[1,1,256,1152]{3,2,1,0:T(8,128)(2,1)S(1)}, bf16[1,1,256,1152]{3,2,1,0:T(8,128)(2,1)}, u32[]{:S(2)}) copy-start(bf16[1,1,256,1152]{3,2,1,0:T(8,128)(2,1)} %param.8) | copy-start | bytes 1769476
  15.2 38.5 %all-to-all-start.2 = ((bf16[8,2,9216]{2,1,0:T(2,128)(2,1)}), bf16[8,2,9216]{2,1,0:T(2,128)(2,1)}, u32[]{:S(2)}, u32[]{:S(2)}) async-start(bf16[8,2,9216]{2,1,0:T(2,128)(2,1)} %reshape.739), calls=%async_computation.2 | async-start | bytes 589824 | tf_op jit(solution)/shard_map/all_to_all | solution.py:87
  22.8 5.1 %copy-start.70 = (f32[72]{0:T(128)}, f32[72]{0:T(128)S(1)}, u32[]{:S(2)}) copy-start(f32[72]{0:T(128)S(1)} %get-tuple-element.36) | copy-start | bytes 868
  22.8 5.1 %copy-start.72 = (f32[72]{0:T(128)}, f32[72]{0:T(128)S(1)}, u32[]{:S(2)}) copy-start(f32[72]{0:T(128)S(1)} %get-tuple-element.37) | copy-start | bytes 868
  22.9 4.0 copy-start.58
  23.3 3.7 copy-start.66
  23.3 3.7 copy-start.60
  26.9 3.1 copy-start.12
  27.1 1.3 copy-start.54
  30.1 2.3 copy-start.8
  30.1 1.5 copy-start.6
  30.4 2.0 copy-start.20
  31.6 2.6 copy-start.77
  53.8 18.3 %all-to-all-start = ((bf16[8,2,27648]{2,1,0:T(2,128)(2,1)}), bf16[8,2,27648]{2,1,0:T(2,128)(2,1)}, u32[]{:S(2)}, u32[]{:S(2)}) async-start(bf16[8,2,27648]{2,1,0:T(2,128)(2,1)} %reshape.737), calls=%async_computation | async-start | bytes 1769472 | tf_op jit(solution)/shard_map/all_to_all | solution.py:77
  96.6 9.0 %copy-start.24 = (f32[8,32,8]{0,2,1:T(8,128)}, f32[8,32,8]{0,2,1:T(8,128)S(1)}, u32[]{:S(2)}) copy-start(f32[8,32,8]{0,2,1:T(8,128)S(1)} %copy.78) | copy-start | bytes 24580
  105.6 3.9 copy-start.18
  105.6 3.9 copy-start.27
  105.6 1.4 copy-start.33
  109.5 1.2 copy-start.17
  109.5 1.2 copy-start.25
  109.5 1.2 copy-start.75
  109.6 1.2 copy-start.76
  110.7 2.7 copy-start.29
  119.1 22.8 %all-to-all-start.1 = ((bf16[8,32,576]{2,1,0:T(8,128)(2,1)}), bf16[8,32,576]{2,1,0:T(8,128)(2,1)}, u32[]{:S(2)}, u32[]{:S(2)}) async-start(bf16[8,32,576]{2,1,0:T(8,128)(2,1)} %reshape.711), calls=%async_computation.1 | async-start | bytes 655360 | tf_op jit(solution)/shard_map/all_to_all | solution.py:79
  132.2 2.2 copy-start.16
  132.2 2.2 copy-start.23
  132.2 2.2 copy-start.26
  132.2 2.3 copy-start.30
  134.4 1.2 copy-start.19
  134.4 1.2 copy-start.28
  134.4 1.4 copy-start.32
  141.9 6.0 %copy-start.37 = (f32[8,256]{1,0:T(8,128)S(1)}, f32[8,256]{1,0:T(8,128)}, u32[]{:S(2)}) copy-start(f32[8,256]{1,0:T(8,128)} %copy-done.36) | copy-start | bytes 24580
  141.9 6.0 %copy-start.41 = (f32[1152]{0:T(1024)S(1)}, f32[1152]{0:T(1024)}, u32[]{:S(2)}) copy-start(f32[1152]{0:T(1024)} %copy-done.40) | copy-start | bytes 13828
  141.9 18.5 %all-to-all-start.3 = ((bf16[8,32,1728]{2,1,0:T(8,128)(2,1)}), bf16[8,32,1728]{2,1,0:T(8,128)(2,1)}, u32[]{:S(2)}, u32[]{:S(2)}) async-start(bf16[8,32,1728]{2,1,0:T(8,128)(2,1)} %reshape.714), calls=%async_computation.3 | async-start | bytes 1835008 | tf_op jit(solution)/shard_map/all_to_all | solution.py:89
  147.7 266.7 %all-reduce.13.cloned.1.call-start = ((), (), s32[]{:S(2)}) async-start(), calls=%async_computation.4 | async-start | bytes 44826624
  147.9 12.5 %copy-start.47 = (f32[1152]{0:T(1024)S(1)}, f32[1152]{0:T(1024)}, u32[]{:S(2)}) copy-start(f32[1152]{0:T(1024)} %copy-done.46) | copy-start | bytes 13828
  147.9 12.5 %copy-start.63 = (f32[256]{0:T(256)S(1)}, f32[256]{0:T(256)}, u32[]{:S(2)}) copy-start(f32[256]{0:T(256)} %copy-done.62) | copy-start | bytes 3076
  160.5 4.3 %copy-start.69 = (f32[256]{0:T(256)S(1)}, f32[256]{0:T(256)}, u32[]{:S(2)}) copy-start(f32[256]{0:T(256)} %copy-done.68) | copy-start | bytes 3076
  160.5 4.3 %copy-start.3 = (f32[256,1152]{1,0:T(8,128)S(1)}, f32[256,1152]{1,0:T(8,128)}, u32[]{:S(2)}) copy-start(f32[256,1152]{1,0:T(8,128)} %copy-done.2) | copy-start | bytes 3538948
  160.5 4.3 %copy-start.65 = (f32[256]{0:T(256)S(1)}, f32[256]{0:T(256)}, u32[]{:S(2)}) copy-start(f32[256]{0:T(256)} %copy-done.64) | copy-start | bytes 3076
  164.8 1.1 copy-start.22
  166.1 1.2 copy-start.21
  167.3 2.3 copy-start.45
  169.6 5.9 %copy-start.9 = (bf16[8,256,256]{1,2,0:T(8,128)(2,1)S(1)}, bf16[8,256,256]{1,2,0:T(8,128)(2,1)}, u32[]{:S(2)}) copy-start(bf16[8,256,256]{1,2,0:T(8,128)(2,1)} %copy-done.8) | copy-start | bytes 3145732
  175.5 1.2 copy-start.13
  175.5 1.2 copy-start.35
  177.4 1.1 copy-start.51
  177.4 1.1 copy-start.71
  177.4 1.1 copy-start.73
  178.5 1.1 copy-start.53
  179.7 1.3 copy-start.55
  179.7 1.3 copy-start.57
  187.0 1.3 copy-start.4
  191.2 3.6 copy-start.67
  194.8 1.2 copy-start.11
  195.3 225.2 %copy-start.1 = (bf16[576,1152]{1,0:T(8,128)(2,1)S(1)}, bf16[576,1152]{1,0:T(8,128)(2,1)}, u32[]{:S(2)}) copy-start(bf16[576,1152]{1,0:T(8,128)(2,1)} %param.13) | copy-start | bytes 3981316
  (19 other events, 16.2 us)
Sparse Core Ops, SparseCore 0:
  187.2 227.1 all-reduce.12
where the time goes:
time: 434 us; the launch traced here: 428 us
  waiting for transfers between devices  229 us (53%)
  local copies, waits for them, and re-layouts  78.4 us (18%)
  matrix products  51.4 us (12%)
  other arithmetic  30.3 us (7%)
  starting transfers between devices  22.7 us (5%)
  between operations  15.3 us (4%)
    unnamed x2, waiting for transfers between devices  217 us
    unnamed x165, local copies, waits for them, and re-layouts  32.8 us
    dot_general x4, matrix products, outer_sum(): lax.dot_general(flat_left, flat_right, (((0,), (0,)), ((), ())), preferre...  16.3 us
    unnamed x2, other arithmetic  11.1 us
    dot_general x4, matrix products, times_t(): lax.dot_general(left, weight, (((left.ndim - 1,), (1,)), ((), ())), prefe...  10.6 us
    all_to_all x1, waiting for transfers between devices, shards(): lax.all_to_all(qkv_grad_patch, 'seq', split_axis=0, concat_axis=1, tiled=...  9.11 us
  transfers between devices with their start and end apart: 5, of which 3 were waited for; matrix products, arithmetic and copies ran while one was open for 16% of the time, Pallas kernels for 0%

commit v1 on v0

v1 whole, which is shorter than its diff:
```python
import jax
import jax.numpy as jnp
from jax import lax
from jax.experimental import pallas as pl
from jax.experimental.pallas import tpu as pltpu
from jax.sharding import PartitionSpec as P

T = 256
D = 1152
HEADS = 8
HEAD_DIM = 72
A = HEADS * HEAD_DIM
Q = 3 * A
A_PAD = 640
Q_PAD = 1792
LOCAL = 32
EPS = 1e-06
BF = jnp.bfloat16
F32 = jnp.float32
MESH = ("dp", "seq")
VMEM_LIMIT = 48 * 1024 * 1024


def dot(left, right, over_left, over_right):
    return lax.dot_general(
        left, right, (((over_left,), (over_right,)), ((), ())), preferred_element_type=F32
    )


def call(body, outs, args, flops, scratch=()):
    shapes = tuple(jax.ShapeDtypeStruct(shape, kind) for shape, kind in outs)
    size = sum(x.size * x.dtype.itemsize for x in args)
    size += sum(x.size * x.dtype.itemsize for x in shapes)
    return pl.pallas_call(
        body,
        out_shape=shapes,
        in_specs=[pl.BlockSpec(memory_space=pltpu.VMEM)] * len(args),
        out_specs=tuple(pl.BlockSpec(memory_space=pltpu.VMEM) for _ in shapes),
        scratch_shapes=list(scratch),
        cost_estimate=pl.CostEstimate(flops=flops, bytes_accessed=size, transcendentals=0),
        compiler_params=pltpu.CompilerParams(vmem_limit_bytes=VMEM_LIMIT),
    )(*args)


def normalized(x32):
    mean = jnp.mean(x32, axis=-1, keepdims=True)
    centered = x32 - mean
    spread = lax.rsqrt(jnp.mean(centered * centered, axis=-1, keepdims=True) + EPS)
    return centered * spread, spread


def normalized_back(unit, spread, scale, grad):
    grad = grad * (1.0 + scale)
    inner = jnp.mean(grad * unit, axis=-1, keepdims=True)
    return spread * (grad - jnp.mean(grad, axis=-1, keepdims=True) - unit * inner)


def flip(source, target, blocks):
    for b in range(blocks):
        target[128 * b : 128 * b + 128, :] = source[:, 128 * b : 128 * b + 128].T


def flip_back(source, target, blocks):
    for b in range(blocks):
        target[:, 128 * b : 128 * b + 128] = source[128 * b : 128 * b + 128, :].T


def head_rows(which, h):
    start = which * A + h * HEAD_DIM
    return slice(start, start + HEAD_DIM)


def head_norm(rows, gain):
    root = lax.rsqrt(jnp.mean(rows * rows, axis=0, keepdims=True) + EPS)
    return root, (rows * root * gain).astype(BF)


def head_norm_back(rows, root, gain, grad):
    grad = grad.astype(BF).astype(F32) * gain
    inner = jnp.mean(rows * grad, axis=0, keepdims=True)
    return (root * grad - rows * (root * root * root * inner)).astype(BF).astype(F32)


def same_patch():
    key = lax.broadcasted_iota(jnp.int32, (T, T), 0)
    query = lax.broadcasted_iota(jnp.int32, (T, T), 1)
    return ((key ^ query) & (LOCAL - 1)) == 0


def head_probs(queries, keys, mask):
    scores = dot(keys, queries, 0, 0) * HEAD_DIM ** (-0.5)
    if mask is not None:
        scores = jnp.where(mask, scores, -1e30)
    expo = jnp.exp(scores - jnp.max(scores, axis=0, keepdims=True))
    return expo * (1.0 / jnp.sum(expo, axis=0, keepdims=True))


def head_back(q_rows, k_rows, v_rows, gains, probs, grad):
    q_root, queries = head_norm(q_rows, gains[0])
    k_root, keys = head_norm(k_rows, gains[1])
    grad = grad.astype(BF)
    probs16 = probs.astype(BF)
    v_grad = dot(grad, probs16, 1, 1).astype(BF).astype(F32)
    p_grad = dot(v_rows.astype(BF), grad, 0, 0).astype(BF).astype(F32)
    inner = jnp.sum(p_grad * probs, axis=0, keepdims=True)
    s_grad = (probs * (p_grad - inner) * HEAD_DIM ** (-0.5)).astype(BF)
    q_grad = head_norm_back(q_rows, q_root, gains[0], dot(keys, s_grad, 1, 0))
    k_grad = head_norm_back(k_rows, k_root, gains[1], dot(queries, s_grad, 1, 1))
    return q_grad, k_grad, v_grad


def order(core, chip):
    row = lax.broadcasted_iota(jnp.int32, (1, A), 1)
    part = (row >= 192).astype(jnp.int32) + (row >= 384).astype(jnp.int32)
    rest = row - 192 * part
    first = (rest * 171) >> 12
    rest = rest - 24 * first
    second = (rest * 11) >> 5
    piece = 3 * part + rest - 3 * second
    place = []
    for axis in range(3):
        step = axis - part
        step = jnp.where(step < 0, step + 3, step)
        one = jnp.where(step == 0, first >> 2, jnp.where(step == 1, first >> 1, first)) & 1
        two = (second >> (2 - axis)) & 1
        near = jnp.where(core == 0, one, two) ^ ((chip[axis] ^ (chip[axis] >> 1)) & 1)
        far = jnp.where(core == 0, two, one) ^ (chip[axis] >> 1)
        place.append(2 * far + (near ^ far))
    x, y, z = place
    device = x * 32 + (y >> 1) * 16 + core * 8 + (y & 1) * 4 + z
    return 9 * device + piece


def position():
    dp, seq = lax.axis_index("dp"), lax.axis_index("seq")
    return dp & 1, (dp >> 2, ((dp >> 1) & 1) * 2 + (seq >> 2), seq & 3)


def picker(core, chip):
    feature = lax.broadcasted_iota(jnp.int32, (D, A), 0)
    return (feature == order(core, chip)).astype(F32).astype(BF)


def pickers():
    core, chip = position()
    return picker(core, chip), picker(1 - core, chip)


def forward_spatial(
    latents, cot, mod, gains, w_qkv, w_out, w_out_t,
    both, qkv_t, probs_t, normed, att, scaled_t, wide, flat, tall
):
    scaled = (mod[5:6, :] * cot[...].astype(F32)).astype(BF)
    scaled_t[...] = scaled
    both[:, D:] = dot(scaled, w_out_t[...], 1, 1).astype(BF)
    unit, _ = normalized(latents[...].astype(F32))
    norm = (unit * (1.0 + mod[1:2, :]) + mod[0:1, :]).astype(BF)
    normed[...] = norm
    wide[:, Q:] = jnp.zeros((T, Q_PAD - Q), F32)
    wide[:, :Q] = dot(norm, w_qkv[...], 1, 0).astype(BF).astype(F32)
    flip(wide, qkv_t, Q_PAD // 128)
    tall[A:, :] = jnp.zeros((A_PAD - A, T), F32)
    for h in range(HEADS):
        queries = head_norm(qkv_t[head_rows(0, h), :], gains[:, 0:1])[1]
        keys = head_norm(qkv_t[head_rows(1, h), :], gains[:, 1:2])[1]
        probs = head_probs(queries, keys, None)
        probs_t[h] = probs
        values = qkv_t[head_rows(2, h), :].astype(BF)
        tall[head_rows(0, h), :] = dot(values, probs.astype(BF), 1, 0)
    flip_back(tall, flat, A_PAD // 128)
    att16 = flat[:, :A].astype(BF)
    att[...] = att16
    result = dot(att16, w_out[...], 1, 0)
    both[:, :D] = (latents[...].astype(F32) + mod[2:3, :] * result).astype(BF)


def temporal(
    both, mod, gains, w_qkv, back, normed, qkv_grad, wide, tall_qkv, tall_grad, flat, tall, tall_att
):
    unit, _ = normalized(both[:, :D].astype(F32))
    norm = (unit * (1.0 + mod[4:5, :]) + mod[3:4, :]).astype(BF)
    normed[...] = norm
    wide[:, Q:] = jnp.zeros((T, Q_PAD - Q), F32)
    wide[:, :Q] = dot(norm, w_qkv[...], 1, 0).astype(BF).astype(F32)
    flip(wide, tall_qkv, Q_PAD // 128)
    flat[:, A:] = jnp.zeros((T, A_PAD - A), F32)
    flat[:, :A] = both[:, D:].astype(F32)
    flip(flat, tall, A_PAD // 128)
    tall_att[A:, :] = jnp.zeros((A_PAD - A, T), F32)
    tall_grad[Q:, :] = jnp.zeros((Q_PAD - Q, T), F32)
    mask = same_patch()
    pair = (gains[:, 0:1], gains[:, 1:2])
    for h in range(HEADS):
        q_rows = tall_qkv[head_rows(0, h), :]
        k_rows = tall_qkv[head_rows(1, h), :]
        v_rows = tall_qkv[head_rows(2, h), :]
        probs = head_probs(head_norm(q_rows, pair[0])[1], head_norm(k_rows, pair[1])[1], mask)
        tall_att[head_rows(0, h), :] = dot(v_rows.astype(BF), probs.astype(BF), 1, 0)
        grads = head_back(q_rows, k_rows, v_rows, pair, probs, tall[head_rows(0, h), :])
        for which in range(3):
            tall_grad[head_rows(which, h), :] = grads[which]
    flip_back(tall_att, flat, A_PAD // 128)
    back[:, D:] = flat[:, :A].astype(BF)
    flip_back(tall_grad, wide, Q_PAD // 128)
    grad = wide[:, :Q].astype(BF)
    qkv_grad[...] = grad
    back[:, :D] = dot(grad, w_qkv[...], 1, 1).astype(BF)


def pick_two(first, second, mine, theirs):
    own, other = pickers()
    for k, source in enumerate((first, second)):
        mine[:, k * A : k * A + A] = dot(source[...], own, 1, 0).astype(BF)
        theirs[:, k * A : k * A + A] = dot(source[...], other, 1, 0).astype(BF)


def pick_one(source, mine, theirs):
    own, other = pickers()
    mine[...] = dot(source[...], own, 1, 0).astype(BF)
    theirs[...] = dot(source[...], other, 1, 0).astype(BF)


def enter_spatial_back(back, both, cot, mod, w_out, mid_grad, att_grad, mine, theirs):
    unit, spread = normalized(both[:, :D].astype(F32))
    grad = normalized_back(unit, spread, mod[4:5, :], back[:, :D].astype(F32))
    total = (cot[...].astype(F32) + grad).astype(BF)
    mid_grad[...] = total
    scaled = (mod[2:3, :] * total.astype(F32)).astype(BF)
    att_grad[...] = dot(scaled, w_out[...], 1, 1).astype(BF)
    own, other = pickers()
    mine[...] = dot(scaled, own, 1, 0).astype(BF)
    theirs[:, :A] = dot(scaled, other, 1, 0).astype(BF)
    theirs[:, A:] = back[:, D:]


def spatial_attention_back(
    att_grad, qkv_t, probs_t, gains, qkv_grad, tall_grad, wide, flat, tall
):
    flat[:, A:] = jnp.zeros((T, A_PAD - A), F32)
    flat[:, :A] = att_grad[...].astype(F32)
    flip(flat, tall, A_PAD // 128)
    tall_grad[Q:, :] = jnp.zeros((Q_PAD - Q, T), F32)
    pair = (gains[:, 0:1], gains[:, 1:2])
    for h in range(HEADS):
        grads = head_back(
            qkv_t[head_rows(0, h), :], qkv_t[head_rows(1, h), :], qkv_t[head_rows(2, h), :],
            pair, probs_t[h], tall[head_rows(0, h), :]
        )
        for which in range(3):
            tall_grad[head_rows(which, h), :] = grads[which]
    flip_back(tall_grad, wide, Q_PAD // 128)
    qkv_grad[...] = wide[:, :Q].astype(BF)


def leave_spatial_back(mid_grad, qkv_grad, latents, mod, w_qkv, latents_grad):
    norm_grad = dot(qkv_grad[...], w_qkv[...], 1, 1).astype(BF).astype(F32)
    unit, spread = normalized(latents[...].astype(F32))
    grad = normalized_back(unit, spread, mod[1:2, :], norm_grad)
    latents_grad[...] = (mid_grad[...].astype(F32) + grad).astype(BF)


def project_output(both, back, mod, w_out, output):
    result = dot(back[:, D:], w_out[...], 1, 0)
    output[...] = (both[:, :D].astype(F32) + mod[5:6, :] * result).astype(BF)


def weight_rows(columns):
    def body(*refs):
        keep, sends = refs[-4], refs[-3:]
        ins = refs[:-4]
        start = 0
        for k, width in enumerate(columns):
            left, left_in, right, right_in = (ref[...] for ref in ins[4 * k : 4 * k + 4])
            total = dot(left, right, 0, 0) + dot(left_in, right_in, 0, 0)
            padded = -(-width // 128) * 128
            for p in range(3):
                rows = total[192 * p : 192 * p + 192]
                keep[p, :, start : start + width] = rows[:96]
                sends[p][:, start : start + width] = rows[96:].astype(BF)
                if padded > width:
                    keep[p, :, start + width : start + padded] = jnp.zeros((96, padded - width), F32)
                    sends[p][:, start + width : start + padded] = jnp.zeros((96, padded - width), BF)
            start += padded

    return body


def add_halve(keep, got, kept, send):
    half = kept.shape[0]
    total = keep[...] + got[...].astype(F32)
    kept[...] = total[:half]
    send[...] = total[half:].astype(BF)


def add_halve_first(keep, got, kept, send):
    half = kept.shape[0]
    total = keep[0] + got[...].astype(F32)
    kept[...] = total[:half]
    send[...] = total[half:].astype(BF)


def make_add_halve_first(p):
    def body(keep, got, kept, send):
        half = kept.shape[0]
        total = keep[p] + got[...].astype(F32)
        kept[...] = total[:half]
        send[...] = total[half:].astype(BF)

    return body


def join_halve(*refs):
    kept, send = refs[-2:]
    ins = refs[:-2]
    start = 0
    for g in range(0, len(ins), 6):
        width = ins[g].shape[1]
        for p in range(3):
            total = ins[g + p][...] + ins[g + 3 + p][...].astype(F32)
            half = total.shape[0] // 2
            kept[p, :, start : start + width] = total[:half]
            send[p, :, start : start + width] = total[half:].astype(BF)
        start += width


def tail_halve(keep, got, kept, send):
    half = kept.shape[1]
    for p in range(3):
        total = keep[p] + got[p].astype(F32)
        kept[p] = total[:half]
        send[p] = total[half:].astype(BF)


def last_add(keep, got, *outs):
    start = 0
    for out in outs:
        width = out.shape[1]
        for p in range(3):
            rows = keep[p, :, start : start + width] + got[p, :, start : start + width].astype(F32)
            out[3 * p : 3 * p + 3, :] = rows
        start += -(-width // 128) * 128


def pairs(change):
    found = []
    for device in range(128):
        dp, seq = divmod(device, 8)
        x, y, z, core = dp >> 2, ((dp >> 1) & 1) * 2 + (seq >> 2), seq & 3, dp & 1
        x, y, z, core = change(x, y, z, core)
        found.append((device, (x * 4 + (y >> 1) * 2 + core) * 8 + (y & 1) * 4 + z))
    return found


def to_other_core(value):
    return lax.ppermute(value, MESH, pairs(lambda x, y, z, c: (x, y, z, 1 - c)))


def along(value, axis, late):
    def change(x, y, z, core):
        place = [x, y, z]
        place[axis] ^= 1 if (core == 0) != late else 3
        return (*place, core)

    return lax.ppermute(value, MESH, pairs(change))


def early_rounds(keep, sends):
    columns = keep.shape[2]
    kept, out = [], []
    for p in range(3):
        got = along(sends[p], p, False)
        mine, send = call(
            make_add_halve_first(p),
            [((48, columns), F32), ((48, columns), BF)],
            (keep, got),
            96 * columns,
        )
        kept.append(mine)
        out.append(send)
    for p in range(3):
        got = along(out[p], (p + 1) % 3, False)
        kept[p], out[p] = call(
            add_halve, [((24, columns), F32), ((24, columns), BF)], (kept[p], got), 48 * columns
        )
    return kept, [along(out[p], (p + 2) % 3, False) for p in range(3)]


def weight_partials(groups, columns):
    width = sum(-(-w // 128) * 128 for w in columns)
    outs = [((3, 96, width), F32)] + [((96, width), BF)] * 3
    args = [x for group in groups for x in group]
    keep, *sends = call(weight_rows(columns), outs, args, 2 * 512 * A * width)
    return keep, sends


def shards(
    latents, cotangent, modulation, qk_gains, spatial_qkv, spatial_out, temporal_qkv, temporal_out
):
    x, cot = latents.reshape(T, D), cotangent.reshape(T, D)
    mod = modulation.reshape(6, D)
    gains_s, gains_t = qk_gains[0].T, qk_gains[1].T
    wide, tall_qkv = pltpu.VMEM((T, Q_PAD), F32), pltpu.VMEM((Q_PAD, T), F32)
    flat, tall = pltpu.VMEM((T, A_PAD), F32), pltpu.VMEM((A_PAD, T), F32)

    both, qkv_t, probs_t, normed_s, att_s, scaled_t = call(
        forward_spatial,
        [
            ((T, D + A), BF), ((Q_PAD, T), F32), ((HEADS, T, T), F32),
            ((T, D), BF), ((T, A), BF), ((T, D), BF),
        ],
        (x, cot, mod, gains_s, spatial_qkv, spatial_out, temporal_out),
        2 * T * D * (Q + 2 * A),
        (wide, flat, tall),
    )
    patch = lax.all_to_all(both.reshape(8, LOCAL, D + A), "seq", 0, 0, tiled=True)
    early_mine, early_theirs = call(
        pick_two, [((T, D), BF), ((T, D), BF)], (normed_s, scaled_t), 4 * T * D * D
    )
    early_in, att_s_in = to_other_core(early_theirs), to_other_core(att_s)

    back_patch, normed_t, qkv_grad_t = call(
        temporal,
        [((T, D + A), BF), ((T, D), BF), ((T, Q), BF)],
        (patch.reshape(T, D + A), mod, gains_t, temporal_qkv),
        4 * T * D * Q,
        (wide, tall_qkv, tall_qkv, flat, tall, tall),
    )
    back = lax.all_to_all(back_patch.reshape(8, LOCAL, D + A), "seq", 0, 0, tiled=True)
    back = back.reshape(T, D + A)
    t_mine, t_theirs = call(pick_one, [((T, A), BF), ((T, A), BF)], (normed_t,), 4 * T * D * A)
    t_in, qkv_grad_t_in = to_other_core(t_theirs), to_other_core(qkv_grad_t)
    keep_t, sends_t = weight_partials([(t_mine, t_in, qkv_grad_t, qkv_grad_t_in)], (Q,))
    kept_t, got_t = early_rounds(keep_t, sends_t)

    mid_grad, att_grad_s, late_mine, late_theirs = call(
        enter_spatial_back,
        [((T, D), BF), ((T, A), BF), ((T, A), BF), ((T, D), BF)],
        (back, both, cot, mod, spatial_out),
        6 * T * D * A,
    )
    late_in = to_other_core(late_theirs)
    (qkv_grad_s,) = call(
        spatial_attention_back,
        [((T, Q), BF)],
        (att_grad_s, qkv_t, probs_t, gains_s),
        2 * T * T * HEADS * 128 * 5,
        (tall_qkv, wide, flat, tall),
    )
    qkv_grad_s_in = to_other_core(qkv_grad_s)
    (latents_grad,) = call(
        leave_spatial_back,
        [((T, D), BF)],
        (mid_grad, qkv_grad_s, x, mod, spatial_qkv),
        2 * T * D * Q,
    )
    (output,) = call(
        project_output, [((T, D), BF)], (both, back, mod, temporal_out), 2 * T * D * A
    )
    keep_s, sends_s = weight_partials(
        [
            (early_mine[:, :A], early_in[:, :A], qkv_grad_s, qkv_grad_s_in),
            (late_mine, late_in[:, :A], att_s, att_s_in),
            (early_mine[:, A:], early_in[:, A:], back[:, D:], late_in[:, A:]),
        ],
        (Q, A, A),
    )
    kept_s, got_s = early_rounds(keep_s, sends_s)
    columns = Q_PAD * 2 + A_PAD * 2
    kept, send = call(
        join_halve,
        [((3, 12, columns), F32), ((3, 12, columns), BF)],
        (*kept_s, *got_s, *kept_t, *got_t),
        72 * columns,
    )
    got = along(send, 0, True)
    kept, send = call(
        tail_halve, [((3, 6, columns), F32), ((3, 6, columns), BF)], (kept, got), 36 * columns
    )
    got = along(send, 1, True)
    kept, send = call(
        tail_halve, [((3, 3, columns), F32), ((3, 3, columns), BF)], (kept, got), 18 * columns
    )
    got = along(send, 2, True)
    sq, so, to, tq = call(
        last_add,
        [((9, Q), F32), ((9, A), F32), ((9, A), F32), ((9, Q), F32)],
        (kept, got),
        9 * columns,
    )
    shape = (1, 1, T, D)
    return output.reshape(shape), latents_grad.reshape(shape), sq, so.T, tq, to.T


def solution(mesh):
    tokens = P("dp", "seq", None, None)
    rows, cols = P(("dp", "seq"), None), P(None, ("dp", "seq"))
    return jax.shard_map(
        shards,
        mesh=mesh,
        in_specs=(tokens, tokens, P("dp", None, None, None), P(), P(), P(), P(), P()),
        out_specs=(tokens, tokens, rows, cols, rows, cols),
        check_vma=False,
    )
```

time: 434 us -> 169 us (0.39); the launches traced: 428 us -> 167 us
  waiting for transfers between devices: 229 us -> 32.7 us
  Pallas kernels: 0 us -> 52.3 us
  matrix products: 51.4 us -> 0 us
  local copies, waits for them, and re-layouts: 78.4 us -> 45.2 us
  other arithmetic: 30.3 us -> 0 us
  between operations: 15.3 us -> 1 us
  starting transfers between devices: 22.7 us -> 36.1 us
    unnamed x2 -> x0, waiting for transfers between devices: 217 us -> none
    pallas_call x0 -> x26, Pallas kernels: none -> 52.3 us  [call(): pl.pallas_call(body, out_shape=shapes, in_specs=[pl.BlockSpec(memory_spac...]
    dot_general x24 -> x0, matrix products: 51.4 us -> none  [the longest x4 16.3 us: outer_sum(): lax.dot_general(flat_left, flat_right, (((0,), (0,)), ((), ())), preferre...]
    ppermute x0 -> x27, starting transfers between devices: none -> 25.9 us  [the longest x21 23.9 us: along(): return lax.ppermute(value, MESH, pairs(change))]
    ppermute x0 -> x27, waiting for transfers between devices: none -> 17.9 us  [the longest x21 17.8 us: along(): return lax.ppermute(value, MESH, pairs(change))]
    reshape x4 -> x1, local copies, waits for them, and re-layouts: 12.4 us -> 0.02 us  [shards(): mod = modulation.reshape(6, D)]
    all_to_all x4 -> x2, starting transfers between devices: 22.5 us -> 10.1 us  [the longest x1 6.41 us: shards(): lax.all_to_all(both.reshape(8, LOCAL, D + A), 'seq', 0, 0, tiled=True)]
    all_to_all x2 -> x0, local copies, waits for them, and re-layouts: 11.3 us -> none  [the longest x1 7.63 us: shards(): lax.all_to_all(qkv_frame, 'seq', split_axis=1, concat_axis=0, tiled=True)]
  transfers between devices with their start and end apart: 5 -> 29, of which waited for: 3 -> 9; matrix products, arithmetic and copies ran while one was open for 16% -> 11% of each run, Pallas kernels for 0% -> 19%
where the time goes in v1:
time: 169 us; the launch traced here: 167 us
  Pallas kernels  52.3 us (31%)
  local copies, waits for them, and re-layouts  45.2 us (27%)
  starting transfers between devices  36.1 us (21%)
  waiting for transfers between devices  32.7 us (19%)
    pallas_call x26, Pallas kernels, call(): pl.pallas_call(body, out_shape=shapes, in_specs=[pl.BlockSpec(memory_spac...  52.3 us
    unnamed x79, local copies, waits for them, and re-layouts  33.2 us
    ppermute x21, starting transfers between devices, along(): return lax.ppermute(value, MESH, pairs(change))  23.9 us
    ppermute x21, waiting for transfers between devices, along(): return lax.ppermute(value, MESH, pairs(change))  17.8 us
    all_to_all x1, waiting for transfers between devices, shards(): lax.all_to_all(back_patch.reshape(8, LOCAL, D + A), 'seq', 0, 0, tiled=True)  7.99 us
    all_to_all x1, waiting for transfers between devices, shards(): lax.all_to_all(both.reshape(8, LOCAL, D + A), 'seq', 0, 0, tiled=True)  6.82 us
    all_to_all x1, starting transfers between devices, shards(): lax.all_to_all(both.reshape(8, LOCAL, D + A), 'seq', 0, 0, tiled=True)  6.41 us
    ppermute x2, local copies, waits for them, and re-layouts, to_other_core(): return lax.ppermute(value, MESH, pairs(lambda x, y, z, c: (x, y, z, 1 - c)))  4.47 us
  transfers between devices with their start and end apart: 29, of which 9 were waited for; matrix products, arithmetic and copies ran while one was open for 11% of the time, Pallas kernels for 19%

profile of v1, /device:TPU:0, one launch (start us, length us, event | category | flops | bytes accessed | tf_op | source)
XLA Modules:
  0.0 167.3 jit_solution(8783955142287277633)
XLA Ops:
  2.3 6.6 %copy.28.w_qkv = bf16[1152,1728]{1,0:T(8,128)(2,1)} copy(bf16[1152,1728]{0,1:T(8,128)(2,1)} %param.12) | data formatting | bytes 7962624 | tf_op args[4]
  8.9 9.3 %shard_map.127 = (bf16[256,1728]{1,0:T(8,128)(2,1)}, f32[1792,256]{1,0:T(8,128)}, f32[8,256,256]{2,1,0:T(8,128)}, bf16[256,1152]{1,0:T(8,128)(2,1)S(1)}, bf16[25...) custom-call(bf16[256,1152]{1,0:T(8,128)(2,1)S(1)} %bitcast.19, bf16[256,1152]{1,0:T(8,128)(2,1)S(1)} %bitcast.21, ...), custom_call_target="tpu_custom_call" | custom-call | flops 1698693120 | bytes 14134848 | tf_op jit(solution)/shard_map/pallas_call | solution.py:34
  18.2 0.8 copy-done.25
  19.0 0.8 copy-done.27
  20.5 6.4 %all-to-all-start = ((bf16[8,32,1728]{2,1,0:T(8,128)(2,1)}), bf16[8,32,1728]{2,1,0:T(8,128)(2,1)S(1)}, u32[]{:S(2)}, u32[]{:S(2)}) async-start(bf16[8,32,1728]{2,1,0:T(8,128)(2,1)} %bitcast.4), calls=%async_computation | async-start | bytes 1835008 | tf_op jit(solution)/shard_map/all_to_all | solution.py:415
  27.0 6.5 %copy.30.w_qkv = bf16[1152,1728]{1,0:T(8,128)(2,1)} copy(bf16[1152,1728]{0,1:T(8,128)(2,1)} %param.14) | data formatting | bytes 7962624 | tf_op args[6]
  33.5 6.8 %all-to-all-done = bf16[8,32,1728]{2,1,0:T(8,128)(2,1)S(1)} async-done(((bf16[8,32,1728]{2,1,0:T(8,128)(2,1)}), bf16[8,32,1728]{2,1,0:T(8,128)(2,1)S(1)}, u32[]{:S(2)}, u32[]{:S(2)}) %all-to-all-start) | async-done | bytes 884768 | tf_op jit(solution)/shard_map/all_to_all | solution.py:415
  40.3 10.3 %shard_map.128 = (bf16[256,1728]{1,0:T(8,128)(2,1)S(1)}, bf16[256,1152]{1,0:T(8,128)(2,1)S(1)}, bf16[256,1728]{1,0:T(8,128)(2,1)S(1)}) custom-call(bf16[256,1728]{1,0:T(8,128)(2,1)S(1)} %bitcast.24, f32[6,1152]{1,0:T(8,128)S(1)} %reshape.41.mod, f32[72,2]{1,0:T(8,128)S(1)} %bitcast.27, bf16[1152,1728]{1,0:T(8,128)(2,1)} %copy.30.w_qkv), custom_call_target="tpu_custom_call" | custom-call | flops 2038431744 | bytes 7253568 | tf_op jit(solution)/shard_map/pallas_call | solution.py:34
  50.6 1.0 copy-done.14
  51.6 0.9 copy-done.17
  52.5 0.8 copy-done.35
  53.3 3.7 %all-to-all-start.1 = ((bf16[8,32,1728]{2,1,0:T(8,128)(2,1)}), bf16[8,32,1728]{2,1,0:T(8,128)(2,1)S(1)}, u32[]{:S(2)}, u32[]{:S(2)}) async-start(bf16[8,32,1728]{2,1,0:T(8,128)(2,1)} %bitcast.23), calls=%async_computation.1 | async-start | bytes 1835008 | tf_op jit(solution)/shard_map/all_to_all | solution.py:428
  57.1 1.1 copy-done.26
  58.1 1.1 copy-done.28
  59.2 3.3 %shard_map.133 = (bf16[256,1152]{1,0:T(8,128)(2,1)S(1)}, bf16[256,1152]{1,0:T(8,128)(2,1)}) custom-call(bf16[256,1152]{1,0:T(8,128)(2,1)S(1)} %copy-done.26, bf16[256,1152]{1,0:T(8,128)(2,1)S(1)} %copy-done.28), custom_call_target="tpu_custom_call" | custom-call | flops 1358954496 | bytes 2359296 | tf_op jit(solution)/shard_map/pallas_call | solution.py:34
  62.6 8.0 %all-to-all-done.1 = bf16[8,32,1728]{2,1,0:T(8,128)(2,1)S(1)} async-done(((bf16[8,32,1728]{2,1,0:T(8,128)(2,1)}), bf16[8,32,1728]{2,1,0:T(8,128)(2,1)S(1)}, u32[]{:S(2)}, u32[]{:S(2)}) %all-to-all-start.1) | async-done | bytes 884768 | tf_op jit(solution)/shard_map/all_to_all | solution.py:428
  70.6 4.0 %shard_map.130 = (bf16[256,1152]{1,0:T(8,128)(2,1)S(1)}, bf16[256,576]{1,0:T(8,128)(2,1)S(1)}, bf16[256,576]{1,0:T(8,128)(2,1)S(1)}, bf16[256,1152]{1,0:T(8,128)(2,1)S(1)}) custom-call(bf16[256,1728]{1,0:T(8,128)(2,1)S(1)} %bitcast.16, bf16[256,1728]{1,0:T(8,128)(2,1)} %get-tuple-element.65.both, bf16[256,1152]{1,0:T(8,128)(2,1)S(1)} %bitcast.22, ...), custom_call_target="tpu_custom_call" | custom-call | flops 1019215872 | bytes 5483520 | tf_op jit(solution)/shard_map/pallas_call | solution.py:34
  74.6 0.8 copy-done.19
  76.1 0.8 copy-done.24
  77.0 1.5 copy-done.11
  78.5 2.9 %shard_map.131.qkv_grad.refs_2_ = bf16[256,1728]{1,0:T(8,128)(2,1)S(1)} custom-call(bf16[256,576]{1,0:T(8,128)(2,1)S(1)} %get-tuple-element.68.att_grad, f32[1792,256]{1,0:T(8,128)S(1)} %copy-done.11, f32[8,256,256]{2,1,0:T(8,128)S(1)} %copy-done.10, f32[72,2]{1,0:T(8,128)S(1)} %bitcast.26), custom_call_target="tpu_custom_call" | custom-call | flops 671088640 | bytes 5112384 | tf_op jit(solution)/shard_map/pallas_call | solution.py:34
  81.3 1.3 copy.32
  83.2 1.0 fusion.2
  84.2 1.3 copy.34
  86.0 1.2 fusion.1
  88.0 1.2 fusion
  89.2 2.2 %copy.33.refs_3_ = bf16[256,1728]{1,0:T(8,128)(2,1)} copy(bf16[256,1728]{0,1:T(8,128)(2,1)} %collective-permute-done.1) | data formatting | bytes 1769472 | tf_op jit(solution)/shard_map/ppermute | solution.py:355
  91.5 1.0 copy-done.23
  92.5 1.0 copy-done.30
  93.4 1.0 copy-done.32
  94.4 5.7 %shard_map.134 = (f32[3,96,3072]{2,1,0:T(8,128)}, bf16[96,3072]{1,0:T(8,128)(2,1)}, bf16[96,3072]{1,0:T(8,128)(2,1)}, bf16[96,3072]{1,0:T(8,128)(2,1)}) custom-call(bf16[256,576]{1,0:T(8,128)(2,1)S(1)} %copy-done.22, bf16[256,576]{1,0:T(8,128)(2,1)S(1)} %get-tuple-element.127.refs_1_, bf16[256,1728]{1,0:T(8,128)(2,1)S(1)} %shard_map.131.qkv_grad.refs_2_, ...), custom_call_target="tpu_custom_call" | custom-call | flops 1811939328 | bytes 10027008 | tf_op jit(solution)/shard_map/pallas_call | solution.py:34
  100.1 1.5 collective-permute-start.4
  101.6 1.1 copy-done.36
  102.7 1.9 %shard_map.141 = (bf16[256,576]{1,0:T(8,128)(2,1)S(1)}, bf16[256,576]{1,0:T(8,128)(2,1)}) custom-call(bf16[256,1152]{1,0:T(8,128)(2,1)S(1)} %copy-done.36), custom_call_target="tpu_custom_call" | custom-call | flops 679477248 | bytes 1179648 | tf_op jit(solution)/shard_map/pallas_call | solution.py:34
  105.4 1.0 collective-permute-start.13
  106.4 1.5 collective-permute-start.6
  107.8 0.9 collective-permute-start.8
  108.7 2.2 %copy.35.refs_3_ = bf16[256,1728]{1,0:T(8,128)(2,1)} copy(bf16[256,1728]{0,1:T(8,128)(2,1)} %collective-permute-done.14) | data formatting | bytes 1769472 | tf_op jit(solution)/shard_map/ppermute | solution.py:355
  110.9 1.2 copy-done.16
  112.1 1.2 copy-done.18
  113.3 1.0 copy-done.34
  114.3 2.2 %shard_map.142 = (f32[3,96,1792]{2,1,0:T(8,128)S(1)}, bf16[96,1792]{1,0:T(8,128)(2,1)S(1)}, bf16[96,1792]{1,0:T(8,128)(2,1)S(1)}, bf16[96,1792]{1,0:T(8,128)(2,1)S(1)}) custom-call(bf16[256,576]{1,0:T(8,128)(2,1)S(1)} %copy-done.34, bf16[256,576]{1,0:T(8,128)(2,1)} %collective-permute-done.13.refs_1_, bf16[256,1728]{1,0:T(8,128)(2,1)S(1)} %copy-done.16, ...), custom_call_target="tpu_custom_call" | custom-call | flops 1056964608 | bytes 5455872 | tf_op jit(solution)/shard_map/pallas_call | solution.py:34
  117.4 1.2 collective-permute-start.19
  118.6 1.2 shard_map.135
  119.7 1.5 collective-permute-start.5
  121.3 1.2 shard_map.137
  122.4 0.9 collective-permute-start.7
  123.4 1.2 shard_map.139
  124.6 1.9 %collective-permute-start.9 = (bf16[48,3072]{1,0:T(8,128)(2,1)S(1)}, bf16[48,3072]{1,0:T(8,128)(2,1)S(1)}, u32[]{:S(2)}, u32[]{:S(2)}) collective-permute-start(bf16[48,3072]{1,0:T(8,128)(2,1)S(1)} %get-tuple-element.89), channel_id=1, source_target_pairs={{0,32},{1,33},{2,34},{3,35},{4,36},{5,37},{6,38},{7,39},{8,104},{9... | collective-permute-start | bytes 884744 | tf_op jit(solution)/shard_map/ppermute | solution.py:364
  127.3 1.3 collective-permute-start.18
  128.6 3.4 %collective-permute-done.16.got = bf16[48,1792]{1,0:T(8,128)(2,1)S(1)} collective-permute-done((bf16[48,1792]{1,0:T(8,128)(2,1)S(1)}, bf16[48,1792]{1,0:T(8,128)(2,1)S(1)}, u32[]{:S(2)}, u32[]{:S(2)}) %collective-permute-start.16) | collective-permute-done | bytes 172064 | tf_op jit(solution)/shard_map/ppermute | solution.py:364
  132.3 1.2 collective-permute-start.21
  133.6 0.9 collective-permute-start.10
  134.6 1.9 %collective-permute-start.11 = (bf16[24,3072]{1,0:T(8,128)(2,1)S(1)}, bf16[24,3072]{1,0:T(8,128)(2,1)S(1)}, u32[]{:S(2)}, u32[]{:S(2)}) collective-permute-start(bf16[24,3072]{1,0:T(8,128)(2,1)S(1)} %get-tuple-element.92), channel_id=1, source_target_pairs={{0,32},{1,33},{2,34},{3,35},{4,36},{5,37},{6,38},{7,39},{8,104},{9... | collective-permute-start | bytes 442376 | tf_op jit(solution)/shard_map/ppermute | solution.py:364
  137.7 1.4 collective-permute-start.23
  139.2 2.8 %collective-permute-done.22.refs_10_ = bf16[24,1792]{1,0:T(8,128)(2,1)S(1)} collective-permute-done((bf16[24,1792]{1,0:T(8,128)(2,1)S(1)}, bf16[24,1792]{1,0:T(8,128)(2,1)S(1)}, u32[]{:S(2)}, u32[]{:S(2)}) %collective-permute-start.22) | collective-permute-done | bytes 86048 | tf_op jit(solution)/shard_map/ppermute | solution.py:364
  141.9 0.8 collective-permute-done.23.refs_11_
  142.9 1.7 %collective-permute-start.24 = (bf16[3,12,4864]{2,1,0:T(8,128)(2,1)S(1)}, bf16[3,12,4864]{2,1,0:T(8,128)(2,1)S(1)}, u32[]{:S(2)}, u32[]{:S(2)}) collective-permute-start(bf16[3,12,4864]{2,1,0:T(8,128)(2,1)S(1)} %get-tuple-element.115), channel_id=1, source_target_pairs={{0,96},{1,97},{2,98},{3,99},{4,100},{5,101},{6,102},{7,103},{8,40}... | collective-permute-start | bytes 1050632 | tf_op jit(solution)/shard_map/ppermute | solution.py:364
  144.6 8.2 %collective-permute-done.24.got = bf16[3,12,4864]{2,1,0:T(8,128)(2,1)S(1)} collective-permute-done((bf16[3,12,4864]{2,1,0:T(8,128)(2,1)S(1)}, bf16[3,12,4864]{2,1,0:T(8,128)(2,1)S(1)}, u32[]{:S(2)}, u32[]{:S(2)}) %collective-permute-start.24) | collective-permute-done | bytes 350240 | tf_op jit(solution)/shard_map/ppermute | solution.py:364
  152.9 2.4 %collective-permute-start.25 = (bf16[3,6,4864]{2,1,0:T(8,128)(2,1)S(1)}, bf16[3,6,4864]{2,1,0:T(8,128)(2,1)S(1)}, u32[]{:S(2)}, u32[]{:S(2)}) collective-permute-start(bf16[3,6,4864]{2,1,0:T(8,128)(2,1)S(1)} %get-tuple-element.117), channel_id=1, source_target_pairs={{0,20},{1,21},{2,22},{3,23},{4,16},{5,17},{6,18},{7,19},{8,12},{9,... | collective-permute-start | bytes 525320 | tf_op jit(solution)/shard_map/ppermute | solution.py:364
  155.4 2.6 %shard_map.129 = bf16[256,1152]{1,0:T(8,128)(2,1)} custom-call(bf16[256,1728]{1,0:T(8,128)(2,1)} %get-tuple-element.65.both, bf16[256,1728]{1,0:T(8,128)(2,1)S(1)} %bitcast.18, f32[6,1152]{1,0:T(8,128)S(1)} %copy-done.13, bf16[576,1152]{1,0:T(8,128)(2,1)S(1)} %copy-done.6), custom_call_target="tpu_custom_call" | custom-call | flops 339738624 | bytes 3714048 | tf_op jit(solution)/shard_map/pallas_call | solution.py:34
  158.0 2.3 %collective-permute-done.25.got = bf16[3,6,4864]{2,1,0:T(8,128)(2,1)S(1)} collective-permute-done((bf16[3,6,4864]{2,1,0:T(8,128)(2,1)S(1)}, bf16[3,6,4864]{2,1,0:T(8,128)(2,1)S(1)}, u32[]{:S(2)}, u32[]{:S(2)}) %collective-permute-start.25) | collective-permute-done | bytes 175136 | tf_op jit(solution)/shard_map/ppermute | solution.py:364
  160.4 1.1 collective-permute-start.26
  161.5 4.8 %shard_map.132 = bf16[256,1152]{1,0:T(8,128)(2,1)} custom-call(bf16[256,1152]{1,0:T(8,128)(2,1)S(1)} %copy-done.20, bf16[256,1728]{1,0:T(8,128)(2,1)S(1)} %copy-done.4, bf16[256,1152]{1,0:T(8,128)(2,1)S(1)} %bitcast.20, f32[6,1152]{1,0:T(8,128)S(1)} %copy-done.13, bf16[1152,1728]{1,0:T(8,128)(2,1)} %copy.28.w_qkv), custom_call_target="tpu_custom_call" | custom-call | flops 1019215872 | bytes 6663168 | tf_op jit(solution)/shard_map/pallas_call | solution.py:34
  (109 shorter events, 10.4 us)
Async XLA Ops:
  2.2 68.3 %copy-start.12 = (f32[6,1152]{1,0:T(8,128)}, f32[6,1152]{1,0:T(8,128)S(1)}, u32[]{:S(2)}) copy-start(f32[6,1152]{1,0:T(8,128)S(1)} %reshape.41.mod) | copy-start | bytes 82948
  2.2 6.6 %copy-start.5 = (bf16[576,1152]{1,0:T(8,128)(2,1)S(1)}, bf16[576,1152]{1,0:T(8,128)(2,1)}, u32[]{:S(2)}) copy-start(bf16[576,1152]{1,0:T(8,128)(2,1)} %w_out.5) | copy-start | bytes 3981316
  2.2 6.6 %copy-start.7 = (bf16[1,1,256,1152]{3,2,1,0:T(8,128)(2,1)S(1)}, bf16[1,1,256,1152]{3,2,1,0:T(8,128)(2,1)}, u32[]{:S(2)}) copy-start(bf16[1,1,256,1152]{3,2,1,0:T(8,128)(2,1)} %param.8) | copy-start | bytes 1769476
  2.2 6.6 %copy-start.9 = (bf16[1,1,256,1152]{3,2,1,0:T(8,128)(2,1)S(1)}, bf16[1,1,256,1152]{3,2,1,0:T(8,128)(2,1)}, u32[]{:S(2)}) copy-start(bf16[1,1,256,1152]{3,2,1,0:T(8,128)(2,1)} %param.9) | copy-start | bytes 1769476
  18.2 0.8 copy-start.25
  19.0 0.8 copy-start.27
  20.5 19.8 %all-to-all-start = ((bf16[8,32,1728]{2,1,0:T(8,128)(2,1)}), bf16[8,32,1728]{2,1,0:T(8,128)(2,1)S(1)}, u32[]{:S(2)}, u32[]{:S(2)}) async-start(bf16[8,32,1728]{2,1,0:T(8,128)(2,1)} %bitcast.4), calls=%async_computation | async-start | bytes 1835008 | tf_op jit(solution)/shard_map/all_to_all | solution.py:415
  50.6 1.0 copy-start.14
  51.6 0.9 copy-start.17
  52.5 0.8 copy-start.35
  53.3 17.2 %all-to-all-start.1 = ((bf16[8,32,1728]{2,1,0:T(8,128)(2,1)}), bf16[8,32,1728]{2,1,0:T(8,128)(2,1)S(1)}, u32[]{:S(2)}, u32[]{:S(2)}) async-start(bf16[8,32,1728]{2,1,0:T(8,128)(2,1)} %bitcast.23), calls=%async_computation.1 | async-start | bytes 1835008 | tf_op jit(solution)/shard_map/all_to_all | solution.py:428
  57.1 1.1 copy-start.26
  58.1 1.1 copy-start.28
  62.6 23.4 %collective-permute-start = (bf16[256,1152]{1,0:T(8,128)(2,1)}, bf16[256,1152]{1,0:T(8,128)(2,1)}, u32[]{:S(2)}, u32[]{:S(2)}) collective-permute-start(bf16[256,1152]{1,0:T(8,128)(2,1)} %get-tuple-element.74), channel_id=1, source_target_pairs={{0,8},{1,9},{2,10},{3,11},{4,12},{5,13},{6,14},{7,15},{8,0},{9,1},... | collective-permute-start | bytes 1769480 | tf_op jit(solution)/shard_map/ppermute | solution.py:355
  70.6 16.7 %copy-start.1 = (bf16[8,32,1728]{2,1,0:T(8,128)(2,1)}, bf16[8,32,1728]{2,1,0:T(8,128)(2,1)S(1)}, u32[]{:S(2)}) copy-start(bf16[8,32,1728]{2,1,0:T(8,128)(2,1)S(1)} %all-to-all-done.1) | copy-start | bytes 2654212
  70.6 6.4 %copy-start.10 = (f32[8,256,256]{2,1,0:T(8,128)S(1)}, f32[8,256,256]{2,1,0:T(8,128)}, u32[]{:S(2)}) copy-start(f32[8,256,256]{2,1,0:T(8,128)} %get-tuple-element.70.probs_t) | copy-start | bytes 6291460
  74.6 0.8 copy-start.19
  76.1 0.8 copy-start.24
  77.0 1.5 copy-start.11
  78.5 5.7 %copy-start.15 = (bf16[256,1728]{1,0:T(8,128)(2,1)S(1)}, bf16[256,1728]{1,0:T(8,128)(2,1)}, u32[]{:S(2)}) copy-start(bf16[256,1728]{1,0:T(8,128)(2,1)} %copy-done.14) | copy-start | bytes 2654212
  81.3 10.1 %copy-start.3 = (bf16[256,1728]{1,0:T(8,128)(2,1)}, bf16[256,1728]{1,0:T(8,128)(2,1)S(1)}, u32[]{:S(2)}) copy-start(bf16[256,1728]{1,0:T(8,128)(2,1)S(1)} %shard_map.131.qkv_grad.refs_2_) | copy-start | bytes 2654212
  82.7 6.6 %collective-permute-start.1 = (bf16[256,1728]{0,1:T(8,128)(2,1)}, bf16[256,1728]{0,1:T(8,128)(2,1)}, u32[]{:S(2)}, u32[]{:S(2)}) collective-permute-start(bf16[256,1728]{0,1:T(8,128)(2,1)} %copy.32), channel_id=1, source_target_pairs={{0,8},{1,9},{2,10},{3,11},{4,12},{5,13},{6,14},{7,15},{8,0},{9,1},... | collective-permute-start | bytes 2654216 | tf_op jit(solution)/shard_map/ppermute | solution.py:355
  82.7 5.3 %collective-permute-start.2 = (bf16[256,1152]{1,0:T(8,128)(2,1)}, bf16[256,1152]{1,0:T(8,128)(2,1)}, u32[]{:S(2)}, u32[]{:S(2)}) collective-permute-start(bf16[256,1152]{1,0:T(8,128)(2,1)} %copy-done.24), channel_id=1, source_target_pairs={{0,8},{1,9},{2,10},{3,11},{4,12},{5,13},{6,14},{7,15},{8,0},{9,1},... | collective-permute-start | bytes 1769480 | tf_op jit(solution)/shard_map/ppermute | solution.py:355
  83.2 8.3 %collective-permute-start.3 = (bf16[256,576]{1,0:T(8,128)(2,1)}, bf16[256,576]{1,0:T(8,128)(2,1)}, u32[]{:S(2)}, u32[]{:S(2)}) collective-permute-start(bf16[256,576]{1,0:T(8,128)(2,1)} %copy-done.29), channel_id=1, source_target_pairs={{0,8},{1,9},{2,10},{3,11},{4,12},{5,13},{6,14},{7,15},{8,0},{9,1},... | collective-permute-start | bytes 884744 | tf_op jit(solution)/shard_map/ppermute | solution.py:355
  84.1 7.3 %copy-start.21 = (bf16[256,576]{1,0:T(8,128)(2,1)S(1)}, bf16[256,576]{1,0:T(8,128)(2,1)}, u32[]{:S(2)}) copy-start(bf16[256,576]{1,0:T(8,128)(2,1)} %get-tuple-element.128.refs_8_) | copy-start | bytes 884740
  84.1 7.3 %copy-start.22 = (bf16[256,576]{1,0:T(8,128)(2,1)S(1)}, bf16[256,576]{1,0:T(8,128)(2,1)}, u32[]{:S(2)}) copy-start(bf16[256,576]{1,0:T(8,128)(2,1)} %get-tuple-element.129.refs_0_) | copy-start | bytes 884740
  85.5 23.2 %collective-permute-start.14 = (bf16[256,1728]{0,1:T(8,128)(2,1)}, bf16[256,1728]{0,1:T(8,128)(2,1)}, u32[]{:S(2)}, u32[]{:S(2)}) collective-permute-start(bf16[256,1728]{0,1:T(8,128)(2,1)} %copy.34), channel_id=1, source_target_pairs={{0,8},{1,9},{2,10},{3,11},{4,12},{5,13},{6,14},{7,15},{8,0},{9,1},... | collective-permute-start | bytes 2654216 | tf_op jit(solution)/shard_map/ppermute | solution.py:355
  91.5 1.0 copy-start.23
  92.5 1.0 copy-start.30
  93.4 1.0 copy-start.32
  100.1 17.2 %collective-permute-start.4 = (bf16[96,3072]{1,0:T(8,128)(2,1)}, bf16[96,3072]{1,0:T(8,128)(2,1)}, u32[]{:S(2)}, u32[]{:S(2)}) collective-permute-start(bf16[96,3072]{1,0:T(8,128)(2,1)} %get-tuple-element.79), channel_id=1, source_target_pairs={{0,32},{1,33},{2,34},{3,35},{4,36},{5,37},{6,38},{7,39},{8,104},{9... | collective-permute-start | bytes 1769480 | tf_op jit(solution)/shard_map/ppermute | solution.py:364
  101.6 1.1 copy-start.36
  102.7 15.8 %copy-start = (f32[3,96,3072]{2,1,0:T(8,128)S(1)}, f32[3,96,3072]{2,1,0:T(8,128)}, u32[]{:S(2)}) copy-start(f32[3,96,3072]{2,1,0:T(8,128)} %get-tuple-element.78.keep) | copy-start | bytes 10616836
  104.6 0.7 copy-start.33
  105.4 5.6 %collective-permute-start.13 = (bf16[256,576]{1,0:T(8,128)(2,1)}, bf16[256,576]{1,0:T(8,128)(2,1)}, u32[]{:S(2)}, u32[]{:S(2)}) collective-permute-start(bf16[256,576]{1,0:T(8,128)(2,1)} %get-tuple-element.96), channel_id=1, source_target_pairs={{0,8},{1,9},{2,10},{3,11},{4,12},{5,13},{6,14},{7,15},{8,0},{9,1},... | collective-permute-start | bytes 884744 | tf_op jit(solution)/shard_map/ppermute | solution.py:355
  106.4 13.3 %collective-permute-start.6 = (bf16[96,3072]{1,0:T(8,128)(2,1)}, bf16[96,3072]{1,0:T(8,128)(2,1)}, u32[]{:S(2)}, u32[]{:S(2)}) collective-permute-start(bf16[96,3072]{1,0:T(8,128)(2,1)} %get-tuple-element.83), channel_id=1, source_target_pairs={{0,4},{1,5},{2,6},{3,7},{4,0},{5,1},{6,2},{7,3},{8,28},{9,29},{10,... | collective-permute-start | bytes 1769480 | tf_op jit(solution)/shard_map/ppermute | solution.py:364
  107.8 14.6 %collective-permute-start.8 = (bf16[96,3072]{1,0:T(8,128)(2,1)}, bf16[96,3072]{1,0:T(8,128)(2,1)}, u32[]{:S(2)}, u32[]{:S(2)}) collective-permute-start(bf16[96,3072]{1,0:T(8,128)(2,1)} %get-tuple-element.87), channel_id=1, source_target_pairs={{0,1},{1,0},{2,3},{3,2},{4,5},{5,4},{6,7},{7,6},{8,11},{9,10},{10,... | collective-permute-start | bytes 1769480 | tf_op jit(solution)/shard_map/ppermute | solution.py:364
  110.9 1.2 copy-start.16
  112.1 1.2 copy-start.18
  113.3 1.0 copy-start.34
  116.5 8.0 %collective-permute-start.15 = (bf16[96,1792]{1,0:T(8,128)(2,1)S(1)}, bf16[96,1792]{1,0:T(8,128)(2,1)S(1)}, u32[]{:S(2)}, u32[]{:S(2)}) collective-permute-start(bf16[96,1792]{1,0:T(8,128)(2,1)S(1)} %get-tuple-element.99), channel_id=1, source_target_pairs={{0,32},{1,33},{2,34},{3,35},{4,36},{5,37},{6,38},{7,39},{8,104},{9... | collective-permute-start | bytes 1032200 | tf_op jit(solution)/shard_map/ppermute | solution.py:364
  116.8 9.7 %collective-permute-start.17 = (bf16[96,1792]{1,0:T(8,128)(2,1)S(1)}, bf16[96,1792]{1,0:T(8,128)(2,1)S(1)}, u32[]{:S(2)}, u32[]{:S(2)}) collective-permute-start(bf16[96,1792]{1,0:T(8,128)(2,1)S(1)} %get-tuple-element.103), channel_id=1, source_target_pairs={{0,4},{1,5},{2,6},{3,7},{4,0},{5,1},{6,2},{7,3},{8,28},{9,29},{10,... | collective-permute-start | bytes 1032200 | tf_op jit(solution)/shard_map/ppermute | solution.py:364
  117.4 9.9 %collective-permute-start.19 = (bf16[96,1792]{1,0:T(8,128)(2,1)S(1)}, bf16[96,1792]{1,0:T(8,128)(2,1)S(1)}, u32[]{:S(2)}, u32[]{:S(2)}) collective-permute-start(bf16[96,1792]{1,0:T(8,128)(2,1)S(1)} %get-tuple-element.107), channel_id=1, source_target_pairs={{0,1},{1,0},{2,3},{3,2},{4,5},{5,4},{6,7},{7,6},{8,11},{9,10},{10,... | collective-permute-start | bytes 1032200 | tf_op jit(solution)/shard_map/ppermute | solution.py:364
  119.7 12.6 %collective-permute-start.5 = (bf16[48,3072]{1,0:T(8,128)(2,1)S(1)}, bf16[48,3072]{1,0:T(8,128)(2,1)S(1)}, u32[]{:S(2)}, u32[]{:S(2)}) collective-permute-start(bf16[48,3072]{1,0:T(8,128)(2,1)S(1)} %get-tuple-element.81), channel_id=1, source_target_pairs={{0,4},{1,5},{2,6},{3,7},{4,0},{5,1},{6,2},{7,3},{8,28},{9,29},{10,... | collective-permute-start | bytes 884744 | tf_op jit(solution)/shard_map/ppermute | solution.py:364
  122.4 11.2 %collective-permute-start.7 = (bf16[48,3072]{1,0:T(8,128)(2,1)S(1)}, bf16[48,3072]{1,0:T(8,128)(2,1)S(1)}, u32[]{:S(2)}, u32[]{:S(2)}) collective-permute-start(bf16[48,3072]{1,0:T(8,128)(2,1)S(1)} %get-tuple-element.85), channel_id=1, source_target_pairs={{0,1},{1,0},{2,3},{3,2},{4,5},{5,4},{6,7},{7,6},{8,11},{9,10},{10,... | collective-permute-start | bytes 884744 | tf_op jit(solution)/shard_map/ppermute | solution.py:364
  124.6 10.0 %collective-permute-start.9 = (bf16[48,3072]{1,0:T(8,128)(2,1)S(1)}, bf16[48,3072]{1,0:T(8,128)(2,1)S(1)}, u32[]{:S(2)}, u32[]{:S(2)}) collective-permute-start(bf16[48,3072]{1,0:T(8,128)(2,1)S(1)} %get-tuple-element.89), channel_id=1, source_target_pairs={{0,32},{1,33},{2,34},{3,35},{4,36},{5,37},{6,38},{7,39},{8,104},{9... | collective-permute-start | bytes 884744 | tf_op jit(solution)/shard_map/ppermute | solution.py:364
  126.5 5.5 %collective-permute-start.16 = (bf16[48,1792]{1,0:T(8,128)(2,1)S(1)}, bf16[48,1792]{1,0:T(8,128)(2,1)S(1)}, u32[]{:S(2)}, u32[]{:S(2)}) collective-permute-start(bf16[48,1792]{1,0:T(8,128)(2,1)S(1)} %get-tuple-element.101), channel_id=1, source_target_pairs={{0,4},{1,5},{2,6},{3,7},{4,0},{5,1},{6,2},{7,3},{8,28},{9,29},{10,... | collective-permute-start | bytes 516104 | tf_op jit(solution)/shard_map/ppermute | solution.py:364
  127.3 9.3 %collective-permute-start.18 = (bf16[48,1792]{1,0:T(8,128)(2,1)S(1)}, bf16[48,1792]{1,0:T(8,128)(2,1)S(1)}, u32[]{:S(2)}, u32[]{:S(2)}) collective-permute-start(bf16[48,1792]{1,0:T(8,128)(2,1)S(1)} %get-tuple-element.105), channel_id=1, source_target_pairs={{0,1},{1,0},{2,3},{3,2},{4,5},{5,4},{6,7},{7,6},{8,11},{9,10},{10,... | collective-permute-start | bytes 516104 | tf_op jit(solution)/shard_map/ppermute | solution.py:364
  132.0 5.4 %collective-permute-start.20 = (bf16[48,1792]{1,0:T(8,128)(2,1)S(1)}, bf16[48,1792]{1,0:T(8,128)(2,1)S(1)}, u32[]{:S(2)}, u32[]{:S(2)}) collective-permute-start(bf16[48,1792]{1,0:T(8,128)(2,1)S(1)} %get-tuple-element.109), channel_id=1, source_target_pairs={{0,32},{1,33},{2,34},{3,35},{4,36},{5,37},{6,38},{7,39},{8,104},{9... | collective-permute-start | bytes 516104 | tf_op jit(solution)/shard_map/ppermute | solution.py:364
  132.3 5.4 %collective-permute-start.21 = (bf16[24,1792]{1,0:T(8,128)(2,1)S(1)}, bf16[24,1792]{1,0:T(8,128)(2,1)S(1)}, u32[]{:S(2)}, u32[]{:S(2)}) collective-permute-start(bf16[24,1792]{1,0:T(8,128)(2,1)S(1)} %get-tuple-element.111), channel_id=1, source_target_pairs={{0,1},{1,0},{2,3},{3,2},{4,5},{5,4},{6,7},{7,6},{8,11},{9,10},{10,... | collective-permute-start | bytes 258056 | tf_op jit(solution)/shard_map/ppermute | solution.py:364
  133.5 21.8 %copy-start.2 = (bf16[8,32,1728]{2,1,0:T(8,128)(2,1)S(1)}, bf16[8,32,1728]{2,1,0:T(8,128)(2,1)}, u32[]{:S(2)}) copy-start(bf16[8,32,1728]{2,1,0:T(8,128)(2,1)} %copy-done.1) | copy-start | bytes 2654212
  133.5 21.8 %copy-start.6 = (bf16[576,1152]{1,0:T(8,128)(2,1)S(1)}, bf16[576,1152]{1,0:T(8,128)(2,1)}, u32[]{:S(2)}) copy-start(bf16[576,1152]{1,0:T(8,128)(2,1)} %w_out.4) | copy-start | bytes 3981316
  133.5 21.8 %copy-start.13 = (f32[6,1152]{1,0:T(8,128)S(1)}, f32[6,1152]{1,0:T(8,128)}, u32[]{:S(2)}) copy-start(f32[6,1152]{1,0:T(8,128)} %copy-done.12) | copy-start | bytes 82948
  133.6 9.1 %collective-permute-start.10 = (bf16[24,3072]{1,0:T(8,128)(2,1)S(1)}, bf16[24,3072]{1,0:T(8,128)(2,1)S(1)}, u32[]{:S(2)}, u32[]{:S(2)}) collective-permute-start(bf16[24,3072]{1,0:T(8,128)(2,1)S(1)} %get-tuple-element.91), channel_id=1, source_target_pairs={{0,1},{1,0},{2,3},{3,2},{4,5},{5,4},{6,7},{7,6},{8,11},{9,10},{10,... | collective-permute-start | bytes 442376 | tf_op jit(solution)/shard_map/ppermute | solution.py:364
  134.6 8.1 %collective-permute-start.11 = (bf16[24,3072]{1,0:T(8,128)(2,1)S(1)}, bf16[24,3072]{1,0:T(8,128)(2,1)S(1)}, u32[]{:S(2)}, u32[]{:S(2)}) collective-permute-start(bf16[24,3072]{1,0:T(8,128)(2,1)S(1)} %get-tuple-element.92), channel_id=1, source_target_pairs={{0,32},{1,33},{2,34},{3,35},{4,36},{5,37},{6,38},{7,39},{8,104},{9... | collective-permute-start | bytes 442376 | tf_op jit(solution)/shard_map/ppermute | solution.py:364
  136.6 6.2 %collective-permute-start.12 = (bf16[24,3072]{1,0:T(8,128)(2,1)S(1)}, bf16[24,3072]{1,0:T(8,128)(2,1)S(1)}, u32[]{:S(2)}, u32[]{:S(2)}) collective-permute-start(bf16[24,3072]{1,0:T(8,128)(2,1)S(1)} %get-tuple-element.93), channel_id=1, source_target_pairs={{0,4},{1,5},{2,6},{3,7},{4,0},{5,1},{6,2},{7,3},{8,28},{9,29},{10,... | collective-permute-start | bytes 442376 | tf_op jit(solution)/shard_map/ppermute | solution.py:364
  137.4 4.5 %collective-permute-start.22 = (bf16[24,1792]{1,0:T(8,128)(2,1)S(1)}, bf16[24,1792]{1,0:T(8,128)(2,1)S(1)}, u32[]{:S(2)}, u32[]{:S(2)}) collective-permute-start(bf16[24,1792]{1,0:T(8,128)(2,1)S(1)} %get-tuple-element.112), channel_id=1, source_target_pairs={{0,32},{1,33},{2,34},{3,35},{4,36},{5,37},{6,38},{7,39},{8,104},{9... | collective-permute-start | bytes 258056 | tf_op jit(solution)/shard_map/ppermute | solution.py:364
  137.7 5.0 %collective-permute-start.23 = (bf16[24,1792]{1,0:T(8,128)(2,1)S(1)}, bf16[24,1792]{1,0:T(8,128)(2,1)S(1)}, u32[]{:S(2)}, u32[]{:S(2)}) collective-permute-start(bf16[24,1792]{1,0:T(8,128)(2,1)S(1)} %get-tuple-element.113), channel_id=1, source_target_pairs={{0,4},{1,5},{2,6},{3,7},{4,0},{5,1},{6,2},{7,3},{8,28},{9,29},{10,... | collective-permute-start | bytes 258056 | tf_op jit(solution)/shard_map/ppermute | solution.py:364
  142.7 18.8 %copy-start.4 = (bf16[256,1728]{1,0:T(8,128)(2,1)S(1)}, bf16[256,1728]{1,0:T(8,128)(2,1)}, u32[]{:S(2)}) copy-start(bf16[256,1728]{1,0:T(8,128)(2,1)} %copy-done.3) | copy-start | bytes 2654212
  142.7 18.8 %copy-start.8 = (bf16[1,1,256,1152]{3,2,1,0:T(8,128)(2,1)S(1)}, bf16[1,1,256,1152]{3,2,1,0:T(8,128)(2,1)}, u32[]{:S(2)}) copy-start(bf16[1,1,256,1152]{3,2,1,0:T(8,128)(2,1)} %param.8) | copy-start | bytes 1769476
  142.7 18.8 %copy-start.20 = (bf16[256,1152]{1,0:T(8,128)(2,1)S(1)}, bf16[256,1152]{1,0:T(8,128)(2,1)}, u32[]{:S(2)}) copy-start(bf16[256,1152]{1,0:T(8,128)(2,1)} %copy-done.19) | copy-start | bytes 1769476
  142.9 9.9 %collective-permute-start.24 = (bf16[3,12,4864]{2,1,0:T(8,128)(2,1)S(1)}, bf16[3,12,4864]{2,1,0:T(8,128)(2,1)S(1)}, u32[]{:S(2)}, u32[]{:S(2)}) collective-permute-start(bf16[3,12,4864]{2,1,0:T(8,128)(2,1)S(1)} %get-tuple-element.115), channel_id=1, source_target_pairs={{0,96},{1,97},{2,98},{3,99},{4,100},{5,101},{6,102},{7,103},{8,40}... | collective-permute-start | bytes 1050632 | tf_op jit(solution)/shard_map/ppermute | solution.py:364
  152.9 7.4 %collective-permute-start.25 = (bf16[3,6,4864]{2,1,0:T(8,128)(2,1)S(1)}, bf16[3,6,4864]{2,1,0:T(8,128)(2,1)S(1)}, u32[]{:S(2)}, u32[]{:S(2)}) collective-permute-start(bf16[3,6,4864]{2,1,0:T(8,128)(2,1)S(1)} %get-tuple-element.117), channel_id=1, source_target_pairs={{0,20},{1,21},{2,22},{3,23},{4,16},{5,17},{6,18},{7,19},{8,12},{9,... | collective-permute-start | bytes 525320 | tf_op jit(solution)/shard_map/ppermute | solution.py:364
  160.4 6.1 %collective-permute-start.26 = (bf16[3,3,4864]{2,1,0:T(4,128)(2,1)S(1)}, bf16[3,3,4864]{2,1,0:T(4,128)(2,1)S(1)}, u32[]{:S(2)}, u32[]{:S(2)}) collective-permute-start(bf16[3,3,4864]{2,1,0:T(4,128)(2,1)S(1)} %get-tuple-element.119), channel_id=1, source_target_pairs={{0,3},{1,2},{2,1},{3,0},{4,7},{5,6},{6,5},{7,4},{8,9},{9,8},{10,11... | collective-permute-start | bytes 262664 | tf_op jit(solution)/shard_map/ppermute | solution.py:364
  (2 other events, 1.4 us)

commit v2 on v1

v2 whole, which is shorter than its diff:
```python
import jax
import jax.numpy as jnp
from jax import lax
from jax.experimental import pallas as pl
from jax.experimental.pallas import tpu as pltpu
from jax.sharding import PartitionSpec as P

T = 256
D = 1152
HEADS = 8
HEAD_DIM = 72
A = HEADS * HEAD_DIM
Q = 3 * A
A_PAD = 640
Q_PAD = 1792
LOCAL = 32
EPS = 1e-06
BF = jnp.bfloat16
F32 = jnp.float32
MESH = ("dp", "seq")
MIB = 1024 * 1024


def dot(left, right, over_left, over_right):
    return lax.dot_general(
        left, right, (((over_left,), (over_right,)), ((), ())), preferred_element_type=F32
    )


def call(body, outs, args, flops, scratch=(), limit=24, apart=()):
    shapes = tuple(jax.ShapeDtypeStruct(shape, kind) for shape, kind in outs)
    size = sum(x.size * x.dtype.itemsize for x in args)
    size += sum(x.size * x.dtype.itemsize for x in shapes)
    spaces = [pltpu.HBM if k in apart else pltpu.VMEM for k in range(len(args))]
    return pl.pallas_call(
        body,
        out_shape=shapes,
        in_specs=[pl.BlockSpec(memory_space=space) for space in spaces],
        out_specs=tuple(pl.BlockSpec(memory_space=pltpu.VMEM) for _ in shapes),
        scratch_shapes=list(scratch),
        cost_estimate=pl.CostEstimate(flops=flops, bytes_accessed=size, transcendentals=0),
        compiler_params=pltpu.CompilerParams(vmem_limit_bytes=limit * MIB),
    )(*args)


def in_order(*values):
    return lax.optimization_barrier(values)


def normalized(x32):
    mean = jnp.mean(x32, axis=-1, keepdims=True)
    centered = x32 - mean
    spread = lax.rsqrt(jnp.mean(centered * centered, axis=-1, keepdims=True) + EPS)
    return centered * spread, spread


def normalized_back(unit, spread, scale, grad):
    grad = grad * (1.0 + scale)
    inner = jnp.mean(grad * unit, axis=-1, keepdims=True)
    return spread * (grad - jnp.mean(grad, axis=-1, keepdims=True) - unit * inner)


def flip(source, target, blocks):
    for b in range(blocks):
        target[128 * b : 128 * b + 128, :] = source[:, 128 * b : 128 * b + 128].T


def flip_back(source, target, blocks):
    for b in range(blocks):
        target[:, 128 * b : 128 * b + 128] = source[128 * b : 128 * b + 128, :].T


def gain_columns(gains, block):
    row = lax.broadcasted_iota(jnp.int32, (HEAD_DIM, HEAD_DIM), 0)
    column = lax.broadcasted_iota(jnp.int32, (HEAD_DIM, HEAD_DIM), 1)
    return tuple(
        jnp.sum(jnp.where(row == column, gains[block, k : k + 1, :], 0.0), axis=1, keepdims=True)
        for k in range(2)
    )


def head_rows(which, h):
    start = which * A + h * HEAD_DIM
    return slice(start, start + HEAD_DIM)


def head_norm(rows, gain):
    root = lax.rsqrt(jnp.mean(rows * rows, axis=0, keepdims=True) + EPS)
    return root, (rows * root * gain).astype(BF)


def head_norm_back(rows, root, gain, grad):
    grad = grad.astype(BF).astype(F32) * gain
    inner = jnp.mean(rows * grad, axis=0, keepdims=True)
    return (root * grad - rows * (root * root * root * inner)).astype(BF).astype(F32)


def same_patch():
    key = lax.broadcasted_iota(jnp.int32, (T, T), 0)
    query = lax.broadcasted_iota(jnp.int32, (T, T), 1)
    return ((key ^ query) & (LOCAL - 1)) == 0


def head_probs(queries, keys, mask):
    scores = dot(keys, queries, 0, 0) * HEAD_DIM ** (-0.5)
    if mask is not None:
        scores = jnp.where(mask, scores, -1e30)
    expo = jnp.exp(scores - jnp.max(scores, axis=0, keepdims=True))
    return expo * (1.0 / jnp.sum(expo, axis=0, keepdims=True))


def head_back(q_rows, k_rows, v_rows, gains, probs, grad):
    q_root, queries = head_norm(q_rows, gains[0])
    k_root, keys = head_norm(k_rows, gains[1])
    grad = grad.astype(BF)
    probs16 = probs.astype(BF)
    v_grad = dot(grad, probs16, 1, 1).astype(BF).astype(F32)
    p_grad = dot(v_rows.astype(BF), grad, 0, 0).astype(BF).astype(F32)
    inner = jnp.sum(p_grad * probs, axis=0, keepdims=True)
    s_grad = (probs * (p_grad - inner) * HEAD_DIM ** (-0.5)).astype(BF)
    q_grad = head_norm_back(q_rows, q_root, gains[0], dot(keys, s_grad, 1, 0))
    k_grad = head_norm_back(k_rows, k_root, gains[1], dot(queries, s_grad, 1, 1))
    return q_grad, k_grad, v_grad


def order(core, chip):
    row = lax.broadcasted_iota(jnp.int32, (1, A_PAD), 1)
    part = (row >= 192).astype(jnp.int32) + (row >= 384).astype(jnp.int32)
    rest = row - 192 * part
    first = (rest * 171) >> 12
    rest = rest - 24 * first
    second = (rest * 11) >> 5
    piece = 3 * part + rest - 3 * second
    place = []
    for axis in range(3):
        step = axis - part
        step = jnp.where(step < 0, step + 3, step)
        one = jnp.where(step == 0, first >> 2, jnp.where(step == 1, first >> 1, first)) & 1
        two = (second >> (2 - axis)) & 1
        near = jnp.where(core == 0, one, two) ^ ((chip[axis] ^ (chip[axis] >> 1)) & 1)
        far = jnp.where(core == 0, two, one) ^ (chip[axis] >> 1)
        place.append(2 * far + (near ^ far))
    x, y, z = place
    device = x * 32 + (y >> 1) * 16 + core * 8 + (y & 1) * 4 + z
    return jnp.where(row < A, 9 * device + piece, -1)


def position():
    dp, seq = lax.axis_index("dp"), lax.axis_index("seq")
    return dp & 1, (dp >> 2, ((dp >> 1) & 1) * 2 + (seq >> 2), seq & 3)


def picker(core, chip):
    feature = lax.broadcasted_iota(jnp.int32, (D, A_PAD), 0)
    return (feature == order(core, chip)).astype(F32).astype(BF)


def pickers():
    core, chip = position()
    return picker(core, chip), picker(1 - core, chip)


def forward_spatial(
    latents, cot, mod, gains, w_qkv_any, w_out_any, w_out_t_any,
    both, qkv_t, probs_t, normed, att, scaled_t, flat, tall, w_qkv, w_out, w_out_t, sems
):
    loads = [
        pltpu.make_async_copy(source, target, sems.at[k])
        for k, (source, target) in enumerate(
            ((w_qkv_any, w_qkv), (w_out_t_any, w_out_t), (w_out_any, w_out))
        )
    ]
    for load in loads:
        load.start()
    unit, _ = normalized(latents[...].astype(F32))
    norm = (unit * (1.0 + mod[1, 0:1, :]) + mod[0, 0:1, :]).astype(BF)
    normed[...] = norm
    scaled = (mod[2, 1:2, :] * cot[...].astype(F32)).astype(BF)
    scaled_t[...] = scaled
    loads[0].wait()
    qkv_t[...] = dot(w_qkv[...], norm, 1, 1).astype(BF).astype(F32)
    tall[A:, :] = jnp.zeros((A_PAD - A, T), F32)
    pair = gain_columns(gains, 0)
    for h in range(HEADS):
        queries = head_norm(qkv_t[head_rows(0, h), :], pair[0])[1]
        keys = head_norm(qkv_t[head_rows(1, h), :], pair[1])[1]
        probs = head_probs(queries, keys, None)
        probs_t[h] = probs
        values = qkv_t[head_rows(2, h), :].astype(BF)
        tall[head_rows(0, h), :] = dot(values, probs.astype(BF), 1, 0)
    flip_back(tall, flat, A_PAD // 128)
    att[...] = flat[...].astype(BF)
    loads[1].wait()
    both[:, D:] = dot(scaled, w_out_t[...], 1, 1).astype(BF)
    loads[2].wait()
    result = dot(att[:, :A], w_out[...], 1, 0)
    both[:, :D] = (latents[...].astype(F32) + mod[2, 0:1, :] * result).astype(BF)


def temporal(
    both, mod, gains, w_qkv, back, normed, qkv_grad, tall_qkv, tall_grad, wide, flat, tall, tall_att
):
    unit, _ = normalized(both[:, :D].astype(F32))
    norm = (unit * (1.0 + mod[1, 1:2, :]) + mod[0, 1:2, :]).astype(BF)
    normed[...] = norm
    tall_qkv[...] = dot(w_qkv[...], norm, 1, 1).astype(BF).astype(F32)
    flat[:, A:] = jnp.zeros((T, A_PAD - A), F32)
    flat[:, :A] = both[:, D:].astype(F32)
    flip(flat, tall, A_PAD // 128)
    tall_att[A:, :] = jnp.zeros((A_PAD - A, T), F32)
    tall_grad[Q:, :] = jnp.zeros((Q_PAD - Q, T), F32)
    mask = same_patch()
    pair = gain_columns(gains, 1)
    for h in range(HEADS):
        q_rows = tall_qkv[head_rows(0, h), :]
        k_rows = tall_qkv[head_rows(1, h), :]
        v_rows = tall_qkv[head_rows(2, h), :]
        probs = head_probs(head_norm(q_rows, pair[0])[1], head_norm(k_rows, pair[1])[1], mask)
        tall_att[head_rows(0, h), :] = dot(v_rows.astype(BF), probs.astype(BF), 1, 0)
        grads = head_back(q_rows, k_rows, v_rows, pair, probs, tall[head_rows(0, h), :])
        for which in range(3):
            tall_grad[head_rows(which, h), :] = grads[which]
    flip_back(tall_att, flat, A_PAD // 128)
    back[:, D:] = flat[:, :A].astype(BF)
    flip_back(tall_grad, wide, Q_PAD // 128)
    qkv_grad[...] = wide[...].astype(BF)
    back[:, :D] = dot(qkv_grad[:, :Q], w_qkv[...], 1, 0).astype(BF)


def pick_early(normed, scaled, att, mine, theirs):
    own, other = pickers()
    for k, source in enumerate((normed, scaled)):
        columns = slice(k * A_PAD, k * A_PAD + A_PAD)
        theirs[:, columns] = dot(source[...], other, 1, 0).astype(BF)
        mine[:, columns] = dot(source[...], own, 1, 0).astype(BF)
    theirs[:, 2 * A_PAD :] = att[...]


def pick_temporal(source, mine, theirs):
    own, other = pickers()
    mine[...] = dot(source[...], own, 1, 0).astype(BF)
    theirs[...] = dot(source[...], other, 1, 0).astype(BF)


def enter_spatial_back(back, both, cot, mod, w_out, mid_grad, att_grad, mine, theirs):
    unit, spread = normalized(both[:, :D].astype(F32))
    grad = normalized_back(unit, spread, mod[1, 1:2, :], back[:, :D].astype(F32))
    total = (cot[...].astype(F32) + grad).astype(BF)
    mid_grad[...] = total
    scaled = (mod[2, 0:1, :] * total.astype(F32)).astype(BF)
    att_grad[:, A:] = jnp.zeros((T, A_PAD - A), F32)
    att_grad[:, :A] = dot(scaled, w_out[...], 1, 1).astype(BF).astype(F32)
    own, other = pickers()
    mine[...] = dot(scaled, own, 1, 0).astype(BF)
    theirs[:, :A_PAD] = dot(scaled, other, 1, 0).astype(BF)
    theirs[:, A_PAD + A :] = jnp.zeros((T, A_PAD - A), BF)
    theirs[:, A_PAD : A_PAD + A] = back[:, D:]


def spatial_attention_back(att_grad, qkv_t, probs_t, gains, qkv_grad, tall_grad, wide, tall):
    flip(att_grad, tall, A_PAD // 128)
    tall_grad[Q:, :] = jnp.zeros((Q_PAD - Q, T), F32)
    pair = gain_columns(gains, 0)
    for h in range(HEADS):
        grads = head_back(
            qkv_t[head_rows(0, h), :], qkv_t[head_rows(1, h), :], qkv_t[head_rows(2, h), :],
            pair, probs_t[h], tall[head_rows(0, h), :]
        )
        for which in range(3):
            tall_grad[head_rows(which, h), :] = grads[which]
    flip_back(tall_grad, wide, Q_PAD // 128)
    qkv_grad[...] = wide[...].astype(BF)


def leave_spatial_back(mid_grad, qkv_grad, latents, mod, w_qkv, latents_grad):
    norm_grad = dot(qkv_grad[:, :Q], w_qkv[...], 1, 0).astype(BF).astype(F32)
    unit, spread = normalized(latents[...].astype(F32))
    grad = normalized_back(unit, spread, mod[1, 0:1, :], norm_grad)
    latents_grad[...] = (mid_grad[...].astype(F32) + grad).astype(BF)


def project_output(both, back, mod, w_out, output):
    result = dot(back[:, D:], w_out[...], 1, 0)
    output[...] = (both[:, :D].astype(F32) + mod[2, 1:2, :] * result).astype(BF)


def weight_rows(groups):
    def body(*refs):
        keep, sends = refs[-4], refs[-3:]
        start = 0
        for left, left_in, right, right_in, width in groups:
            total = None
            for (l_ref, l_at), (r_ref, r_at) in ((left, right), (left_in, right_in)):
                more = dot(
                    refs[l_ref][:, l_at : l_at + A], refs[r_ref][:, r_at : r_at + width], 0, 0
                )
                total = more if total is None else total + more
            padded = -(-width // 128) * 128
            for p in range(3):
                rows = total[192 * p : 192 * p + 192]
                keep[p, :, start : start + width] = rows[:96]
                sends[p][:, start : start + width] = rows[96:].astype(BF)
                if padded > width:
                    gap = slice(start + width, start + padded)
                    keep[p, :, gap] = jnp.zeros((96, padded - width), F32)
                    sends[p][:, gap] = jnp.zeros((96, padded - width), BF)
            start += padded

    return body


def first_halve(p):
    def body(*refs):
        kept, send = refs[-2:]
        half = kept.shape[0]
        start = 0
        for keep, got in ((refs[0], refs[1]), (refs[2], refs[3])):
            width = got.shape[1]
            total = keep[p] + got[...].astype(F32)
            kept[:, start : start + width] = total[:half]
            send[:, start : start + width] = total[half:].astype(BF)
            start += width

    return body


def add_halve(keep, got, kept, send):
    half = kept.shape[0]
    total = keep[...] + got[...].astype(F32)
    kept[...] = total[:half]
    send[...] = total[half:].astype(BF)


def join_halve(*refs):
    kept, send = refs[-2:]
    for p in range(3):
        total = refs[p][...] + refs[3 + p][...].astype(F32)
        half = total.shape[0] // 2
        kept[p] = total[:half]
        send[p] = total[half:].astype(BF)


def tail_halve(keep, got, kept, send):
    half = kept.shape[1]
    for p in range(3):
        total = keep[p] + got[p].astype(F32)
        kept[p] = total[:half]
        send[p] = total[half:].astype(BF)


def last_add(keep, got, *outs):
    start = 0
    for out in outs:
        width = out.shape[1]
        for p in range(3):
            rows = keep[p, :, start : start + width] + got[p, :, start : start + width].astype(F32)
            out[3 * p : 3 * p + 3, :] = rows
        start += -(-width // 128) * 128


def pairs(change):
    found = []
    for device in range(128):
        dp, seq = divmod(device, 8)
        x, y, z, core = dp >> 2, ((dp >> 1) & 1) * 2 + (seq >> 2), seq & 3, dp & 1
        x, y, z, core = change(x, y, z, core)
        found.append((device, (x * 4 + (y >> 1) * 2 + core) * 8 + (y & 1) * 4 + z))
    return found


def to_other_core(value):
    return lax.ppermute(value, MESH, pairs(lambda x, y, z, c: (x, y, z, 1 - c)))


def along(value, axis, late):
    def change(x, y, z, core):
        place = [x, y, z]
        place[axis] ^= 1 if (core == 0) != late else 3
        return (*place, core)

    return lax.ppermute(value, MESH, pairs(change))


def weight_partials(groups, args):
    width = sum(-(-group[-1] // 128) * 128 for group in groups)
    outs = [((3, 96, width), F32)] + [((96, width), BF)] * 3
    keep, *sends = call(weight_rows(groups), outs, args, 2 * 512 * A * width)
    return keep, sends


def shards(
    latents, cotangent, modulation, qk_gains, spatial_qkv, spatial_out, temporal_qkv, temporal_out
):
    x, cot = latents.reshape(T, D), cotangent.reshape(T, D)
    mod = modulation[0].transpose(1, 0, 2)
    w_qkv_s, w_qkv_t = spatial_qkv.T, temporal_qkv.T
    wide, tall_grad = pltpu.VMEM((T, Q_PAD), F32), pltpu.VMEM((Q_PAD, T), F32)
    flat, tall = pltpu.VMEM((T, A_PAD), F32), pltpu.VMEM((A_PAD, T), F32)

    both, qkv_t, probs_t, normed_s, att_s, scaled_t = call(
        forward_spatial,
        [
            ((T, D + A), BF), ((Q, T), F32), ((HEADS, T, T), F32),
            ((T, D), BF), ((T, A_PAD), BF), ((T, D), BF),
        ],
        (x, cot, mod, qk_gains, w_qkv_s, spatial_out, temporal_out),
        2 * T * D * (Q + 2 * A),
        (
            flat, tall, pltpu.VMEM((Q, D), BF), pltpu.VMEM((A, D), BF), pltpu.VMEM((A, D), BF),
            pltpu.SemaphoreType.DMA((3,)),
        ),
        apart=(4, 5, 6),
    )
    patch = lax.all_to_all(both.reshape(8, LOCAL, D + A), "seq", 0, 0, tiled=True)
    early_mine, early_theirs = call(
        pick_early,
        [((T, 2 * A_PAD), BF), ((T, 3 * A_PAD), BF)],
        (normed_s, scaled_t, att_s),
        4 * T * D * D,
    )
    patch, early_mine, early_theirs = in_order(patch, early_mine, early_theirs)
    early_in = to_other_core(early_theirs)

    back_patch, normed_t, qkv_grad_t = call(
        temporal,
        [((T, D + A), BF), ((T, D), BF), ((T, Q_PAD), BF)],
        (patch.reshape(T, D + A), mod, qk_gains, w_qkv_t),
        4 * T * D * Q,
        (pltpu.VMEM((Q, T), F32), tall_grad, wide, flat, tall, tall),
    )
    back = lax.all_to_all(back_patch.reshape(8, LOCAL, D + A), "seq", 0, 0, tiled=True)
    back = back.reshape(T, D + A)
    qkv_grad_t_in = to_other_core(qkv_grad_t)
    t_mine, t_theirs = call(
        pick_temporal, [((T, A_PAD), BF), ((T, A_PAD), BF)], (normed_t,), 4 * T * D * A
    )
    t_in = to_other_core(t_theirs)
    back, t_in, qkv_grad_t_in = in_order(back, t_in, qkv_grad_t_in)

    mid_grad, att_grad_s, late_mine, late_theirs = call(
        enter_spatial_back,
        [((T, D), BF), ((T, A_PAD), F32), ((T, A_PAD), BF), ((T, 2 * A_PAD), BF)],
        (back, both, cot, mod, spatial_out),
        6 * T * D * A,
    )
    late_in = to_other_core(late_theirs)
    (qkv_grad_s,) = call(
        spatial_attention_back,
        [((T, Q_PAD), BF)],
        (att_grad_s, qkv_t, probs_t, qk_gains),
        2 * T * T * HEADS * 128 * 5,
        (tall_grad, wide, tall),
    )
    qkv_grad_s_in = to_other_core(qkv_grad_s)
    keep_a, sends_a = weight_partials(
        (
            ((0, 0), (1, 0), (2, 0), (3, 0), Q),
            ((4, A_PAD), (5, A_PAD), (6, D), (7, A_PAD), A),
            ((8, 0), (7, 0), (9, 0), (5, 2 * A_PAD), A),
        ),
        (
            t_mine, t_in, qkv_grad_t, qkv_grad_t_in, early_mine, early_in, back, late_in, late_mine,
            att_s,
        ),
    )
    got_a = [along(sends_a[p], p, False) for p in range(3)]
    keep_b, sends_b = weight_partials(
        (((0, 0), (1, 0), (2, 0), (3, 0), Q),),
        (early_mine, early_in, qkv_grad_s, qkv_grad_s_in),
    )
    keep_b, *sends_b, mid_grad, back = in_order(keep_b, *sends_b, mid_grad, back)
    got_b = [along(sends_b[p], p, False) for p in range(3)]
    (latents_grad,) = call(
        leave_spatial_back,
        [((T, D), BF)],
        (mid_grad, qkv_grad_s, x, mod, w_qkv_s),
        2 * T * D * Q,
    )
    (output,) = call(
        project_output, [((T, D), BF)], (both, back, mod, temporal_out), 2 * T * D * A
    )
    keep_b, latents_grad, output = in_order(keep_b, latents_grad, output)

    columns = 2 * Q_PAD + 2 * A_PAD
    kept, got = [], []
    for p in range(3):
        mine, send = call(
            first_halve(p),
            [((48, columns), F32), ((48, columns), BF)],
            (keep_a, got_a[p], keep_b, got_b[p]),
            96 * columns,
        )
        kept.append(mine)
        got.append(along(send, (p + 1) % 3, False))
    for p in range(3):
        kept[p], send = call(
            add_halve, [((24, columns), F32), ((24, columns), BF)], (kept[p], got[p]), 48 * columns
        )
        got[p] = along(send, (p + 2) % 3, False)
    kept, send = call(
        join_halve,
        [((3, 12, columns), F32), ((3, 12, columns), BF)],
        (*kept, *got),
        72 * columns,
    )
    got = along(send, 0, True)
    kept, send = call(
        tail_halve, [((3, 6, columns), F32), ((3, 6, columns), BF)], (kept, got), 36 * columns
    )
    got = along(send, 1, True)
    kept, send = call(
        tail_halve, [((3, 3, columns), F32), ((3, 3, columns), BF)], (kept, got), 18 * columns
    )
    got = along(send, 2, True)
    tq, to, so, sq = call(
        last_add,
        [((9, Q), F32), ((9, A), F32), ((9, A), F32), ((9, Q), F32)],
        (kept, got),
        9 * columns,
    )
    shape = (1, 1, T, D)
    return output.reshape(shape), latents_grad.reshape(shape), sq, so.T, tq, to.T


def solution(mesh):
    tokens = P("dp", "seq", None, None)
    rows, cols = P(("dp", "seq"), None), P(None, ("dp", "seq"))
    return jax.shard_map(
        shards,
        mesh=mesh,
        in_specs=(tokens, tokens, P("dp", None, None, None), P(), P(), P(), P(), P()),
        out_specs=(tokens, tokens, rows, cols, rows, cols),
        check_vma=False,
    )
```

time: 169 us -> 145 us (0.86)
  local copies, waits for them, and re-layouts: 45.2 us -> 18 us
  waiting for transfers between devices: 32.7 us -> 48.6 us
  Pallas kernels: 52.3 us -> 43.9 us
  starting transfers between devices: 36.1 us -> 32.6 us
    unnamed x79 -> x52, local copies, waits for them, and re-layouts: 33.2 us -> 18 us
    ppermute x21 -> x15, waiting for transfers between devices: 17.8 us -> 27.9 us  [along(): return lax.ppermute(value, MESH, pairs(change))]
    pallas_call x26 -> x20, Pallas kernels: 52.3 us -> 43.9 us  [call(): pl.pallas_call(body, out_shape=shapes, in_specs=[pl.BlockSpec(memory_spac...]
    slice x5 -> x0, local copies, waits for them, and re-layouts: 4.88 us -> none  [the longest x1 1.23 us: shards(): late_in[:, A:]]
    ppermute x2 -> x0, local copies, waits for them, and re-layouts: 4.47 us -> none  [to_other_core(): return lax.ppermute(value, MESH, pairs(lambda x, y, z, c: (x, y, z, 1 - c)))]
    all_to_all x1, waiting for transfers between devices: 6.82 us -> 10 us  [shards(): lax.all_to_all(both.reshape(8, LOCAL, D + A), 'seq', 0, 0, tiled=True)]
    ppermute x21 -> x15, starting transfers between devices: 23.9 us -> 21.2 us  [along(): return lax.ppermute(value, MESH, pairs(change))]
    pallas_call x2 -> x0, local copies, waits for them, and re-layouts: 2.64 us -> none  [call(): pl.pallas_call(body, out_shape=shapes, in_specs=[pl.BlockSpec(memory_spac...]
  transfers between devices with their start and end apart: 29 -> 22, of which waited for: 9 -> 12; matrix products, arithmetic and copies ran while one was open for 11% -> 0% of each run, Pallas kernels for 19% -> 16%
where the time goes in v2:
time: 145 us; the launch traced here: 144 us
  waiting for transfers between devices  48.6 us (34%)
  Pallas kernels  43.9 us (30%)
  starting transfers between devices  32.6 us (22%)
  local copies, waits for them, and re-layouts  18 us (12%)
    pallas_call x20, Pallas kernels, call(): pl.pallas_call(body, out_shape=shapes, in_specs=[pl.BlockSpec(memory_spac...  43.9 us
    ppermute x15, waiting for transfers between devices, along(): return lax.ppermute(value, MESH, pairs(change))  27.9 us
    ppermute x15, starting transfers between devices, along(): return lax.ppermute(value, MESH, pairs(change))  21.2 us
    unnamed x52, local copies, waits for them, and re-layouts  18 us
    all_to_all x1, waiting for transfers between devices, shards(): lax.all_to_all(both.reshape(8, LOCAL, D + A), 'seq', 0, 0, tiled=True)  10 us
    all_to_all x1, waiting for transfers between devices, shards(): lax.all_to_all(back_patch.reshape(8, LOCAL, D + A), 'seq', 0, 0, tiled=True)  9.47 us
    all_to_all x1, starting transfers between devices, shards(): lax.all_to_all(both.reshape(8, LOCAL, D + A), 'seq', 0, 0, tiled=True)  6.41 us
    all_to_all x1, starting transfers between devices, shards(): lax.all_to_all(back_patch.reshape(8, LOCAL, D + A), 'seq', 0, 0, tiled=True)  3.78 us
  transfers between devices with their start and end apart: 22, of which 12 were waited for; matrix products, arithmetic and copies ran while one was open for 0% of the time, Pallas kernels for 16%

profile of v2, /device:TPU:0, one launch (start us, length us, event | category | flops | bytes accessed | tf_op | source)
XLA Modules:
  0.0 144.0 jit_solution(11227192947149515354)
XLA Ops:
  0.6 2.1 %copy-done = bf16[1152,1728]{0,1:T(8,128)(2,1)S(1)} copy-done((bf16[1152,1728]{0,1:T(8,128)(2,1)S(1)}, bf16[1152,1728]{0,1:T(8,128)(2,1)}, u32[]{:S(2)}) %copy-start) | copy-done | bytes 3981336
  2.8 1.3 copy-done.2
  4.1 1.3 copy-done.4
  5.4 1.1 copy-done.6
  6.5 1.1 copy-done.8
  7.5 0.7 copy-done.15
  8.3 0.7 copy-done.17
  9.0 9.4 %shard_map.127 = (bf16[256,1728]{1,0:T(8,128)(2,1)}, f32[1728,256]{1,0:T(8,128)S(1)}, f32[8,256,256]{2,1,0:T(8,128)S(1)}, bf16[256,1152]{1,0:T(8,128)(2,1)S(1)},...) custom-call(bf16[256,1152]{1,0:T(8,128)(2,1)S(1)} %bitcast.20, bf16[256,1152]{1,0:T(8,128)(2,1)S(1)} %bitcast.22, ...), custom_call_target="tpu_custom_call" | custom-call | flops 1698693120 | bytes 14102656 | tf_op jit(solution)/shard_map/pallas_call | solution.py:35
  18.4 1.3 copy-done.10
  19.7 1.2 copy-done.12
  20.9 6.4 %all-to-all-start = ((bf16[8,32,1728]{2,1,0:T(8,128)(2,1)}), bf16[8,32,1728]{2,1,0:T(8,128)(2,1)S(1)}, u32[]{:S(2)}, u32[]{:S(2)}) async-start(bf16[8,32,1728]{2,1,0:T(8,128)(2,1)} %bitcast.5), calls=%async_computation | async-start | bytes 1835008 | tf_op jit(solution)/shard_map/all_to_all | solution.py:414
  27.3 3.4 %shard_map.128 = (bf16[256,1280]{1,0:T(8,128)(2,1)S(1)}, bf16[256,1920]{1,0:T(8,128)(2,1)}) custom-call(bf16[256,1152]{1,0:T(8,128)(2,1)S(1)} %get-tuple-element.69.normed, bf16[256,1152]{1,0:T(8,128)(2,1)S(1)} %get-tuple-element.70.scaled, bf16[256,640]{1,0:T(8,128)(2,1)S(1)} %get-tuple-element.71.att.refs_9_), custom_call_target="tpu_custom_call" | custom-call | flops 1358954496 | bytes 3145728 | tf_op jit(solution)/shard_map/pallas_call | solution.py:35
  30.7 10.0 %all-to-all-done = bf16[8,32,1728]{2,1,0:T(8,128)(2,1)S(1)} async-done(((bf16[8,32,1728]{2,1,0:T(8,128)(2,1)}), bf16[8,32,1728]{2,1,0:T(8,128)(2,1)S(1)}, u32[]{:S(2)}, u32[]{:S(2)}) %all-to-all-start) | async-done | bytes 884768 | tf_op jit(solution)/shard_map/all_to_all | solution.py:414
  40.7 2.1 %copy-done.19 = bf16[1152,1728]{0,1:T(8,128)(2,1)S(1)} copy-done((bf16[1152,1728]{0,1:T(8,128)(2,1)S(1)}, bf16[1152,1728]{0,1:T(8,128)(2,1)}, u32[]{:S(2)}) %copy-start.19) | copy-done | bytes 3981336
  42.8 9.7 %shard_map.129 = (bf16[256,1728]{1,0:T(8,128)(2,1)S(1)}, bf16[256,1152]{1,0:T(8,128)(2,1)S(1)}, bf16[256,1792]{1,0:T(8,128)(2,1)}) custom-call(bf16[256,1728]{1,0:T(8,128)(2,1)S(1)} %bitcast.25, f32[3,2,1152]{2,1,0:T(2,128)S(1)} %bitcast.27, f32[2,2,72]{2,1,0:T(2,128)S(1)} %copy-done.18, bf16[1728,1152]{1,0:T(8,128)(2,1)S(1)} %bitcast.31), custom_call_target="tpu_custom_call" | custom-call | flops 2038431744 | bytes 7286912 | tf_op jit(solution)/shard_map/pallas_call | solution.py:35
  52.5 0.9 copy-done.14
  53.5 0.8 copy-done.24
  54.3 3.8 %all-to-all-start.1 = ((bf16[8,32,1728]{2,1,0:T(8,128)(2,1)}), bf16[8,32,1728]{2,1,0:T(8,128)(2,1)S(1)}, u32[]{:S(2)}, u32[]{:S(2)}) async-start(bf16[8,32,1728]{2,1,0:T(8,128)(2,1)} %bitcast.24), calls=%async_computation.1 | async-start | bytes 1835008 | tf_op jit(solution)/shard_map/all_to_all | solution.py:431
  58.1 1.1 copy-done.25
  59.1 1.2 shard_map.130
  60.4 0.7 copy-done.22
  61.1 0.4 collective-permute-start.1
  61.6 1.2 collective-permute-done.1.refs_1_
  62.8 9.5 %all-to-all-done.1 = bf16[8,32,1728]{2,1,0:T(8,128)(2,1)S(1)} async-done(((bf16[8,32,1728]{2,1,0:T(8,128)(2,1)}), bf16[8,32,1728]{2,1,0:T(8,128)(2,1)S(1)}, u32[]{:S(2)}, u32[]{:S(2)}) %all-to-all-start.1) | async-done | bytes 884768 | tf_op jit(solution)/shard_map/all_to_all | solution.py:431
  72.3 3.8 %shard_map.131 = (bf16[256,1152]{1,0:T(8,128)(2,1)S(1)}, f32[256,640]{1,0:T(8,128)S(1)}, bf16[256,640]{1,0:T(8,128)(2,1)S(1)}, bf16[256,1280]{1,0:T(8,128)(2,1)S(1)}) custom-call(bf16[256,1728]{1,0:T(8,128)(2,1)S(1)} %bitcast.17, bf16[256,1728]{1,0:T(8,128)(2,1)} %get-tuple-element.68.both, bf16[256,1152]{1,0:T(8,128)(2,1)S(1)} %bitcast.23, ...), custom_call_target="tpu_custom_call" | custom-call | flops 1019215872 | bytes 5942272 | tf_op jit(solution)/shard_map/pallas_call | solution.py:35
  76.2 1.5 %copy-done.13 = f32[1728,256]{1,0:T(8,128)S(1)} copy-done((f32[1728,256]{1,0:T(8,128)S(1)}, f32[1728,256]{1,0:T(8,128)}, u32[]{:S(2)}) %copy-start.13) | copy-done | bytes 1769496
  77.6 2.8 %shard_map.132.refs_2_.qkv_grad = bf16[256,1792]{1,0:T(8,128)(2,1)S(1)} custom-call(f32[256,640]{1,0:T(8,128)S(1)} %get-tuple-element.82.att_grad, f32[1728,256]{1,0:T(8,128)S(1)} %copy-done.13, f32[8,256,256]{2,1,0:T(8,128)S(1)} %copy-done.11, f32[2,2,72]{2,1,0:T(2,128)S(1)} %copy-done.18), custom_call_target="tpu_custom_call" | custom-call | flops 671088640 | bytes 5440640 | tf_op jit(solution)/shard_map/pallas_call | solution.py:35
  80.5 0.6 collective-permute-start.3
  81.1 3.9 %shard_map.136 = (f32[3,96,3072]{2,1,0:T(8,128)S(1)}, bf16[96,3072]{1,0:T(8,128)(2,1)S(1)}, bf16[96,3072]{1,0:T(8,128)(2,1)S(1)}, bf16[96,3072]{1,0:T(8,128)(2,1)S(1)}) custom-call(bf16[256,640]{1,0:T(8,128)(2,1)S(1)} %copy-done.23, bf16[256,640]{1,0:T(8,128)(2,1)S(1)} %collective-permute-done.1.refs_1_, bf16[256,1792]{1,0:T(8,128)(2,1)} %get-tuple-element.80.refs_2_, ...), custom_call_target="tpu_custom_call" | custom-call | flops 1811939328 | bytes 11632640 | tf_op jit(solution)/shard_map/pallas_call | solution.py:35
  85.0 1.6 %collective-permute-start.5 = (bf16[96,3072]{1,0:T(8,128)(2,1)S(1)}, bf16[96,3072]{1,0:T(8,128)(2,1)S(1)}, u32[]{:S(2)}, u32[]{:S(2)}) collective-permute-start(bf16[96,3072]{1,0:T(8,128)(2,1)S(1)} %get-tuple-element.101), channel_id=1, source_target_pairs={{0,32},{1,33},{2,34},{3,35},{4,36},{5,37},{6,38},{7,39},{8,104},{9... | collective-permute-start | bytes 1769480 | tf_op jit(solution)/shard_map/ppermute | solution.py:381
  86.6 1.5 %collective-permute-start.8 = (bf16[96,3072]{1,0:T(8,128)(2,1)S(1)}, bf16[96,3072]{1,0:T(8,128)(2,1)S(1)}, u32[]{:S(2)}, u32[]{:S(2)}) collective-permute-start(bf16[96,3072]{1,0:T(8,128)(2,1)S(1)} %get-tuple-element.107), channel_id=1, source_target_pairs={{0,4},{1,5},{2,6},{3,7},{4,0},{5,1},{6,2},{7,3},{8,28},{9,29},{10,... | collective-permute-start | bytes 1769480 | tf_op jit(solution)/shard_map/ppermute | solution.py:381
  88.1 0.8 collective-permute-start.11
  88.9 2.6 %shard_map.133 = (f32[3,96,1792]{2,1,0:T(8,128)S(1)}, bf16[96,1792]{1,0:T(8,128)(2,1)S(1)}, bf16[96,1792]{1,0:T(8,128)(2,1)S(1)}, bf16[96,1792]{1,0:T(8,128)(2,1)S(1)}) custom-call(bf16[256,1280]{1,0:T(8,128)(2,1)S(1)} %copy-done.21, bf16[256,1920]{1,0:T(8,128)(2,1)} %collective-permute-done.refs_1_.refs_5_, ...), custom_call_target="tpu_custom_call" | custom-call | flops 1056964608 | bytes 6569984 | tf_op jit(solution)/shard_map/pallas_call | solution.py:35
  91.5 0.6 collective-permute-start.6
  92.2 0.6 collective-permute-start.9
  92.7 2.2 %collective-permute-done.5.refs_1_ = bf16[96,3072]{1,0:T(8,128)(2,1)S(1)} collective-permute-done((bf16[96,3072]{1,0:T(8,128)(2,1)S(1)}, bf16[96,3072]{1,0:T(8,128)(2,1)S(1)}, u32[]{:S(2)}, u32[]{:S(2)}) %collective-permute-start.5) | collective-permute-done | bytes 589856 | tf_op jit(solution)/shard_map/ppermute | solution.py:381
  95.0 0.9 collective-permute-start.12
  95.8 2.6 %shard_map.135 = bf16[256,1152]{1,0:T(8,128)(2,1)} custom-call(bf16[256,1728]{1,0:T(8,128)(2,1)} %get-tuple-element.68.both, bf16[256,1728]{1,0:T(8,128)(2,1)S(1)} %bitcast.19, f32[3,2,1152]{2,1,0:T(2,128)S(1)} %bitcast.29, bf16[576,1152]{1,0:T(8,128)(2,1)S(1)} %copy-done.5), custom_call_target="tpu_custom_call" | custom-call | flops 339738624 | bytes 3714048 | tf_op jit(solution)/shard_map/pallas_call | solution.py:35
  98.5 2.6 %shard_map.134 = bf16[256,1152]{1,0:T(8,128)(2,1)} custom-call(bf16[256,1152]{1,0:T(8,128)(2,1)S(1)} %get-tuple-element.91.mid_grad, bf16[256,1792]{1,0:T(8,128)(2,1)S(1)} %shard_map.132.refs_2_.qkv_grad, bf16[256,1152]{1,0:T(8,128)(2,1)S(1)} %bitcast.21, f32[3,2,1152]{2,1,0:T(2,128)S(1)} %bitcast.30, bf16[1728,1152]{1,0:T(8,128)(2,1)S(1)} %bitcast.16), custom_call_target="tpu_custom_call" | custom-call | flops 1019215872 | bytes 6695936 | tf_op jit(solution)/shard_map/pallas_call | solution.py:35
  101.1 0.2 shard_map.137
  101.2 1.5 %collective-permute-start.7 = (bf16[48,4864]{1,0:T(8,128)(2,1)S(1)}, bf16[48,4864]{1,0:T(8,128)(2,1)S(1)}, u32[]{:S(2)}, u32[]{:S(2)}) collective-permute-start(bf16[48,4864]{1,0:T(8,128)(2,1)S(1)} %get-tuple-element.105), channel_id=1, source_target_pairs={{0,4},{1,5},{2,6},{3,7},{4,0},{5,1},{6,2},{7,3},{8,28},{9,29},{10,... | collective-permute-start | bytes 1400840 | tf_op jit(solution)/shard_map/ppermute | solution.py:381
  102.8 0.2 shard_map.139
  102.9 1.3 collective-permute-start.10
  104.2 0.2 shard_map.141
  104.4 1.6 %collective-permute-start.13 = (bf16[48,4864]{1,0:T(8,128)(2,1)S(1)}, bf16[48,4864]{1,0:T(8,128)(2,1)S(1)}, u32[]{:S(2)}, u32[]{:S(2)}) collective-permute-start(bf16[48,4864]{1,0:T(8,128)(2,1)S(1)} %get-tuple-element.115), channel_id=1, source_target_pairs={{0,32},{1,33},{2,34},{3,35},{4,36},{5,37},{6,38},{7,39},{8,104},{9... | collective-permute-start | bytes 1400840 | tf_op jit(solution)/shard_map/ppermute | solution.py:381
  105.9 3.9 %collective-permute-done.7.got = bf16[48,4864]{1,0:T(8,128)(2,1)S(1)} collective-permute-done((bf16[48,4864]{1,0:T(8,128)(2,1)S(1)}, bf16[48,4864]{1,0:T(8,128)(2,1)S(1)}, u32[]{:S(2)}, u32[]{:S(2)}) %collective-permute-start.7) | collective-permute-done | bytes 466976 | tf_op jit(solution)/shard_map/ppermute | solution.py:381
  110.0 1.3 collective-permute-start.14
  111.2 0.4 collective-permute-done.10.got
  111.6 0.1 shard_map.140
  111.7 1.6 %collective-permute-start.15 = (bf16[24,4864]{1,0:T(8,128)(2,1)S(1)}, bf16[24,4864]{1,0:T(8,128)(2,1)S(1)}, u32[]{:S(2)}, u32[]{:S(2)}) collective-permute-start(bf16[24,4864]{1,0:T(8,128)(2,1)S(1)} %get-tuple-element.118), channel_id=1, source_target_pairs={{0,32},{1,33},{2,34},{3,35},{4,36},{5,37},{6,38},{7,39},{8,104},{9... | collective-permute-start | bytes 700424 | tf_op jit(solution)/shard_map/ppermute | solution.py:381
  113.3 1.2 collective-permute-start.16
  114.6 1.5 %collective-permute-done.14.refs_3_ = bf16[24,4864]{1,0:T(8,128)(2,1)S(1)} collective-permute-done((bf16[24,4864]{1,0:T(8,128)(2,1)S(1)}, bf16[24,4864]{1,0:T(8,128)(2,1)S(1)}, u32[]{:S(2)}, u32[]{:S(2)}) %collective-permute-start.14) | collective-permute-done | bytes 233504 | tf_op jit(solution)/shard_map/ppermute | solution.py:381
  116.1 1.7 %collective-permute-done.15.refs_4_ = bf16[24,4864]{1,0:T(8,128)(2,1)S(1)} collective-permute-done((bf16[24,4864]{1,0:T(8,128)(2,1)S(1)}, bf16[24,4864]{1,0:T(8,128)(2,1)S(1)}, u32[]{:S(2)}, u32[]{:S(2)}) %collective-permute-start.15) | collective-permute-done | bytes 233504 | tf_op jit(solution)/shard_map/ppermute | solution.py:381
  117.8 1.7 %collective-permute-done.16.refs_5_ = bf16[24,4864]{1,0:T(8,128)(2,1)S(1)} collective-permute-done((bf16[24,4864]{1,0:T(8,128)(2,1)S(1)}, bf16[24,4864]{1,0:T(8,128)(2,1)S(1)}, u32[]{:S(2)}, u32[]{:S(2)}) %collective-permute-start.16) | collective-permute-done | bytes 233504 | tf_op jit(solution)/shard_map/ppermute | solution.py:381
  119.5 0.2 shard_map.143
  119.7 2.6 %collective-permute-start.17 = (bf16[3,12,4864]{2,1,0:T(8,128)(2,1)S(1)}, bf16[3,12,4864]{2,1,0:T(8,128)(2,1)S(1)}, u32[]{:S(2)}, u32[]{:S(2)}) collective-permute-start(bf16[3,12,4864]{2,1,0:T(8,128)(2,1)S(1)} %get-tuple-element.121), channel_id=1, source_target_pairs={{0,96},{1,97},{2,98},{3,99},{4,100},{5,101},{6,102},{7,103},{8,40}... | collective-permute-start | bytes 1050632 | tf_op jit(solution)/shard_map/ppermute | solution.py:381
  122.3 7.3 %collective-permute-done.17.got = bf16[3,12,4864]{2,1,0:T(8,128)(2,1)S(1)} collective-permute-done((bf16[3,12,4864]{2,1,0:T(8,128)(2,1)S(1)}, bf16[3,12,4864]{2,1,0:T(8,128)(2,1)S(1)}, u32[]{:S(2)}, u32[]{:S(2)}) %collective-permute-start.17) | collective-permute-done | bytes 350240 | tf_op jit(solution)/shard_map/ppermute | solution.py:381
  129.5 0.1 shard_map.144
  129.7 2.7 %collective-permute-start.18 = (bf16[3,6,4864]{2,1,0:T(8,128)(2,1)S(1)}, bf16[3,6,4864]{2,1,0:T(8,128)(2,1)S(1)}, u32[]{:S(2)}, u32[]{:S(2)}) collective-permute-start(bf16[3,6,4864]{2,1,0:T(8,128)(2,1)S(1)} %get-tuple-element.123), channel_id=1, source_target_pairs={{0,20},{1,21},{2,22},{3,23},{4,16},{5,17},{6,18},{7,19},{8,12},{9,... | collective-permute-start | bytes 525320 | tf_op jit(solution)/shard_map/ppermute | solution.py:381
  132.3 4.7 %collective-permute-done.18.got = bf16[3,6,4864]{2,1,0:T(8,128)(2,1)S(1)} collective-permute-done((bf16[3,6,4864]{2,1,0:T(8,128)(2,1)S(1)}, bf16[3,6,4864]{2,1,0:T(8,128)(2,1)S(1)}, u32[]{:S(2)}, u32[]{:S(2)}) %collective-permute-start.18) | collective-permute-done | bytes 175136 | tf_op jit(solution)/shard_map/ppermute | solution.py:381
  137.0 0.1 shard_map.145
  137.2 1.6 %collective-permute-start.19 = (bf16[3,3,4864]{2,1,0:T(4,128)(2,1)S(1)}, bf16[3,3,4864]{2,1,0:T(4,128)(2,1)S(1)}, u32[]{:S(2)}, u32[]{:S(2)}) collective-permute-start(bf16[3,3,4864]{2,1,0:T(4,128)(2,1)S(1)} %get-tuple-element.125), channel_id=1, source_target_pairs={{0,3},{1,2},{2,1},{3,0},{4,7},{5,6},{6,5},{7,4},{8,9},{9,8},{10,11... | collective-permute-start | bytes 262664 | tf_op jit(solution)/shard_map/ppermute | solution.py:381
  138.8 4.5 %collective-permute-done.19.got = bf16[3,3,4864]{2,1,0:T(4,128)(2,1)S(1)} collective-permute-done((bf16[3,3,4864]{2,1,0:T(4,128)(2,1)S(1)}, bf16[3,3,4864]{2,1,0:T(4,128)(2,1)S(1)}, u32[]{:S(2)}, u32[]{:S(2)}) %collective-permute-start.19) | collective-permute-done | bytes 87584 | tf_op jit(solution)/shard_map/ppermute | solution.py:381
  143.3 0.7 shard_map.146
  (52 shorter events, 0.5 us)
Async XLA Ops:
  0.6 2.1 %copy-start = (bf16[1152,1728]{0,1:T(8,128)(2,1)S(1)}, bf16[1152,1728]{0,1:T(8,128)(2,1)}, u32[]{:S(2)}) copy-start(bf16[1152,1728]{0,1:T(8,128)(2,1)} %param.12) | copy-start | bytes 11943940
  2.8 1.3 copy-start.2
  4.1 1.3 copy-start.4
  5.4 1.1 copy-start.6
  6.5 1.1 copy-start.8
  7.5 0.7 copy-start.15
  8.3 0.7 copy-start.17
  18.4 1.3 copy-start.10
  19.7 1.2 copy-start.12
  20.9 19.8 %all-to-all-start = ((bf16[8,32,1728]{2,1,0:T(8,128)(2,1)}), bf16[8,32,1728]{2,1,0:T(8,128)(2,1)S(1)}, u32[]{:S(2)}, u32[]{:S(2)}) async-start(bf16[8,32,1728]{2,1,0:T(8,128)(2,1)} %bitcast.5), calls=%async_computation | async-start | bytes 1835008 | tf_op jit(solution)/shard_map/all_to_all | solution.py:414
  27.3 13.4 %copy-start.16 = (f32[1,2,3,1152]{3,1,2,0:T(2,128)S(1)}, f32[1,2,3,1152]{3,1,2,0:T(2,128)}, u32[]{:S(2)}) copy-start(f32[1,2,3,1152]{3,1,2,0:T(2,128)} %param.10) | copy-start | bytes 82948
  27.3 13.4 %copy-start.18 = (f32[2,2,72]{2,1,0:T(2,128)S(1)}, f32[2,2,72]{2,1,0:T(2,128)}, u32[]{:S(2)}) copy-start(f32[2,2,72]{2,1,0:T(2,128)} %gains.5) | copy-start | bytes 3460
  30.7 21.8 %copy-start.20 = (bf16[256,1280]{1,0:T(8,128)(2,1)}, bf16[256,1280]{1,0:T(8,128)(2,1)S(1)}, u32[]{:S(2)}) copy-start(bf16[256,1280]{1,0:T(8,128)(2,1)S(1)} %get-tuple-element.74.refs_0_.refs_4_) | copy-start | bytes 1966084
  40.7 2.1 %copy-start.19 = (bf16[1152,1728]{0,1:T(8,128)(2,1)S(1)}, bf16[1152,1728]{0,1:T(8,128)(2,1)}, u32[]{:S(2)}) copy-start(bf16[1152,1728]{0,1:T(8,128)(2,1)} %param.14) | copy-start | bytes 11943940
  52.5 0.9 copy-start.14
  53.5 0.8 copy-start.24
  54.3 18.0 %collective-permute-start.2 = (bf16[256,1792]{1,0:T(8,128)(2,1)}, bf16[256,1792]{1,0:T(8,128)(2,1)}, u32[]{:S(2)}, u32[]{:S(2)}) collective-permute-start(bf16[256,1792]{1,0:T(8,128)(2,1)} %get-tuple-element.80.refs_2_), channel_id=1, source_target_pairs={{0,8},{1,9},{2,10},{3,11},{4,12},{5,13},{6,14},{7,15},{8,0},{9,1},... | collective-permute-start | bytes 2752520 | tf_op jit(solution)/shard_map/ppermute | solution.py:372
  54.3 18.0 %copy-start.3 = (bf16[576,1152]{1,0:T(8,128)(2,1)S(1)}, bf16[576,1152]{1,0:T(8,128)(2,1)}, u32[]{:S(2)}) copy-start(bf16[576,1152]{1,0:T(8,128)(2,1)} %w_out.2) | copy-start | bytes 3981316
  54.3 18.0 %copy-start.9 = (bf16[1,1,256,1152]{3,2,1,0:T(8,128)(2,1)S(1)}, bf16[1,1,256,1152]{3,2,1,0:T(8,128)(2,1)}, u32[]{:S(2)}) copy-start(bf16[1,1,256,1152]{3,2,1,0:T(8,128)(2,1)} %param.9) | copy-start | bytes 1769476
  54.3 17.9 %all-to-all-start.1 = ((bf16[8,32,1728]{2,1,0:T(8,128)(2,1)}), bf16[8,32,1728]{2,1,0:T(8,128)(2,1)S(1)}, u32[]{:S(2)}, u32[]{:S(2)}) async-start(bf16[8,32,1728]{2,1,0:T(8,128)(2,1)} %bitcast.24), calls=%async_computation.1 | async-start | bytes 1835008 | tf_op jit(solution)/shard_map/all_to_all | solution.py:431
  58.1 1.1 copy-start.25
  60.4 0.7 copy-start.22
  61.1 1.7 %collective-permute-start.1 = (bf16[256,640]{1,0:T(8,128)(2,1)S(1)}, bf16[256,640]{1,0:T(8,128)(2,1)S(1)}, u32[]{:S(2)}, u32[]{:S(2)}) collective-permute-start(bf16[256,640]{1,0:T(8,128)(2,1)S(1)} %get-tuple-element.79), channel_id=1, source_target_pairs={{0,8},{1,9},{2,10},{3,11},{4,12},{5,13},{6,14},{7,15},{8,0},{9,1},... | collective-permute-start | bytes 983048 | tf_op jit(solution)/shard_map/ppermute | solution.py:372
  61.5 19.5 %collective-permute-start = (bf16[256,1920]{1,0:T(8,128)(2,1)}, bf16[256,1920]{1,0:T(8,128)(2,1)}, u32[]{:S(2)}, u32[]{:S(2)}) collective-permute-start(bf16[256,1920]{1,0:T(8,128)(2,1)} %get-tuple-element.75), channel_id=1, source_target_pairs={{0,8},{1,9},{2,10},{3,11},{4,12},{5,13},{6,14},{7,15},{8,0},{9,1},... | collective-permute-start | bytes 2949128 | tf_op jit(solution)/shard_map/ppermute | solution.py:372
  72.2 3.9 %copy-start.11 = (f32[8,256,256]{2,1,0:T(8,128)S(1)}, f32[8,256,256]{2,1,0:T(8,128)}, u32[]{:S(2)}) copy-start(f32[8,256,256]{2,1,0:T(8,128)} %copy-done.10) | copy-start | bytes 6291460
  76.0 5.0 %collective-permute-start.4 = (bf16[256,1280]{1,0:T(8,128)(2,1)S(1)}, bf16[256,1280]{1,0:T(8,128)(2,1)S(1)}, u32[]{:S(2)}, u32[]{:S(2)}) collective-permute-start(bf16[256,1280]{1,0:T(8,128)(2,1)S(1)} %get-tuple-element.98), channel_id=1, source_target_pairs={{0,8},{1,9},{2,10},{3,11},{4,12},{5,13},{6,14},{7,15},{8,0},{9,1},... | collective-permute-start | bytes 1966088 | tf_op jit(solution)/shard_map/ppermute | solution.py:372
  76.1 1.5 %copy-start.13 = (f32[1728,256]{1,0:T(8,128)S(1)}, f32[1728,256]{1,0:T(8,128)}, u32[]{:S(2)}) copy-start(f32[1728,256]{1,0:T(8,128)} %copy-done.12) | copy-start | bytes 5308420
  77.6 3.4 %copy-start.21 = (bf16[256,1280]{1,0:T(8,128)(2,1)S(1)}, bf16[256,1280]{1,0:T(8,128)(2,1)}, u32[]{:S(2)}) copy-start(bf16[256,1280]{1,0:T(8,128)(2,1)} %copy-done.20) | copy-start | bytes 1966084
  77.6 3.4 %copy-start.23 = (bf16[256,640]{1,0:T(8,128)(2,1)S(1)}, bf16[256,640]{1,0:T(8,128)(2,1)}, u32[]{:S(2)}) copy-start(bf16[256,640]{1,0:T(8,128)(2,1)} %copy-done.22) | copy-start | bytes 983044
  80.5 8.4 %collective-permute-start.3 = (bf16[256,1792]{1,0:T(8,128)(2,1)S(1)}, bf16[256,1792]{1,0:T(8,128)(2,1)S(1)}, u32[]{:S(2)}, u32[]{:S(2)}) collective-permute-start(bf16[256,1792]{1,0:T(8,128)(2,1)S(1)} %shard_map.132.refs_2_.qkv_grad), channel_id=1, source_target_pairs={{0,8},{1,9},{2,10},{3,11},{4,12},{5,13},{6,14},{7,15},{8,0},{9,1},... | collective-permute-start | bytes 2752520 | tf_op jit(solution)/shard_map/ppermute | solution.py:372
  85.0 10.8 %copy-start.5 = (bf16[576,1152]{1,0:T(8,128)(2,1)S(1)}, bf16[576,1152]{1,0:T(8,128)(2,1)}, u32[]{:S(2)}) copy-start(bf16[576,1152]{1,0:T(8,128)(2,1)} %w_out.3) | copy-start | bytes 3981316
  85.0 10.0 %collective-permute-start.5 = (bf16[96,3072]{1,0:T(8,128)(2,1)S(1)}, bf16[96,3072]{1,0:T(8,128)(2,1)S(1)}, u32[]{:S(2)}, u32[]{:S(2)}) collective-permute-start(bf16[96,3072]{1,0:T(8,128)(2,1)S(1)} %get-tuple-element.101), channel_id=1, source_target_pairs={{0,32},{1,33},{2,34},{3,35},{4,36},{5,37},{6,38},{7,39},{8,104},{9... | collective-permute-start | bytes 1769480 | tf_op jit(solution)/shard_map/ppermute | solution.py:381
  86.6 16.2 %collective-permute-start.8 = (bf16[96,3072]{1,0:T(8,128)(2,1)S(1)}, bf16[96,3072]{1,0:T(8,128)(2,1)S(1)}, u32[]{:S(2)}, u32[]{:S(2)}) collective-permute-start(bf16[96,3072]{1,0:T(8,128)(2,1)S(1)} %get-tuple-element.107), channel_id=1, source_target_pairs={{0,4},{1,5},{2,6},{3,7},{4,0},{5,1},{6,2},{7,3},{8,28},{9,29},{10,... | collective-permute-start | bytes 1769480 | tf_op jit(solution)/shard_map/ppermute | solution.py:381
  88.1 16.1 %collective-permute-start.11 = (bf16[96,3072]{1,0:T(8,128)(2,1)S(1)}, bf16[96,3072]{1,0:T(8,128)(2,1)S(1)}, u32[]{:S(2)}, u32[]{:S(2)}) collective-permute-start(bf16[96,3072]{1,0:T(8,128)(2,1)S(1)} %get-tuple-element.112), channel_id=1, source_target_pairs={{0,1},{1,0},{2,3},{3,2},{4,5},{5,4},{6,7},{7,6},{8,11},{9,10},{10,... | collective-permute-start | bytes 1769480 | tf_op jit(solution)/shard_map/ppermute | solution.py:381
  88.9 9.6 %copy-start.1 = (bf16[1152,1728]{0,1:T(8,128)(2,1)S(1)}, bf16[1152,1728]{0,1:T(8,128)(2,1)}, u32[]{:S(2)}) copy-start(bf16[1152,1728]{0,1:T(8,128)(2,1)} %param.12) | copy-start | bytes 11943940
  91.5 7.0 %copy-start.7 = (bf16[1,1,256,1152]{3,2,1,0:T(8,128)(2,1)S(1)}, bf16[1,1,256,1152]{3,2,1,0:T(8,128)(2,1)}, u32[]{:S(2)}) copy-start(bf16[1,1,256,1152]{3,2,1,0:T(8,128)(2,1)} %param.8) | copy-start | bytes 1769476
  91.5 9.5 %collective-permute-start.6 = (bf16[96,1792]{1,0:T(8,128)(2,1)S(1)}, bf16[96,1792]{1,0:T(8,128)(2,1)S(1)}, u32[]{:S(2)}, u32[]{:S(2)}) collective-permute-start(bf16[96,1792]{1,0:T(8,128)(2,1)S(1)} %get-tuple-element.103), channel_id=1, source_target_pairs={{0,32},{1,33},{2,34},{3,35},{4,36},{5,37},{6,38},{7,39},{8,104},{9... | collective-permute-start | bytes 1032200 | tf_op jit(solution)/shard_map/ppermute | solution.py:381
  92.2 10.6 %collective-permute-start.9 = (bf16[96,1792]{1,0:T(8,128)(2,1)S(1)}, bf16[96,1792]{1,0:T(8,128)(2,1)S(1)}, u32[]{:S(2)}, u32[]{:S(2)}) collective-permute-start(bf16[96,1792]{1,0:T(8,128)(2,1)S(1)} %get-tuple-element.108), channel_id=1, source_target_pairs={{0,4},{1,5},{2,6},{3,7},{4,0},{5,1},{6,2},{7,3},{8,28},{9,29},{10,... | collective-permute-start | bytes 1032200 | tf_op jit(solution)/shard_map/ppermute | solution.py:381
  95.0 9.2 %collective-permute-start.12 = (bf16[96,1792]{1,0:T(8,128)(2,1)S(1)}, bf16[96,1792]{1,0:T(8,128)(2,1)S(1)}, u32[]{:S(2)}, u32[]{:S(2)}) collective-permute-start(bf16[96,1792]{1,0:T(8,128)(2,1)S(1)} %get-tuple-element.113), channel_id=1, source_target_pairs={{0,1},{1,0},{2,3},{3,2},{4,5},{5,4},{6,7},{7,6},{8,11},{9,10},{10,... | collective-permute-start | bytes 1032200 | tf_op jit(solution)/shard_map/ppermute | solution.py:381
  101.2 8.6 %collective-permute-start.7 = (bf16[48,4864]{1,0:T(8,128)(2,1)S(1)}, bf16[48,4864]{1,0:T(8,128)(2,1)S(1)}, u32[]{:S(2)}, u32[]{:S(2)}) collective-permute-start(bf16[48,4864]{1,0:T(8,128)(2,1)S(1)} %get-tuple-element.105), channel_id=1, source_target_pairs={{0,4},{1,5},{2,6},{3,7},{4,0},{5,1},{6,2},{7,3},{8,28},{9,29},{10,... | collective-permute-start | bytes 1400840 | tf_op jit(solution)/shard_map/ppermute | solution.py:381
  102.9 8.6 %collective-permute-start.10 = (bf16[48,4864]{1,0:T(8,128)(2,1)S(1)}, bf16[48,4864]{1,0:T(8,128)(2,1)S(1)}, u32[]{:S(2)}, u32[]{:S(2)}) collective-permute-start(bf16[48,4864]{1,0:T(8,128)(2,1)S(1)} %get-tuple-element.110), channel_id=1, source_target_pairs={{0,1},{1,0},{2,3},{3,2},{4,5},{5,4},{6,7},{7,6},{8,11},{9,10},{10,... | collective-permute-start | bytes 1400840 | tf_op jit(solution)/shard_map/ppermute | solution.py:381
  104.4 8.9 %collective-permute-start.13 = (bf16[48,4864]{1,0:T(8,128)(2,1)S(1)}, bf16[48,4864]{1,0:T(8,128)(2,1)S(1)}, u32[]{:S(2)}, u32[]{:S(2)}) collective-permute-start(bf16[48,4864]{1,0:T(8,128)(2,1)S(1)} %get-tuple-element.115), channel_id=1, source_target_pairs={{0,32},{1,33},{2,34},{3,35},{4,36},{5,37},{6,38},{7,39},{8,104},{9... | collective-permute-start | bytes 1400840 | tf_op jit(solution)/shard_map/ppermute | solution.py:381
  110.0 6.1 %collective-permute-start.14 = (bf16[24,4864]{1,0:T(8,128)(2,1)S(1)}, bf16[24,4864]{1,0:T(8,128)(2,1)S(1)}, u32[]{:S(2)}, u32[]{:S(2)}) collective-permute-start(bf16[24,4864]{1,0:T(8,128)(2,1)S(1)} %get-tuple-element.117), channel_id=1, source_target_pairs={{0,1},{1,0},{2,3},{3,2},{4,5},{5,4},{6,7},{7,6},{8,11},{9,10},{10,... | collective-permute-start | bytes 700424 | tf_op jit(solution)/shard_map/ppermute | solution.py:381
  111.7 6.1 %collective-permute-start.15 = (bf16[24,4864]{1,0:T(8,128)(2,1)S(1)}, bf16[24,4864]{1,0:T(8,128)(2,1)S(1)}, u32[]{:S(2)}, u32[]{:S(2)}) collective-permute-start(bf16[24,4864]{1,0:T(8,128)(2,1)S(1)} %get-tuple-element.118), channel_id=1, source_target_pairs={{0,32},{1,33},{2,34},{3,35},{4,36},{5,37},{6,38},{7,39},{8,104},{9... | collective-permute-start | bytes 700424 | tf_op jit(solution)/shard_map/ppermute | solution.py:381
  113.3 6.1 %collective-permute-start.16 = (bf16[24,4864]{1,0:T(8,128)(2,1)S(1)}, bf16[24,4864]{1,0:T(8,128)(2,1)S(1)}, u32[]{:S(2)}, u32[]{:S(2)}) collective-permute-start(bf16[24,4864]{1,0:T(8,128)(2,1)S(1)} %get-tuple-element.119), channel_id=1, source_target_pairs={{0,4},{1,5},{2,6},{3,7},{4,0},{5,1},{6,2},{7,3},{8,28},{9,29},{10,... | collective-permute-start | bytes 700424 | tf_op jit(solution)/shard_map/ppermute | solution.py:381
  119.7 9.9 %collective-permute-start.17 = (bf16[3,12,4864]{2,1,0:T(8,128)(2,1)S(1)}, bf16[3,12,4864]{2,1,0:T(8,128)(2,1)S(1)}, u32[]{:S(2)}, u32[]{:S(2)}) collective-permute-start(bf16[3,12,4864]{2,1,0:T(8,128)(2,1)S(1)} %get-tuple-element.121), channel_id=1, source_target_pairs={{0,96},{1,97},{2,98},{3,99},{4,100},{5,101},{6,102},{7,103},{8,40}... | collective-permute-start | bytes 1050632 | tf_op jit(solution)/shard_map/ppermute | solution.py:381
  129.7 7.4 %collective-permute-start.18 = (bf16[3,6,4864]{2,1,0:T(8,128)(2,1)S(1)}, bf16[3,6,4864]{2,1,0:T(8,128)(2,1)S(1)}, u32[]{:S(2)}, u32[]{:S(2)}) collective-permute-start(bf16[3,6,4864]{2,1,0:T(8,128)(2,1)S(1)} %get-tuple-element.123), channel_id=1, source_target_pairs={{0,20},{1,21},{2,22},{3,23},{4,16},{5,17},{6,18},{7,19},{8,12},{9,... | collective-permute-start | bytes 525320 | tf_op jit(solution)/shard_map/ppermute | solution.py:381
  137.2 6.1 %collective-permute-start.19 = (bf16[3,3,4864]{2,1,0:T(4,128)(2,1)S(1)}, bf16[3,3,4864]{2,1,0:T(4,128)(2,1)S(1)}, u32[]{:S(2)}, u32[]{:S(2)}) collective-permute-start(bf16[3,3,4864]{2,1,0:T(4,128)(2,1)S(1)} %get-tuple-element.125), channel_id=1, source_target_pairs={{0,3},{1,2},{2,1},{3,0},{4,7},{5,6},{6,5},{7,4},{8,9},{9,8},{10,11... | collective-permute-start | bytes 262664 | tf_op jit(solution)/shard_map/ppermute | solution.py:381

commit v3 on v2

--- a/solution.py
+++ b/solution.py
@@ -1,3 +1,5 @@
+import math
+
 import jax
 import jax.numpy as jnp
 from jax import lax
@@ -27,16 +29,28 @@
     )
 
 
-def call(body, outs, args, flops, scratch=(), limit=24, apart=()):
-    shapes = tuple(jax.ShapeDtypeStruct(shape, kind) for shape, kind in outs)
+def call(body, outs, args, flops, scratch=(), limit=16, apart=()):
+    shapes, specs = [], []
+    for k, (shape, kind, *place) in enumerate(outs):
+        if not place:
+            shapes.append(pltpu.VMEM(shape, kind))
+        elif place[0] == "hbm":
+            shapes.append(pltpu.HBM(shape, kind))
+        else:
+            shapes.append(jax.ShapeDtypeStruct(shape, kind))
+        specs.append(pl.BlockSpec(memory_space=pltpu.HBM if place == ["hbm"] else pltpu.VMEM))
     size = sum(x.size * x.dtype.itemsize for x in args)
-    size += sum(x.size * x.dtype.itemsize for x in shapes)
+    size += sum(math.prod(out[0]) * jnp.dtype(out[1]).itemsize for out in outs)
+    args = [
+        pltpu.with_memory_space_constraint(x, pltpu.HBM) if k in apart else x
+        for k, x in enumerate(args)
+    ]
     spaces = [pltpu.HBM if k in apart else pltpu.VMEM for k in range(len(args))]
     return pl.pallas_call(
         body,
-        out_shape=shapes,
+        out_shape=tuple(shapes),
         in_specs=[pl.BlockSpec(memory_space=space) for space in spaces],
-        out_specs=tuple(pl.BlockSpec(memory_space=pltpu.VMEM) for _ in shapes),
+        out_specs=tuple(specs),
         scratch_shapes=list(scratch),
         cost_estimate=pl.CostEstimate(flops=flops, bytes_accessed=size, transcendentals=0),
         compiler_params=pltpu.CompilerParams(vmem_limit_bytes=limit * MIB),
@@ -124,7 +138,7 @@
 
 
 def order(core, chip):
-    row = lax.broadcasted_iota(jnp.int32, (1, A_PAD), 1)
+    row = lax.broadcasted_iota(jnp.int32, (A, 1), 0)
     part = (row >= 192).astype(jnp.int32) + (row >= 384).astype(jnp.int32)
     rest = row - 192 * part
     first = (rest * 171) >> 12
@@ -142,7 +156,7 @@
         place.append(2 * far + (near ^ far))
     x, y, z = place
     device = x * 32 + (y >> 1) * 16 + core * 8 + (y & 1) * 4 + z
-    return jnp.where(row < A, 9 * device + piece, -1)
+    return 9 * device + piece
 
 
 def position():
@@ -151,33 +165,32 @@
 
 
 def picker(core, chip):
-    feature = lax.broadcasted_iota(jnp.int32, (D, A_PAD), 0)
+    feature = lax.broadcasted_iota(jnp.int32, (A, D), 1)
     return (feature == order(core, chip)).astype(F32).astype(BF)
 
 
-def pickers():
-    core, chip = position()
-    return picker(core, chip), picker(1 - core, chip)
-
-
-def forward_spatial(
-    latents, cot, mod, gains, w_qkv_any, w_out_any, w_out_t_any,
-    both, qkv_t, probs_t, normed, att, scaled_t, flat, tall, w_qkv, w_out, w_out_t, sems
-):
+def pick(hot, source):
+    return dot(hot, source, 1, 1).astype(BF)
+
+
+def forward_spatial(*refs):
+    sources, refs = refs[:7], refs[7:]
+    latents, cot, mod, gains, w_qkv, w_out_t, w_out = refs[:7]
+    both_far, both_mid, qkv_t, probs_t, normed, att, scaled_t, flat, tall, both, sems, out_sem = refs[7:]
     loads = [
         pltpu.make_async_copy(source, target, sems.at[k])
-        for k, (source, target) in enumerate(
-            ((w_qkv_any, w_qkv), (w_out_t_any, w_out_t), (w_out_any, w_out))
-        )
+        for k, (source, target) in enumerate(zip(sources, refs[:7]))
     ]
     for load in loads:
         load.start()
+    for load in loads[:4]:
+        load.wait()
     unit, _ = normalized(latents[...].astype(F32))
     norm = (unit * (1.0 + mod[1, 0:1, :]) + mod[0, 0:1, :]).astype(BF)
     normed[...] = norm
     scaled = (mod[2, 1:2, :] * cot[...].astype(F32)).astype(BF)
     scaled_t[...] = scaled
-    loads[0].wait()
+    loads[4].wait()
     qkv_t[...] = dot(w_qkv[...], norm, 1, 1).astype(BF).astype(F32)
     tall[A:, :] = jnp.zeros((A_PAD - A, T), F32)
     pair = gain_columns(gains, 0)
@@ -190,15 +203,21 @@
         tall[head_rows(0, h), :] = dot(values, probs.astype(BF), 1, 0)
     flip_back(tall, flat, A_PAD // 128)
     att[...] = flat[...].astype(BF)
-    loads[1].wait()
+    loads[5].wait()
     both[:, D:] = dot(scaled, w_out_t[...], 1, 1).astype(BF)
-    loads[2].wait()
+    loads[6].wait()
     result = dot(att[:, :A], w_out[...], 1, 0)
-    both[:, :D] = (latents[...].astype(F32) + mod[2, 0:1, :] * result).astype(BF)
+    mid = (latents[...].astype(F32) + mod[2, 0:1, :] * result).astype(BF)
+    both_mid[...] = mid
+    both[:, :D] = mid
+    send = pltpu.make_async_copy(both, both_far, out_sem)
+    send.start()
+    send.wait()
 
 
 def temporal(
-    both, mod, gains, w_qkv, back, normed, qkv_grad, tall_qkv, tall_grad, wide, flat, tall, tall_att
+    both, mod, gains, w_qkv, back_far, normed, qkv_grad,
+    tall_qkv, tall_grad, wide, flat, tall, tall_att, back, out_sem
 ):
     unit, _ = normalized(both[:, :D].astype(F32))
     norm = (unit * (1.0 + mod[1, 1:2, :]) + mod[0, 1:2, :]).astype(BF)
@@ -225,36 +244,40 @@
     flip_back(tall_grad, wide, Q_PAD // 128)
     qkv_grad[...] = wide[...].astype(BF)
     back[:, :D] = dot(qkv_grad[:, :Q], w_qkv[...], 1, 0).astype(BF)
-
-
-def pick_early(normed, scaled, att, mine, theirs):
-    own, other = pickers()
+    send = pltpu.make_async_copy(back, back_far, out_sem)
+    send.start()
+    send.wait()
+
+
+def pick_early(normed, scaled, w_far, own, other, mine, theirs, w_qkv, sem):
+    load = pltpu.make_async_copy(w_far, w_qkv, sem)
+    load.start()
+    core, chip = position()
+    own[...] = picker(core, chip)
+    other[...] = picker(1 - core, chip)
     for k, source in enumerate((normed, scaled)):
-        columns = slice(k * A_PAD, k * A_PAD + A_PAD)
-        theirs[:, columns] = dot(source[...], other, 1, 0).astype(BF)
-        mine[:, columns] = dot(source[...], own, 1, 0).astype(BF)
-    theirs[:, 2 * A_PAD :] = att[...]
-
-
-def pick_temporal(source, mine, theirs):
-    own, other = pickers()
-    mine[...] = dot(source[...], own, 1, 0).astype(BF)
-    theirs[...] = dot(source[...], other, 1, 0).astype(BF)
-
-
-def enter_spatial_back(back, both, cot, mod, w_out, mid_grad, att_grad, mine, theirs):
-    unit, spread = normalized(both[:, :D].astype(F32))
+        rows = slice(k * A, k * A + A)
+        theirs[rows, :] = pick(other[...], source[...])
+        mine[rows, :] = pick(own[...], source[...])
+    load.wait()
+
+
+def pick_later(source, own, other, mine, theirs):
+    theirs[...] = pick(other[...], source[...])
+    mine[...] = pick(own[...], source[...])
+
+
+def enter_spatial_back(back, mid, cot, mod, w_out, mid_grad, scaled_s, att_grad, att_t):
+    unit, spread = normalized(mid[...].astype(F32))
     grad = normalized_back(unit, spread, mod[1, 1:2, :], back[:, :D].astype(F32))
     total = (cot[...].astype(F32) + grad).astype(BF)
     mid_grad[...] = total
     scaled = (mod[2, 0:1, :] * total.astype(F32)).astype(BF)
+    scaled_s[...] = scaled
     att_grad[:, A:] = jnp.zeros((T, A_PAD - A), F32)
     att_grad[:, :A] = dot(scaled, w_out[...], 1, 1).astype(BF).astype(F32)
-    own, other = pickers()
-    mine[...] = dot(scaled, own, 1, 0).astype(BF)
-    theirs[:, :A_PAD] = dot(scaled, other, 1, 0).astype(BF)
-    theirs[:, A_PAD + A :] = jnp.zeros((T, A_PAD - A), BF)
-    theirs[:, A_PAD : A_PAD + A] = back[:, D:]
+    att_t[:, A:] = jnp.zeros((T, A_PAD - A), BF)
+    att_t[:, :A] = back[:, D:]
 
 
 def spatial_attention_back(att_grad, qkv_t, probs_t, gains, qkv_grad, tall_grad, wide, tall):
@@ -279,29 +302,32 @@
     latents_grad[...] = (mid_grad[...].astype(F32) + grad).astype(BF)
 
 
-def project_output(both, back, mod, w_out, output):
-    result = dot(back[:, D:], w_out[...], 1, 0)
-    output[...] = (both[:, :D].astype(F32) + mod[2, 1:2, :] * result).astype(BF)
+def project_output(mid, att_t, mod, w_out, output):
+    result = dot(att_t[:, :A], w_out[...], 1, 0)
+    output[...] = (mid[...].astype(F32) + mod[2, 1:2, :] * result).astype(BF)
 
 
 def weight_rows(groups):
     def body(*refs):
         keep, sends = refs[-4], refs[-3:]
         start = 0
-        for left, left_in, right, right_in, width in groups:
-            total = None
-            for (l_ref, l_at), (r_ref, r_at) in ((left, right), (left_in, right_in)):
-                more = dot(
-                    refs[l_ref][:, l_at : l_at + A], refs[r_ref][:, r_at : r_at + width], 0, 0
-                )
-                total = more if total is None else total + more
+        for (left, left_in, row), (right, right_in, column), width in groups:
+            lefts = [refs[k][row : row + A, :] for k in (left, left_in)]
+            rights = [refs[k][:, column : column + width] for k in (right, right_in)]
+            tall_left = jnp.concatenate(lefts, axis=1)
+            tall_right = jnp.concatenate(rights, axis=0)
             padded = -(-width // 128) * 128
-            for p in range(3):
-                rows = total[192 * p : 192 * p + 192]
-                keep[p, :, start : start + width] = rows[:96]
-                sends[p][:, start : start + width] = rows[96:].astype(BF)
-                if padded > width:
-                    gap = slice(start + width, start + padded)
+            for at in range(0, width, 576):
+                size = min(576, width - at)
+                total = dot(tall_left, tall_right[:, at : at + size], 1, 0)
+                for p in range(3):
+                    rows = total[192 * p : 192 * p + 192]
+                    columns = slice(start + at, start + at + size)
+                    keep[p, :, columns] = rows[:96]
+                    sends[p][:, columns] = rows[96:].astype(BF)
+            if padded > width:
+                gap = slice(start + width, start + padded)
+                for p in range(3):
                     keep[p, :, gap] = jnp.zeros((96, padded - width), F32)
                     sends[p][:, gap] = jnp.zeros((96, padded - width), BF)
             start += padded
@@ -314,7 +340,7 @@
         kept, send = refs[-2:]
         half = kept.shape[0]
         start = 0
-        for keep, got in ((refs[0], refs[1]), (refs[2], refs[3])):
+        for keep, got in zip(refs[0:6:2], refs[1:6:2]):
             width = got.shape[1]
             total = keep[p] + got[...].astype(F32)
             kept[:, start : start + width] = total[:half]
@@ -391,95 +417,95 @@
 def shards(
     latents, cotangent, modulation, qk_gains, spatial_qkv, spatial_out, temporal_qkv, temporal_out
 ):
-    x, cot = latents.reshape(T, D), cotangent.reshape(T, D)
-    mod = modulation[0].transpose(1, 0, 2)
-    w_qkv_s, w_qkv_t = spatial_qkv.T, temporal_qkv.T
     wide, tall_grad = pltpu.VMEM((T, Q_PAD), F32), pltpu.VMEM((Q_PAD, T), F32)
     flat, tall = pltpu.VMEM((T, A_PAD), F32), pltpu.VMEM((A_PAD, T), F32)
-
-    both, qkv_t, probs_t, normed_s, att_s, scaled_t = call(
+    stage, signal = pltpu.VMEM((T, D + A), BF), pltpu.SemaphoreType.DMA(())
+    one_block, pick_flops = ((A, T), BF), 2 * T * D * A
+
+    x, cot, mod, gains, w_qkv_s, w_out_t, w_out_s, both, mid, qkv_t, probs_t, normed_s, att_s, scaled_t = call(
         forward_spatial,
         [
-            ((T, D + A), BF), ((Q, T), F32), ((HEADS, T, T), F32),
+            ((T, D), BF), ((T, D), BF), ((3, 2, D), F32), ((2, 2, HEAD_DIM), F32),
+            ((Q, D), BF), ((A, D), BF), ((A, D), BF),
+            ((T, D + A), BF, "hbm"), ((T, D), BF), ((Q, T), F32), ((HEADS, T, T), F32),
             ((T, D), BF), ((T, A_PAD), BF), ((T, D), BF),
         ],
-        (x, cot, mod, qk_gains, w_qkv_s, spatial_out, temporal_out),
+        (
+            latents.reshape(T, D), cotangent.reshape(T, D), modulation[0].transpose(1, 0, 2), qk_gains,
+            spatial_qkv.T, temporal_out, spatial_out,
+        ),
         2 * T * D * (Q + 2 * A),
-        (
-            flat, tall, pltpu.VMEM((Q, D), BF), pltpu.VMEM((A, D), BF), pltpu.VMEM((A, D), BF),
-            pltpu.SemaphoreType.DMA((3,)),
-        ),
-        apart=(4, 5, 6),
+        (flat, tall, stage, pltpu.SemaphoreType.DMA((7,)), signal),
+        limit=18,
+        apart=range(7),
     )
     patch = lax.all_to_all(both.reshape(8, LOCAL, D + A), "seq", 0, 0, tiled=True)
-    early_mine, early_theirs = call(
+    att_s_in = to_other_core(att_s)
+    own, other, early_mine, early_theirs, w_qkv_t = call(
         pick_early,
-        [((T, 2 * A_PAD), BF), ((T, 3 * A_PAD), BF)],
-        (normed_s, scaled_t, att_s),
-        4 * T * D * D,
+        [((A, D), BF), ((A, D), BF), ((2 * A, T), BF), ((2 * A, T), BF), ((Q, D), BF)],
+        (normed_s, scaled_t, temporal_qkv.T),
+        4 * pick_flops,
+        (signal,),
+        apart=(2,),
     )
     patch, early_mine, early_theirs = in_order(patch, early_mine, early_theirs)
     early_in = to_other_core(early_theirs)
 
     back_patch, normed_t, qkv_grad_t = call(
         temporal,
-        [((T, D + A), BF), ((T, D), BF), ((T, Q_PAD), BF)],
-        (patch.reshape(T, D + A), mod, qk_gains, w_qkv_t),
+        [((T, D + A), BF, "hbm"), ((T, D), BF), ((T, Q_PAD), BF)],
+        (patch.reshape(T, D + A), mod, gains, w_qkv_t),
         4 * T * D * Q,
-        (pltpu.VMEM((Q, T), F32), tall_grad, wide, flat, tall, tall),
+        (pltpu.VMEM((Q, T), F32), tall_grad, wide, flat, tall, tall, stage, signal),
+        limit=20,
     )
     back = lax.all_to_all(back_patch.reshape(8, LOCAL, D + A), "seq", 0, 0, tiled=True)
     back = back.reshape(T, D + A)
     qkv_grad_t_in = to_other_core(qkv_grad_t)
-    t_mine, t_theirs = call(
-        pick_temporal, [((T, A_PAD), BF), ((T, A_PAD), BF)], (normed_t,), 4 * T * D * A
-    )
+    t_mine, t_theirs = call(pick_later, [one_block] * 2, (normed_t, own, other), 2 * pick_flops)
     t_in = to_other_core(t_theirs)
-    back, t_in, qkv_grad_t_in = in_order(back, t_in, qkv_grad_t_in)
-
-    mid_grad, att_grad_s, late_mine, late_theirs = call(
+    keep_t, sends_t = weight_partials(
+        (((0, 1, 0), (2, 3, 0), Q),), (t_mine, t_in, qkv_grad_t, qkv_grad_t_in)
+    )
+    back, *sends_t = in_order(back, *sends_t)
+    got_t = [along(sends_t[p], p, False) for p in range(3)]
+
+    mid_grad, scaled_s, att_grad_s, att_t = call(
         enter_spatial_back,
-        [((T, D), BF), ((T, A_PAD), F32), ((T, A_PAD), BF), ((T, 2 * A_PAD), BF)],
-        (back, both, cot, mod, spatial_out),
-        6 * T * D * A,
-    )
-    late_in = to_other_core(late_theirs)
+        [((T, D), BF), ((T, D), BF), ((T, A_PAD), F32), ((T, A_PAD), BF)],
+        (back, mid, cot, mod, w_out_s),
+        2 * T * D * A,
+    )
+    att_t_in = to_other_core(att_t)
     (qkv_grad_s,) = call(
         spatial_attention_back,
         [((T, Q_PAD), BF)],
-        (att_grad_s, qkv_t, probs_t, qk_gains),
+        (att_grad_s, qkv_t, probs_t, gains),
         2 * T * T * HEADS * 128 * 5,
         (tall_grad, wide, tall),
     )
     qkv_grad_s_in = to_other_core(qkv_grad_s)
-    keep_a, sends_a = weight_partials(
-        (
-            ((0, 0), (1, 0), (2, 0), (3, 0), Q),
-            ((4, A_PAD), (5, A_PAD), (6, D), (7, A_PAD), A),
-            ((8, 0), (7, 0), (9, 0), (5, 2 * A_PAD), A),
-        ),
-        (
-            t_mine, t_in, qkv_grad_t, qkv_grad_t_in, early_mine, early_in, back, late_in, late_mine,
-            att_s,
-        ),
-    )
-    got_a = [along(sends_a[p], p, False) for p in range(3)]
+    qkv_grad_s, scaled_s = in_order(qkv_grad_s, scaled_s)
+    late_mine, late_theirs = call(
+        pick_later, [one_block] * 2, (scaled_s, own, other), 2 * pick_flops
+    )
+    late_in = to_other_core(late_theirs)
     keep_b, sends_b = weight_partials(
-        (((0, 0), (1, 0), (2, 0), (3, 0), Q),),
-        (early_mine, early_in, qkv_grad_s, qkv_grad_s_in),
-    )
-    keep_b, *sends_b, mid_grad, back = in_order(keep_b, *sends_b, mid_grad, back)
+        (((0, 1, 0), (2, 3, 0), Q),), (early_mine, early_in, qkv_grad_s, qkv_grad_s_in)
+    )
+    keep_b, late_in, att_t, *sends_b = in_order(keep_b, late_in, att_t, *sends_b)
     got_b = [along(sends_b[p], p, False) for p in range(3)]
-    (latents_grad,) = call(
-        leave_spatial_back,
-        [((T, D), BF)],
-        (mid_grad, qkv_grad_s, x, mod, w_qkv_s),
-        2 * T * D * Q,
-    )
+    keep_o, sends_o = weight_partials(
+        (((0, 1, A), (2, 3, 0), A), ((4, 5, 0), (6, 7, 0), A)),
+        (early_mine, early_in, att_t, att_t_in, late_mine, late_in, att_s, att_s_in),
+    )
+    keep_o, att_t, *sends_o = in_order(keep_o, att_t, *sends_o)
+    got_o = [along(sends_o[p], p, False) for p in range(3)]
     (output,) = call(
-        project_output, [((T, D), BF)], (both, back, mod, temporal_out), 2 * T * D * A
-    )
-    keep_b, latents_grad, output = in_order(keep_b, latents_grad, output)
+        project_output, [((T, D), BF, "any")], (mid, att_t, mod, w_out_t), 2 * T * D * A
+    )
+    keep_b, output = in_order(keep_b, output)
 
     columns = 2 * Q_PAD + 2 * A_PAD
     kept, got = [], []
@@ -487,11 +513,19 @@
         mine, send = call(
             first_halve(p),
             [((48, columns), F32), ((48, columns), BF)],
-            (keep_a, got_a[p], keep_b, got_b[p]),
+            (keep_t, got_t[p], keep_o, got_o[p], keep_b, got_b[p]),
             96 * columns,
         )
         kept.append(mine)
         got.append(along(send, (p + 1) % 3, False))
+    mid_grad, kept[2] = in_order(mid_grad, kept[2])
+    (latents_grad,) = call(
+        leave_spatial_back,
+        [((T, D), BF, "any")],
+        (mid_grad, qkv_grad_s, x, mod, w_qkv_s),
+        2 * T * D * Q,
+    )
+    kept[0], latents_grad = in_order(kept[0], latents_grad)
     for p in range(3):
         kept[p], send = call(
             add_halve, [((24, columns), F32), ((24, columns), BF)], (kept[p], got[p]), 48 * columns
@@ -514,7 +548,7 @@
     got = along(send, 2, True)
     tq, to, so, sq = call(
         last_add,
-        [((9, Q), F32), ((9, A), F32), ((9, A), F32), ((9, Q), F32)],
+        [((9, Q), F32, "any"), ((9, A), F32, "any"), ((9, A), F32, "any"), ((9, Q), F32, "any")],
         (kept, got),
         9 * columns,
     )

time: 145 us -> 153 us (1.055)
  local copies, waits for them, and re-layouts: 18 us -> 24.5 us
  waiting for transfers between devices: 48.6 us -> 46.5 us
  starting transfers between devices: 32.6 us -> 34.4 us
  Pallas kernels: 43.9 us -> 45.6 us
    unnamed x52 -> x70, local copies, waits for them, and re-layouts: 18 us -> 24.5 us
    ppermute x15 -> x18, waiting for transfers between devices: 27.9 us -> 31.9 us  [along(): return lax.ppermute(value, MESH, pairs(change))]
    all_to_all x1, waiting for transfers between devices: 10 us -> 6.12 us  [shards(): lax.all_to_all(both.reshape(8, LOCAL, D + A), 'seq', 0, 0, tiled=True)]
    all_to_all x1, waiting for transfers between devices: 9.47 us -> 6.14 us  [shards(): lax.all_to_all(back_patch.reshape(8, LOCAL, D + A), 'seq', 0, 0, tiled=True)]
    pallas_call x20 -> x22, Pallas kernels: 43.9 us -> 45.6 us  [call(): pl.pallas_call(body, out_shape=tuple(shapes), in_specs=[pl.BlockSpec(memo...]
    ppermute x15 -> x18, starting transfers between devices: 21.2 us -> 21.6 us  [along(): return lax.ppermute(value, MESH, pairs(change))]
  transfers between devices with their start and end apart: 22 -> 27, of which waited for: 12 -> 13; matrix products, arithmetic and copies ran while one was open for 0% -> 0% of each run, Pallas kernels for 16% -> 10%
where the time goes in v3:
time: 153 us; the launch traced here: 152 us
  waiting for transfers between devices  46.5 us (30%)
  Pallas kernels  45.6 us (30%)
  starting transfers between devices  34.4 us (22%)
  local copies, waits for them, and re-layouts  24.5 us (16%)
    pallas_call x22, Pallas kernels, call(): pl.pallas_call(body, out_shape=tuple(shapes), in_specs=[pl.BlockSpec(memo...  45.6 us
    ppermute x18, waiting for transfers between devices, along(): return lax.ppermute(value, MESH, pairs(change))  31.9 us
    unnamed x70, local copies, waits for them, and re-layouts  24.5 us
    ppermute x18, starting transfers between devices, along(): return lax.ppermute(value, MESH, pairs(change))  21.6 us
    all_to_all x1, starting transfers between devices, shards(): lax.all_to_all(both.reshape(8, LOCAL, D + A), 'seq', 0, 0, tiled=True)  6.41 us
    all_to_all x1, waiting for transfers between devices, shards(): lax.all_to_all(back_patch.reshape(8, LOCAL, D + A), 'seq', 0, 0, tiled=True)  6.14 us
    all_to_all x1, waiting for transfers between devices, shards(): lax.all_to_all(both.reshape(8, LOCAL, D + A), 'seq', 0, 0, tiled=True)  6.12 us
    all_to_all x1, starting transfers between devices, shards(): lax.all_to_all(back_patch.reshape(8, LOCAL, D + A), 'seq', 0, 0, tiled=True)  4.23 us
  transfers between devices with their start and end apart: 27, of which 13 were waited for; matrix products, arithmetic and copies ran while one was open for 0% of the time, Pallas kernels for 10%

profile of v3, /device:TPU:0, one launch (start us, length us, event | category | flops | bytes accessed | tf_op | source)
XLA Modules:
  0.0 152.0 jit_solution(4208016447283808361)
XLA Ops:
  0.6 10.7 %shard_map.127 = (bf16[256,1152]{1,0:T(8,128)(2,1)S(1)}, bf16[256,1152]{1,0:T(8,128)(2,1)S(1)}, f32[3,2,1152]{2,1,0:T(2,128)S(1)}, f32[2,2,72]{2,1,0:T(2,128)S(1...) custom-call(bf16[256,1152]{1,0:T(8,128)(2,1)} %bitcast.19, ...), custom_call_target="tpu_custom_call" | custom-call | flops 1698693120 | bytes 22536448 | tf_op jit(solution)/shard_map/pallas_call | solution.py:49
  11.4 1.9 %copy-done.2 = bf16[1728,1152]{1,0:T(8,128)(2,1)} copy-done((bf16[1728,1152]{1,0:T(8,128)(2,1)}, bf16[1728,1152]{1,0:T(8,128)(2,1)S(1)}, u32[]{:S(2)}) %copy-start.2) | copy-done | bytes 3981336
  13.3 0.8 copy-done.4
  14.1 1.3 copy-done.7
  15.4 1.3 copy-done.9
  16.7 1.1 copy-done.11
  17.8 1.1 copy-done.13
  18.8 0.8 copy-done.15
  19.6 0.8 copy-done.17
  20.5 0.8 copy-done.21
  22.0 6.4 %all-to-all-start = ((bf16[8,32,1728]{2,1,0:T(8,128)(2,1)}), bf16[8,32,1728]{2,1,0:T(8,128)(2,1)}, u32[]{:S(2)}, u32[]{:S(2)}) async-start(bf16[8,32,1728]{2,1,0:T(8,128)(2,1)} %bitcast.18), calls=%async_computation | async-start | bytes 1835008 | tf_op jit(solution)/shard_map/all_to_all | solution.py:442
  28.4 1.1 copy-done.16
  29.5 2.7 %shard_map.128 = (bf16[576,1152]{1,0:T(8,128)(2,1)S(1)}, bf16[576,1152]{1,0:T(8,128)(2,1)S(1)}, bf16[1152,256]{1,0:T(8,128)(2,1)S(1)}, bf16[1152,256]{1,0:T(8,128)(2,1)S(1)}, bf16[1728,1152]{1,0:T(8,128)(2,1)S(1)}) custom-call(bf16[256,1152]{1,0:T(8,128)(2,1)S(1)} %get-tuple-element.97.normed, bf16[256,1152]{1,0:T(8,128)(2,1)S(1)} %copy-done.16, ...), custom_call_target="tpu_custom_call" | custom-call | flops 1358954496 | bytes 12976128 | tf_op jit(solution)/shard_map/pallas_call | solution.py:49
  32.2 0.8 copy-done.19
  33.1 1.9 %copy-done.25 = bf16[1728,1152]{1,0:T(8,128)(2,1)} copy-done((bf16[1728,1152]{1,0:T(8,128)(2,1)}, bf16[1728,1152]{1,0:T(8,128)(2,1)S(1)}, u32[]{:S(2)}) %copy-start.25) | copy-done | bytes 3981336
  35.0 0.8 copy-done.27
  35.8 6.1 %all-to-all-done = bf16[8,32,1728]{2,1,0:T(8,128)(2,1)} async-done(((bf16[8,32,1728]{2,1,0:T(8,128)(2,1)}), bf16[8,32,1728]{2,1,0:T(8,128)(2,1)}, u32[]{:S(2)}, u32[]{:S(2)}) %all-to-all-start) | async-done | bytes 884768 | tf_op jit(solution)/shard_map/all_to_all | solution.py:442
  41.9 2.1 %copy-done.26 = bf16[1728,1152]{1,0:T(8,128)(2,1)S(1)} copy-done((bf16[1728,1152]{1,0:T(8,128)(2,1)S(1)}, bf16[1728,1152]{1,0:T(8,128)(2,1)}, u32[]{:S(2)}) %copy-start.26) | copy-done | bytes 3981336
  44.1 12.7 %shard_map.129 = (bf16[256,1728]{1,0:T(8,128)(2,1)}, bf16[256,1152]{1,0:T(8,128)(2,1)S(1)}, bf16[256,1792]{1,0:T(8,128)(2,1)}) custom-call(bf16[256,1728]{1,0:T(8,128)(2,1)} %bitcast.7.both, f32[3,2,1152]{2,1,0:T(2,128)S(1)} %get-tuple-element.104.mod, f32[2,2,72]{2,1,0:T(2,128)S(1)} %get-tuple-element.105.gains, bf16[1728,1152]{1,0:T(8,128)(2,1)S(1)} %copy-done.26), custom_call_target="tpu_custom_call" | custom-call | flops 2038431744 | bytes 7286912 | tf_op jit(solution)/shard_map/pallas_call | solution.py:49
  56.9 4.2 %all-to-all-start.1 = ((bf16[8,32,1728]{2,1,0:T(8,128)(2,1)}), bf16[8,32,1728]{2,1,0:T(8,128)(2,1)}, u32[]{:S(2)}, u32[]{:S(2)}) async-start(bf16[8,32,1728]{2,1,0:T(8,128)(2,1)} %bitcast.17), calls=%async_computation.1 | async-start | bytes 1835008 | tf_op jit(solution)/shard_map/all_to_all | solution.py:463
  61.1 1.0 shard_map.130
  62.1 0.8 collective-permute-start.1
  62.9 1.2 collective-permute-done.1.refs_1_
  64.1 3.0 %shard_map.131 = (f32[3,96,1792]{2,1,0:T(8,128)S(1)}, bf16[96,1792]{1,0:T(8,128)(2,1)S(1)}, bf16[96,1792]{1,0:T(8,128)(2,1)S(1)}, bf16[96,1792]{1,0:T(8,128)(2,1)S(1)}) custom-call(bf16[576,256]{1,0:T(8,128)(2,1)S(1)} %get-tuple-element.111.refs_0_, bf16[576,256]{1,0:T(8,128)(2,1)S(1)} %collective-permute-done.1.refs_1_, ...), custom_call_target="tpu_custom_call" | custom-call | flops 1056964608 | bytes 5521408 | tf_op jit(solution)/shard_map/pallas_call | solution.py:49
  67.1 0.7 copy-done.29
  67.8 0.7 copy-done.31
  68.6 0.7 copy-done.33
  69.3 6.1 %all-to-all-done.1 = bf16[8,32,1728]{2,1,0:T(8,128)(2,1)} async-done(((bf16[8,32,1728]{2,1,0:T(8,128)(2,1)}), bf16[8,32,1728]{2,1,0:T(8,128)(2,1)}, u32[]{:S(2)}, u32[]{:S(2)}) %all-to-all-start.1) | async-done | bytes 884768 | tf_op jit(solution)/shard_map/all_to_all | solution.py:463
  75.4 1.1 copy-done.5
  76.5 1.3 copy-done.14
  77.8 1.1 copy-done.22
  78.9 2.8 %shard_map.132 = (bf16[256,1152]{1,0:T(8,128)(2,1)S(1)}, bf16[256,1152]{1,0:T(8,128)(2,1)S(1)}, f32[256,640]{1,0:T(8,128)S(1)}, bf16[256,640]{1,0:T(8,128)(2,1)S(1)}) custom-call(bf16[256,1728]{1,0:T(8,128)(2,1)} %bitcast.9.back, bf16[256,1152]{1,0:T(8,128)(2,1)S(1)} %copy-done.5, bf16[256,1152]{1,0:T(8,128)(2,1)S(1)} %copy-done.22, ...), custom_call_target="tpu_custom_call" | custom-call | flops 339738624 | bytes 5581824 | tf_op jit(solution)/shard_map/pallas_call | solution.py:49
  81.7 1.5 copy-done.10
  83.1 2.9 %shard_map.133.refs_2_.qkv_grad = bf16[256,1792]{1,0:T(8,128)(2,1)S(1)} custom-call(f32[256,640]{1,0:T(8,128)S(1)} %get-tuple-element.121.att_grad, f32[1728,256]{1,0:T(8,128)S(1)} %copy-done.10, f32[8,256,256]{2,1,0:T(8,128)S(1)} %copy-done.8, f32[2,2,72]{2,1,0:T(2,128)S(1)} %get-tuple-element.105.gains), custom_call_target="tpu_custom_call" | custom-call | flops 671088640 | bytes 5440640 | tf_op jit(solution)/shard_map/pallas_call | solution.py:49
  87.2 1.0 shard_map.135
  88.3 1.1 collective-permute-done.refs_1_
  89.4 1.5 collective-permute-start.7
  90.9 1.5 collective-permute-start.14
  92.4 1.6 %shard_map.134 = (f32[3,96,1792]{2,1,0:T(8,128)S(1)}, bf16[96,1792]{1,0:T(8,128)(2,1)S(1)}, bf16[96,1792]{1,0:T(8,128)(2,1)S(1)}, bf16[96,1792]{1,0:T(8,128)(2,1)S(1)}) custom-call(bf16[1152,256]{1,0:T(8,128)(2,1)S(1)} %copy-done.20, bf16[1152,256]{1,0:T(8,128)(2,1)S(1)} %collective-permute-done.refs_1_, bf16[256,1792]{1,0:T(8,128)(2,1)S(1)} %shard_map.133.refs_2_.qkv_grad, ...), custom_call_target="tpu_custom_call" | custom-call | flops 1056964608 | bytes 6111232 | tf_op jit(solution)/shard_map/pallas_call | solution.py:49
  94.7 1.1 shard_map.136
  95.8 1.6 %collective-permute-start.8 = (bf16[96,1280]{1,0:T(8,128)(2,1)S(1)}, bf16[96,1280]{1,0:T(8,128)(2,1)S(1)}, u32[]{:S(2)}, u32[]{:S(2)}) collective-permute-start(bf16[96,1280]{1,0:T(8,128)(2,1)S(1)} %get-tuple-element.148), channel_id=1, source_target_pairs={{0,32},{1,33},{2,34},{3,35},{4,36},{5,37},{6,38},{7,39},{8,104},{9... | collective-permute-start | bytes 737288 | tf_op jit(solution)/shard_map/ppermute | solution.py:407
  97.9 0.9 collective-permute-start.10
  98.7 1.2 collective-permute-start.12
  99.9 4.1 %collective-permute-done.8.refs_3_ = bf16[96,1280]{1,0:T(8,128)(2,1)S(1)} collective-permute-done((bf16[96,1280]{1,0:T(8,128)(2,1)S(1)}, bf16[96,1280]{1,0:T(8,128)(2,1)S(1)}, u32[]{:S(2)}, u32[]{:S(2)}) %collective-permute-start.8) | collective-permute-done | bytes 245792 | tf_op jit(solution)/shard_map/ppermute | solution.py:407
  104.5 0.9 collective-permute-start.11
  105.4 1.5 shard_map.137
  107.1 3.1 %collective-permute-done.15.refs_3_ = bf16[96,1280]{1,0:T(8,128)(2,1)S(1)} collective-permute-done((bf16[96,1280]{1,0:T(8,128)(2,1)S(1)}, bf16[96,1280]{1,0:T(8,128)(2,1)S(1)}, u32[]{:S(2)}, u32[]{:S(2)}) %collective-permute-start.15) | collective-permute-done | bytes 245792 | tf_op jit(solution)/shard_map/ppermute | solution.py:407
  111.0 0.9 collective-permute-start.17
  112.1 1.5 collective-permute-start.18
  113.6 2.7 %shard_map.140 = bf16[256,1152]{1,0:T(8,128)(2,1)} custom-call(bf16[256,1152]{1,0:T(8,128)(2,1)S(1)} %get-tuple-element.157.mid_grad, bf16[256,1792]{1,0:T(8,128)(2,1)S(1)} %shard_map.133.refs_2_.qkv_grad, bf16[256,1152]{1,0:T(8,128)(2,1)S(1)} %copy-done.18, f32[3,2,1152]{2,1,0:T(2,128)S(1)} %get-tuple-element.104.mod, bf16[1728,1152]{1,0:T(8,128)(2,1)S(1)} %copy-done.3), custom_call_target="tpu_custom_call" | custom-call | flops 1019215872 | bytes 6695936 | tf_op jit(solution)/shard_map/pallas_call | solution.py:49
  116.3 2.4 %collective-permute-done.13.got = bf16[48,4864]{1,0:T(8,128)(2,1)S(1)} collective-permute-done((bf16[48,4864]{1,0:T(8,128)(2,1)S(1)}, bf16[48,4864]{1,0:T(8,128)(2,1)S(1)}, u32[]{:S(2)}, u32[]{:S(2)}) %collective-permute-start.13) | collective-permute-done | bytes 466976 | tf_op jit(solution)/shard_map/ppermute | solution.py:407
  118.9 0.9 collective-permute-start.19
  119.9 1.3 collective-permute-start.20
  121.4 1.0 collective-permute-start.21
  122.4 2.6 %collective-permute-done.19.refs_3_ = bf16[24,4864]{1,0:T(8,128)(2,1)S(1)} collective-permute-done((bf16[24,4864]{1,0:T(8,128)(2,1)S(1)}, bf16[24,4864]{1,0:T(8,128)(2,1)S(1)}, u32[]{:S(2)}, u32[]{:S(2)}) %collective-permute-start.19) | collective-permute-done | bytes 233504 | tf_op jit(solution)/shard_map/ppermute | solution.py:407
  125.0 1.0 collective-permute-done.20.refs_4_
  126.0 1.5 collective-permute-done.21.refs_5_
  127.7 2.3 %collective-permute-start.22 = (bf16[3,12,4864]{2,1,0:T(8,128)(2,1)S(1)}, bf16[3,12,4864]{2,1,0:T(8,128)(2,1)S(1)}, u32[]{:S(2)}, u32[]{:S(2)}) collective-permute-start(bf16[3,12,4864]{2,1,0:T(8,128)(2,1)S(1)} %get-tuple-element.177), channel_id=1, source_target_pairs={{0,96},{1,97},{2,98},{3,99},{4,100},{5,101},{6,102},{7,103},{8,40}... | collective-permute-start | bytes 1050632 | tf_op jit(solution)/shard_map/ppermute | solution.py:407
  130.0 7.6 %collective-permute-done.22.got = bf16[3,12,4864]{2,1,0:T(8,128)(2,1)S(1)} collective-permute-done((bf16[3,12,4864]{2,1,0:T(8,128)(2,1)S(1)}, bf16[3,12,4864]{2,1,0:T(8,128)(2,1)S(1)}, u32[]{:S(2)}, u32[]{:S(2)}) %collective-permute-start.22) | collective-permute-done | bytes 350240 | tf_op jit(solution)/shard_map/ppermute | solution.py:407
  137.7 2.5 %collective-permute-start.23 = (bf16[3,6,4864]{2,1,0:T(8,128)(2,1)S(1)}, bf16[3,6,4864]{2,1,0:T(8,128)(2,1)S(1)}, u32[]{:S(2)}, u32[]{:S(2)}) collective-permute-start(bf16[3,6,4864]{2,1,0:T(8,128)(2,1)S(1)} %get-tuple-element.179), channel_id=1, source_target_pairs={{0,20},{1,21},{2,22},{3,23},{4,16},{5,17},{6,18},{7,19},{8,12},{9,... | collective-permute-start | bytes 525320 | tf_op jit(solution)/shard_map/ppermute | solution.py:407
  140.2 4.9 %collective-permute-done.23.got = bf16[3,6,4864]{2,1,0:T(8,128)(2,1)S(1)} collective-permute-done((bf16[3,6,4864]{2,1,0:T(8,128)(2,1)S(1)}, bf16[3,6,4864]{2,1,0:T(8,128)(2,1)S(1)}, u32[]{:S(2)}, u32[]{:S(2)}) %collective-permute-start.23) | collective-permute-done | bytes 175136 | tf_op jit(solution)/shard_map/ppermute | solution.py:407
  145.2 1.5 collective-permute-start.24
  146.7 4.6 %collective-permute-done.24.got = bf16[3,3,4864]{2,1,0:T(4,128)(2,1)S(1)} collective-permute-done((bf16[3,3,4864]{2,1,0:T(4,128)(2,1)S(1)}, bf16[3,3,4864]{2,1,0:T(4,128)(2,1)S(1)}, u32[]{:S(2)}, u32[]{:S(2)}) %collective-permute-start.24) | collective-permute-done | bytes 87584 | tf_op jit(solution)/shard_map/ppermute | solution.py:407
  151.3 0.7 shard_map.148
  (82 shorter events, 5.7 us)
Async XLA Ops:
  11.4 1.9 %copy-start.2 = (bf16[1728,1152]{1,0:T(8,128)(2,1)}, bf16[1728,1152]{1,0:T(8,128)(2,1)S(1)}, u32[]{:S(2)}) copy-start(bf16[1728,1152]{1,0:T(8,128)(2,1)S(1)} %get-tuple-element.159.w_qkv) | copy-start | bytes 11943940
  13.3 0.8 copy-start.4
  14.1 1.3 copy-start.7
  15.4 1.3 copy-start.9
  16.7 1.1 copy-start.11
  17.8 1.1 copy-start.13
  18.8 0.8 copy-start.15
  19.6 0.8 copy-start.17
  20.5 0.8 copy-start.21
  21.3 0.7 copy-start.23
  22.0 19.9 %all-to-all-start = ((bf16[8,32,1728]{2,1,0:T(8,128)(2,1)}), bf16[8,32,1728]{2,1,0:T(8,128)(2,1)}, u32[]{:S(2)}, u32[]{:S(2)}) async-start(bf16[8,32,1728]{2,1,0:T(8,128)(2,1)} %bitcast.18), calls=%async_computation | async-start | bytes 1835008 | tf_op jit(solution)/shard_map/all_to_all | solution.py:442
  28.4 1.1 copy-start.16
  32.2 0.8 copy-start.19
  33.1 1.9 %copy-start.25 = (bf16[1728,1152]{1,0:T(8,128)(2,1)}, bf16[1728,1152]{1,0:T(8,128)(2,1)S(1)}, u32[]{:S(2)}) copy-start(bf16[1728,1152]{1,0:T(8,128)(2,1)S(1)} %get-tuple-element.106.w_qkv) | copy-start | bytes 11943940
  35.0 0.8 copy-start.27
  35.8 25.3 %copy-start = (bf16[576,1152]{1,0:T(8,128)(2,1)}, bf16[576,1152]{1,0:T(8,128)(2,1)S(1)}, u32[]{:S(2)}) copy-start(bf16[576,1152]{1,0:T(8,128)(2,1)S(1)} %get-tuple-element.110.other) | copy-start | bytes 3981316
  41.9 2.1 %copy-start.26 = (bf16[1728,1152]{1,0:T(8,128)(2,1)S(1)}, bf16[1728,1152]{1,0:T(8,128)(2,1)}, u32[]{:S(2)}) copy-start(bf16[1728,1152]{1,0:T(8,128)(2,1)} %copy-done.25) | copy-start | bytes 11943940
  56.8 7.3 %collective-permute-start.2 = (bf16[256,1792]{1,0:T(8,128)(2,1)}, bf16[256,1792]{1,0:T(8,128)(2,1)}, u32[]{:S(2)}, u32[]{:S(2)}) collective-permute-start(bf16[256,1792]{1,0:T(8,128)(2,1)} %get-tuple-element.113.refs_2_), channel_id=1, source_target_pairs={{0,8},{1,9},{2,10},{3,11},{4,12},{5,13},{6,14},{7,15},{8,0},{9,1},... | collective-permute-start | bytes 2752520 | tf_op jit(solution)/shard_map/ppermute | solution.py:398
  56.9 18.6 %all-to-all-start.1 = ((bf16[8,32,1728]{2,1,0:T(8,128)(2,1)}), bf16[8,32,1728]{2,1,0:T(8,128)(2,1)}, u32[]{:S(2)}, u32[]{:S(2)}) async-start(bf16[8,32,1728]{2,1,0:T(8,128)(2,1)} %bitcast.17), calls=%async_computation.1 | async-start | bytes 1835008 | tf_op jit(solution)/shard_map/all_to_all | solution.py:463
  62.1 2.0 %collective-permute-start.1 = (bf16[576,256]{1,0:T(8,128)(2,1)S(1)}, bf16[576,256]{1,0:T(8,128)(2,1)S(1)}, u32[]{:S(2)}, u32[]{:S(2)}) collective-permute-start(bf16[576,256]{1,0:T(8,128)(2,1)S(1)} %get-tuple-element.112), channel_id=1, source_target_pairs={{0,8},{1,9},{2,10},{3,11},{4,12},{5,13},{6,14},{7,15},{8,0},{9,1},... | collective-permute-start | bytes 884744 | tf_op jit(solution)/shard_map/ppermute | solution.py:398
  67.1 0.7 copy-start.29
  67.8 0.7 copy-start.31
  68.6 0.7 copy-start.33
  75.4 1.1 copy-start.5
  76.5 1.3 copy-start.14
  77.8 1.1 copy-start.22
  78.9 2.8 %copy-start.8 = (f32[8,256,256]{2,1,0:T(8,128)S(1)}, f32[8,256,256]{2,1,0:T(8,128)}, u32[]{:S(2)}) copy-start(f32[8,256,256]{2,1,0:T(8,128)} %copy-done.7) | copy-start | bytes 6291460
  81.7 1.5 copy-start.10
  83.1 3.0 %copy-start.28 = (bf16[1152,256]{1,0:T(8,128)(2,1)S(1)}, bf16[1152,256]{1,0:T(8,128)(2,1)}, u32[]{:S(2)}) copy-start(bf16[1152,256]{1,0:T(8,128)(2,1)} %copy-done.27) | copy-start | bytes 1769476
  83.1 3.5 %copy-start.24 = (bf16[256,640]{1,0:T(8,128)(2,1)S(1)}, bf16[256,640]{1,0:T(8,128)(2,1)}, u32[]{:S(2)}) copy-start(bf16[256,640]{1,0:T(8,128)(2,1)} %copy-done.23) | copy-start | bytes 983044
  83.1 4.0 %copy-start.1 = (bf16[576,1152]{1,0:T(8,128)(2,1)S(1)}, bf16[576,1152]{1,0:T(8,128)(2,1)}, u32[]{:S(2)}) copy-start(bf16[576,1152]{1,0:T(8,128)(2,1)} %copy-done) | copy-start | bytes 3981316
  86.0 3.4 %copy-start.34 = (bf16[96,1792]{1,0:T(8,128)(2,1)S(1)}, bf16[96,1792]{1,0:T(8,128)(2,1)}, u32[]{:S(2)}) copy-start(bf16[96,1792]{1,0:T(8,128)(2,1)} %copy-done.33) | copy-start | bytes 1032196
  86.0 4.9 %copy-start.32 = (bf16[96,1792]{1,0:T(8,128)(2,1)S(1)}, bf16[96,1792]{1,0:T(8,128)(2,1)}, u32[]{:S(2)}) copy-start(bf16[96,1792]{1,0:T(8,128)(2,1)} %copy-done.31) | copy-start | bytes 1032196
  86.0 6.4 %copy-start.20 = (bf16[1152,256]{1,0:T(8,128)(2,1)S(1)}, bf16[1152,256]{1,0:T(8,128)(2,1)}, u32[]{:S(2)}) copy-start(bf16[1152,256]{1,0:T(8,128)(2,1)} %copy-done.19) | copy-start | bytes 1769476
  86.0 4.9 %collective-permute-start.3 = (bf16[256,1792]{1,0:T(8,128)(2,1)S(1)}, bf16[256,1792]{1,0:T(8,128)(2,1)S(1)}, u32[]{:S(2)}, u32[]{:S(2)}) collective-permute-start(bf16[256,1792]{1,0:T(8,128)(2,1)S(1)} %shard_map.133.refs_2_.qkv_grad), channel_id=1, source_target_pairs={{0,8},{1,9},{2,10},{3,11},{4,12},{5,13},{6,14},{7,15},{8,0},{9,1},... | collective-permute-start | bytes 2752520 | tf_op jit(solution)/shard_map/ppermute | solution.py:398
  86.2 3.3 %collective-permute-start = (bf16[1152,256]{1,0:T(8,128)(2,1)S(1)}, bf16[1152,256]{1,0:T(8,128)(2,1)S(1)}, u32[]{:S(2)}, u32[]{:S(2)}) collective-permute-start(bf16[1152,256]{1,0:T(8,128)(2,1)S(1)} %copy-done.28), channel_id=1, source_target_pairs={{0,8},{1,9},{2,10},{3,11},{4,12},{5,13},{6,14},{7,15},{8,0},{9,1},... | collective-permute-start | bytes 1769480 | tf_op jit(solution)/shard_map/ppermute | solution.py:398
  86.6 8.0 %collective-permute-start.6 = (bf16[256,640]{1,0:T(8,128)(2,1)S(1)}, bf16[256,640]{1,0:T(8,128)(2,1)S(1)}, u32[]{:S(2)}, u32[]{:S(2)}) collective-permute-start(bf16[256,640]{1,0:T(8,128)(2,1)S(1)} %copy-done.24), channel_id=1, source_target_pairs={{0,8},{1,9},{2,10},{3,11},{4,12},{5,13},{6,14},{7,15},{8,0},{9,1},... | collective-permute-start | bytes 983048 | tf_op jit(solution)/shard_map/ppermute | solution.py:398
  86.7 7.9 %collective-permute-start.5 = (bf16[256,640]{1,0:T(8,128)(2,1)S(1)}, bf16[256,640]{1,0:T(8,128)(2,1)S(1)}, u32[]{:S(2)}, u32[]{:S(2)}) collective-permute-start(bf16[256,640]{1,0:T(8,128)(2,1)S(1)} %get-tuple-element.142.refs_2_.att_t), channel_id=1, source_target_pairs={{0,8},{1,9},{2,10},{3,11},{4,12},{5,13},{6,14},{7,15},{8,0},{9,1},... | collective-permute-start | bytes 983048 | tf_op jit(solution)/shard_map/ppermute | solution.py:398
  88.1 5.9 %collective-permute-start.4 = (bf16[576,256]{1,0:T(8,128)(2,1)S(1)}, bf16[576,256]{1,0:T(8,128)(2,1)S(1)}, u32[]{:S(2)}, u32[]{:S(2)}) collective-permute-start(bf16[576,256]{1,0:T(8,128)(2,1)S(1)} %get-tuple-element.128), channel_id=1, source_target_pairs={{0,8},{1,9},{2,10},{3,11},{4,12},{5,13},{6,14},{7,15},{8,0},{9,1},... | collective-permute-start | bytes 884744 | tf_op jit(solution)/shard_map/ppermute | solution.py:398
  89.4 8.4 %collective-permute-start.7 = (bf16[96,1792]{1,0:T(8,128)(2,1)S(1)}, bf16[96,1792]{1,0:T(8,128)(2,1)S(1)}, u32[]{:S(2)}, u32[]{:S(2)}) collective-permute-start(bf16[96,1792]{1,0:T(8,128)(2,1)S(1)} %copy-done.34), channel_id=1, source_target_pairs={{0,32},{1,33},{2,34},{3,35},{4,36},{5,37},{6,38},{7,39},{8,104},{9... | collective-permute-start | bytes 1032200 | tf_op jit(solution)/shard_map/ppermute | solution.py:407
  90.9 7.8 %collective-permute-start.14 = (bf16[96,1792]{1,0:T(8,128)(2,1)S(1)}, bf16[96,1792]{1,0:T(8,128)(2,1)S(1)}, u32[]{:S(2)}, u32[]{:S(2)}) collective-permute-start(bf16[96,1792]{1,0:T(8,128)(2,1)S(1)} %copy-done.32), channel_id=1, source_target_pairs={{0,4},{1,5},{2,6},{3,7},{4,0},{5,1},{6,2},{7,3},{8,28},{9,29},{10,... | collective-permute-start | bytes 1032200 | tf_op jit(solution)/shard_map/ppermute | solution.py:407
  94.0 3.9 %copy-start.30 = (bf16[96,1792]{1,0:T(8,128)(2,1)S(1)}, bf16[96,1792]{1,0:T(8,128)(2,1)}, u32[]{:S(2)}) copy-start(bf16[96,1792]{1,0:T(8,128)(2,1)} %copy-done.29) | copy-start | bytes 1032196
  94.0 11.4 %copy-start.6 = (bf16[256,1152]{1,0:T(8,128)(2,1)S(1)}, bf16[256,1152]{1,0:T(8,128)(2,1)}, u32[]{:S(2)}) copy-start(bf16[256,1152]{1,0:T(8,128)(2,1)} %copy-done.4) | copy-start | bytes 1769476
  94.0 11.4 %copy-start.12 = (bf16[576,1152]{1,0:T(8,128)(2,1)S(1)}, bf16[576,1152]{1,0:T(8,128)(2,1)}, u32[]{:S(2)}) copy-start(bf16[576,1152]{1,0:T(8,128)(2,1)} %copy-done.11) | copy-start | bytes 3981316
  94.0 10.5 %collective-permute-start.9 = (bf16[96,1792]{1,0:T(8,128)(2,1)S(1)}, bf16[96,1792]{1,0:T(8,128)(2,1)S(1)}, u32[]{:S(2)}, u32[]{:S(2)}) collective-permute-start(bf16[96,1792]{1,0:T(8,128)(2,1)S(1)} %get-tuple-element.150), channel_id=1, source_target_pairs={{0,32},{1,33},{2,34},{3,35},{4,36},{5,37},{6,38},{7,39},{8,104},{9... | collective-permute-start | bytes 1032200 | tf_op jit(solution)/shard_map/ppermute | solution.py:407
  95.8 8.2 %collective-permute-start.8 = (bf16[96,1280]{1,0:T(8,128)(2,1)S(1)}, bf16[96,1280]{1,0:T(8,128)(2,1)S(1)}, u32[]{:S(2)}, u32[]{:S(2)}) collective-permute-start(bf16[96,1280]{1,0:T(8,128)(2,1)S(1)} %get-tuple-element.148), channel_id=1, source_target_pairs={{0,32},{1,33},{2,34},{3,35},{4,36},{5,37},{6,38},{7,39},{8,104},{9... | collective-permute-start | bytes 737288 | tf_op jit(solution)/shard_map/ppermute | solution.py:407
  97.3 13.4 %collective-permute-start.16 = (bf16[96,1792]{1,0:T(8,128)(2,1)S(1)}, bf16[96,1792]{1,0:T(8,128)(2,1)S(1)}, u32[]{:S(2)}, u32[]{:S(2)}) collective-permute-start(bf16[96,1792]{1,0:T(8,128)(2,1)S(1)} %get-tuple-element.166), channel_id=1, source_target_pairs={{0,4},{1,5},{2,6},{3,7},{4,0},{5,1},{6,2},{7,3},{8,28},{9,29},{10,... | collective-permute-start | bytes 1032200 | tf_op jit(solution)/shard_map/ppermute | solution.py:407
  97.9 14.0 %collective-permute-start.10 = (bf16[96,1792]{1,0:T(8,128)(2,1)S(1)}, bf16[96,1792]{1,0:T(8,128)(2,1)S(1)}, u32[]{:S(2)}, u32[]{:S(2)}) collective-permute-start(bf16[96,1792]{1,0:T(8,128)(2,1)S(1)} %copy-done.30), channel_id=1, source_target_pairs={{0,1},{1,0},{2,3},{3,2},{4,5},{5,4},{6,7},{7,6},{8,11},{9,10},{10,... | collective-permute-start | bytes 1032200 | tf_op jit(solution)/shard_map/ppermute | solution.py:407
  98.7 13.2 %collective-permute-start.12 = (bf16[96,1792]{1,0:T(8,128)(2,1)S(1)}, bf16[96,1792]{1,0:T(8,128)(2,1)S(1)}, u32[]{:S(2)}, u32[]{:S(2)}) collective-permute-start(bf16[96,1792]{1,0:T(8,128)(2,1)S(1)} %get-tuple-element.155), channel_id=1, source_target_pairs={{0,1},{1,0},{2,3},{3,2},{4,5},{5,4},{6,7},{7,6},{8,11},{9,10},{10,... | collective-permute-start | bytes 1032200 | tf_op jit(solution)/shard_map/ppermute | solution.py:407
  104.0 6.2 %collective-permute-start.15 = (bf16[96,1280]{1,0:T(8,128)(2,1)S(1)}, bf16[96,1280]{1,0:T(8,128)(2,1)S(1)}, u32[]{:S(2)}, u32[]{:S(2)}) collective-permute-start(bf16[96,1280]{1,0:T(8,128)(2,1)S(1)} %get-tuple-element.165), channel_id=1, source_target_pairs={{0,4},{1,5},{2,6},{3,7},{4,0},{5,1},{6,2},{7,3},{8,28},{9,29},{10,... | collective-permute-start | bytes 737288 | tf_op jit(solution)/shard_map/ppermute | solution.py:407
  104.5 7.4 %collective-permute-start.11 = (bf16[96,1280]{1,0:T(8,128)(2,1)S(1)}, bf16[96,1280]{1,0:T(8,128)(2,1)S(1)}, u32[]{:S(2)}, u32[]{:S(2)}) collective-permute-start(bf16[96,1280]{1,0:T(8,128)(2,1)S(1)} %get-tuple-element.154), channel_id=1, source_target_pairs={{0,1},{1,0},{2,3},{3,2},{4,5},{5,4},{6,7},{7,6},{8,11},{9,10},{10,... | collective-permute-start | bytes 737288 | tf_op jit(solution)/shard_map/ppermute | solution.py:407
  110.2 8.6 %collective-permute-start.13 = (bf16[48,4864]{1,0:T(8,128)(2,1)S(1)}, bf16[48,4864]{1,0:T(8,128)(2,1)S(1)}, u32[]{:S(2)}, u32[]{:S(2)}) collective-permute-start(bf16[48,4864]{1,0:T(8,128)(2,1)S(1)} %get-tuple-element.162), channel_id=1, source_target_pairs={{0,4},{1,5},{2,6},{3,7},{4,0},{5,1},{6,2},{7,3},{8,28},{9,29},{10,... | collective-permute-start | bytes 1400840 | tf_op jit(solution)/shard_map/ppermute | solution.py:407
  110.9 2.7 %copy-start.3 = (bf16[1728,1152]{1,0:T(8,128)(2,1)S(1)}, bf16[1728,1152]{1,0:T(8,128)(2,1)}, u32[]{:S(2)}) copy-start(bf16[1728,1152]{1,0:T(8,128)(2,1)} %copy-done.2) | copy-start | bytes 11943940
  110.9 2.7 %copy-start.18 = (bf16[256,1152]{1,0:T(8,128)(2,1)S(1)}, bf16[256,1152]{1,0:T(8,128)(2,1)}, u32[]{:S(2)}) copy-start(bf16[256,1152]{1,0:T(8,128)(2,1)} %copy-done.17) | copy-start | bytes 1769476
  111.0 8.8 %collective-permute-start.17 = (bf16[48,4864]{1,0:T(8,128)(2,1)S(1)}, bf16[48,4864]{1,0:T(8,128)(2,1)S(1)}, u32[]{:S(2)}, u32[]{:S(2)}) collective-permute-start(bf16[48,4864]{1,0:T(8,128)(2,1)S(1)} %get-tuple-element.168), channel_id=1, source_target_pairs={{0,1},{1,0},{2,3},{3,2},{4,5},{5,4},{6,7},{7,6},{8,11},{9,10},{10,... | collective-permute-start | bytes 1400840 | tf_op jit(solution)/shard_map/ppermute | solution.py:407
  112.1 9.1 %collective-permute-start.18 = (bf16[48,4864]{1,0:T(8,128)(2,1)S(1)}, bf16[48,4864]{1,0:T(8,128)(2,1)S(1)}, u32[]{:S(2)}, u32[]{:S(2)}) collective-permute-start(bf16[48,4864]{1,0:T(8,128)(2,1)S(1)} %get-tuple-element.171), channel_id=1, source_target_pairs={{0,32},{1,33},{2,34},{3,35},{4,36},{5,37},{6,38},{7,39},{8,104},{9... | collective-permute-start | bytes 1400840 | tf_op jit(solution)/shard_map/ppermute | solution.py:407
  118.9 6.1 %collective-permute-start.19 = (bf16[24,4864]{1,0:T(8,128)(2,1)S(1)}, bf16[24,4864]{1,0:T(8,128)(2,1)S(1)}, u32[]{:S(2)}, u32[]{:S(2)}) collective-permute-start(bf16[24,4864]{1,0:T(8,128)(2,1)S(1)} %get-tuple-element.173), channel_id=1, source_target_pairs={{0,1},{1,0},{2,3},{3,2},{4,5},{5,4},{6,7},{7,6},{8,11},{9,10},{10,... | collective-permute-start | bytes 700424 | tf_op jit(solution)/shard_map/ppermute | solution.py:407
  119.9 6.1 %collective-permute-start.20 = (bf16[24,4864]{1,0:T(8,128)(2,1)S(1)}, bf16[24,4864]{1,0:T(8,128)(2,1)S(1)}, u32[]{:S(2)}, u32[]{:S(2)}) collective-permute-start(bf16[24,4864]{1,0:T(8,128)(2,1)S(1)} %get-tuple-element.174), channel_id=1, source_target_pairs={{0,32},{1,33},{2,34},{3,35},{4,36},{5,37},{6,38},{7,39},{8,104},{9... | collective-permute-start | bytes 700424 | tf_op jit(solution)/shard_map/ppermute | solution.py:407
  121.4 6.1 %collective-permute-start.21 = (bf16[24,4864]{1,0:T(8,128)(2,1)S(1)}, bf16[24,4864]{1,0:T(8,128)(2,1)S(1)}, u32[]{:S(2)}, u32[]{:S(2)}) collective-permute-start(bf16[24,4864]{1,0:T(8,128)(2,1)S(1)} %get-tuple-element.175), channel_id=1, source_target_pairs={{0,4},{1,5},{2,6},{3,7},{4,0},{5,1},{6,2},{7,3},{8,28},{9,29},{10,... | collective-permute-start | bytes 700424 | tf_op jit(solution)/shard_map/ppermute | solution.py:407
  127.7 9.9 %collective-permute-start.22 = (bf16[3,12,4864]{2,1,0:T(8,128)(2,1)S(1)}, bf16[3,12,4864]{2,1,0:T(8,128)(2,1)S(1)}, u32[]{:S(2)}, u32[]{:S(2)}) collective-permute-start(bf16[3,12,4864]{2,1,0:T(8,128)(2,1)S(1)} %get-tuple-element.177), channel_id=1, source_target_pairs={{0,96},{1,97},{2,98},{3,99},{4,100},{5,101},{6,102},{7,103},{8,40}... | collective-permute-start | bytes 1050632 | tf_op jit(solution)/shard_map/ppermute | solution.py:407
  137.7 7.4 %collective-permute-start.23 = (bf16[3,6,4864]{2,1,0:T(8,128)(2,1)S(1)}, bf16[3,6,4864]{2,1,0:T(8,128)(2,1)S(1)}, u32[]{:S(2)}, u32[]{:S(2)}) collective-permute-start(bf16[3,6,4864]{2,1,0:T(8,128)(2,1)S(1)} %get-tuple-element.179), channel_id=1, source_target_pairs={{0,20},{1,21},{2,22},{3,23},{4,16},{5,17},{6,18},{7,19},{8,12},{9,... | collective-permute-start | bytes 525320 | tf_op jit(solution)/shard_map/ppermute | solution.py:407
  145.2 6.1 %collective-permute-start.24 = (bf16[3,3,4864]{2,1,0:T(4,128)(2,1)S(1)}, bf16[3,3,4864]{2,1,0:T(4,128)(2,1)S(1)}, u32[]{:S(2)}, u32[]{:S(2)}) collective-permute-start(bf16[3,3,4864]{2,1,0:T(4,128)(2,1)S(1)} %get-tuple-element.181), channel_id=1, source_target_pairs={{0,3},{1,2},{2,1},{3,0},{4,7},{5,6},{6,5},{7,4},{8,9},{9,8},{10,11... | collective-permute-start | bytes 262664 | tf_op jit(solution)/shard_map/ppermute | solution.py:407
